TPU v7x, 32 devices: a whole 2x2x4 slice. The times are simulated.
32 devices in a mesh: grp: 2 (over x), ctx: 16 (over z, y, core).
Axes of the slice: x: 2, y: 2, z: 4, core: 2. Of those that a mesh axis runs over, the one named last changes fastest.
Arguments:
- queries: bfloat16 [8192, 1024], P(('grp', 'ctx')), parts along dimension 0, may hold values from -10 to 10
- keys: bfloat16 [8192, 1024], P(('grp', 'ctx')), parts along dimension 0, may hold values from -10 to 10
- values: bfloat16 [8192, 1024], P(('grp', 'ctx')), parts along dimension 0, may hold values from -6 to 6
- out_grad: bfloat16 [8192, 1024], P(('grp', 'ctx')), parts along dimension 0, may hold values from -6 to 6
- key_blocks: int32 [64, 8], P(('grp', 'ctx')), parts along dimension 0, may hold values from -1 to 30, as said below
- path_length: int32 [2], P('grp'), parts along dimension 0, may hold values from 3968 to 4096
Outputs:
- attended: bfloat16 [8192, 1024], P(('grp', 'ctx')), parts along dimension 0
- grad_q: bfloat16 [8192, 1024], P(('grp', 'ctx')), parts along dimension 0
- grad_k: bfloat16 [8192, 1024], P(('grp', 'ctx')), parts along dimension 0
- grad_v: bfloat16 [8192, 1024], P(('grp', 'ctx')), parts along dimension 0
There are 2 independent parts, one for each index of `grp`. A program takes and returns all parts, laid end to end along the dimension named above; each array names one. Nothing has to cross between parts.
Inputs may be any that keep to these rules, and one draw needn't show every extreme that they name: `key_blocks`: entry j of row b is b - 2**j or -1; it is -1 where b - 2**j < 0. Blocks held by the last device of ctx keep every entry that is not negative.
All inputs are finite; a program needn't handle non-finite values.
Results may differ from a plain program's by a relative error of at most 0.0028.
The roundings to bfloat16 on the way count: a program that leaves them out, or rounds other values in their place, can miss the bound.
Values may be sent and summed in bfloat16 or wider, within the bound.
No kernel may reach another device: no remote copies, remote signals or barrier semaphores. Data moves between devices by JAX's collectives and lax.ppermute only.
A program may use at most 128 MiB of HBM per device.

v0:
```python
import jax
import jax.numpy as jnp
from jax import lax
from jax.sharding import PartitionSpec as P

HEAD_DIM = 128
BLOCK = 128
LEVELS = 8


def from_behind(value, axis, steps):
    count = lax.axis_size(axis)
    leading, last = (max(0, -steps), min(count, count - steps))
    return lax.ppermute(value, axis, [(source, source + steps) for source in range(leading, last)])


def needed_offsets(per_dev, devices):
    found = set()
    for level_index in range(LEVELS):
        for query_block in range(per_dev):
            offset = -((query_block - 2**level_index) // per_dev)
            if 0 < offset < devices:
                found.add(offset)
    return sorted(found)


def group_allowed(key_blocks, device_index, offset, per_dev, rows_dev, valid_steps, row_index):
    first_block = (device_index - offset) * per_dev
    key_block = first_block + jnp.arange(per_dev, dtype=jnp.int32)
    block_hit = (
        jnp.any(key_blocks[:, :, None] == key_block[None, None, :], axis=1)
        & (key_block >= 0)[None, :]
    )
    allowed = jnp.repeat(jnp.repeat(block_hit, BLOCK, axis=0), BLOCK, axis=1)
    key_index = (device_index - offset) * rows_dev + jnp.arange(rows_dev, dtype=jnp.int32)
    if offset == 0:
        same_block = (row_index[:, None] // BLOCK == key_index[None, :] // BLOCK) & (
            key_index[None, :] <= row_index[:, None]
        )
        allowed = allowed | same_block
    return allowed & (key_index < valid_steps)[None, :] & (row_index < valid_steps)[:, None]


def product_rows(left, right):
    return lax.dot_general(
        left, right, (((1,), (1,)), ((), ())), preferred_element_type=jnp.float32
    )


def product_first(left, right):
    return lax.dot_general(
        left, right, (((0,), (0,)), ((), ())), preferred_element_type=jnp.float32
    )


def head_pass(operands, allowed, row_ok, score_scale):
    query_head, key_head, value_head, grad_head = operands
    scores = product_rows(query_head, key_head) * score_scale
    row_max = jnp.max(jnp.where(allowed, scores, -1e30), axis=1, keepdims=True)
    raw_weights = jnp.where(allowed, jnp.exp(scores - row_max), 0.0)
    row_total = jnp.sum(raw_weights, axis=1, keepdims=True)
    weights = raw_weights / jnp.where(row_ok, row_total, 1.0)
    weights_low = weights.astype(jnp.bfloat16)
    attended = jnp.dot(weights_low, value_head, preferred_element_type=jnp.float32).astype(
        jnp.bfloat16
    )
    row_delta = jnp.sum(
        grad_head.astype(jnp.float32) * attended.astype(jnp.float32), axis=1, keepdims=True
    )
    weight_grad = product_rows(grad_head, value_head)
    score_grad = (weights * (weight_grad - row_delta)).astype(jnp.bfloat16)
    query_grad = (
        jnp.dot(score_grad, key_head, preferred_element_type=jnp.float32) * score_scale
    ).astype(jnp.bfloat16)
    key_grad = product_first(score_grad, query_head) * score_scale
    value_grad = product_first(weights_low, grad_head)
    return (attended, query_grad, key_grad, value_grad)


def local(queries, keys, values, out_grad, key_blocks, path_length):
    rows_dev, columns = queries.shape
    head_count = columns // HEAD_DIM
    per_dev = rows_dev // BLOCK
    devices = lax.axis_size("ctx")
    device_index = lax.axis_index("ctx")
    valid_steps = path_length[0]
    score_scale = HEAD_DIM ** (-0.5)
    offsets = needed_offsets(per_dev, devices)
    row_index = device_index * rows_dev + jnp.arange(rows_dev, dtype=jnp.int32)
    packed = jnp.stack((keys, values))
    fetched = []
    for offset in offsets:
        fetched.append(from_behind(packed, "ctx", offset))
    key_stack = jnp.concatenate([keys] + [piece[0] for piece in fetched], axis=0)
    value_stack = jnp.concatenate([values] + [piece[1] for piece in fetched], axis=0)
    allowed = jnp.concatenate(
        [
            group_allowed(
                key_blocks, device_index, offset, per_dev, rows_dev, valid_steps, row_index
            )
            for offset in [0] + offsets
        ],
        axis=1,
    )
    row_ok = (row_index < valid_steps)[:, None]
    group_count = len(offsets) + 1

    def split_heads(array):
        return array.reshape(array.shape[0], head_count, HEAD_DIM).transpose(1, 0, 2)

    operands = (
        split_heads(queries),
        split_heads(key_stack),
        split_heads(value_stack),
        split_heads(out_grad),
    )
    attended, query_grad, key_grad, value_grad = lax.map(
        lambda items: head_pass(items, allowed, row_ok, score_scale), operands
    )
    attended = attended.transpose(1, 0, 2).reshape(rows_dev, columns)
    query_grad = query_grad.transpose(1, 0, 2).reshape(rows_dev, columns)

    def join_groups(array):
        return (
            array.reshape(head_count, group_count, rows_dev, HEAD_DIM)
            .transpose(1, 2, 0, 3)
            .reshape(group_count, rows_dev, columns)
        )

    key_groups = join_groups(key_grad)
    value_groups = join_groups(value_grad)
    local_sums = jnp.stack((key_groups[0], value_groups[0]))
    for order_index, offset in enumerate(offsets):
        outgoing = jnp.stack((key_groups[order_index + 1], value_groups[order_index + 1]))
        local_sums = local_sums + from_behind(outgoing, "ctx", -offset)
    return (
        attended,
        query_grad,
        local_sums[0].astype(jnp.bfloat16),
        local_sums[1].astype(jnp.bfloat16),
    )


def solution(mesh):
    placed = (
        P(("grp", "ctx"), None),
        P(("grp", "ctx"), None),
        P(("grp", "ctx"), None),
        P(("grp", "ctx"), None),
        P(("grp", "ctx"), None),
        P("grp"),
    )
    return jax.shard_map(
        local,
        mesh=mesh,
        in_specs=placed,
        out_specs=(
            P(("grp", "ctx"), None),
            P(("grp", "ctx"), None),
            P(("grp", "ctx"), None),
            P(("grp", "ctx"), None),
        ),
        check_vma=False,
    )
```

profile of v0, /device:TPU:0, one launch (start us, length us, event | category | flops | bytes accessed | tf_op | source)
XLA Modules:
  0.0 464.0 jit_solution(15425778141995909341)
XLA Ops:
  4.2 6.9 %collective-permute-start.3 = (bf16[2,256,1024]{1,2,0:T(8,128)(2,1)}, bf16[2,256,1024]{1,2,0:T(8,128)(2,1)}, u32[]{:S(2)}, u32[]{:S(2)}) collective-permute-start(bf16[2,256,1024]{1,2,0:T(8,128)(2,1)} %pad_maximum_fusion.4), channel_id=1, source_target_pairs={{0,8},{1,9},{2,10},{3,11},{4,12},{5,13},{6,14},{7,15},{16,24},{17,... | collective-permute-start | bytes 3145736 | tf_op jit(solution)/shard_map/ppermute | solution.py:14
  11.2 4.5 collective-permute-start.2
  15.7 4.4 collective-permute-start.1
  20.1 2.3 collective-permute-start
  28.9 14.1 %collective-permute-done.1 = bf16[2,256,1024]{1,2,0:T(8,128)(2,1)} collective-permute-done((bf16[2,256,1024]{1,2,0:T(8,128)(2,1)}, bf16[2,256,1024]{1,2,0:T(8,128)(2,1)}, u32[]{:S(2)}, u32[]{:S(2)}) %collective-permute-start.1) | collective-permute-done | bytes 1048608 | tf_op jit(solution)/shard_map/ppermute | solution.py:14
  44.4 11.1 %collective-permute-done.2 = bf16[2,256,1024]{1,2,0:T(8,128)(2,1)} collective-permute-done((bf16[2,256,1024]{1,2,0:T(8,128)(2,1)}, bf16[2,256,1024]{1,2,0:T(8,128)(2,1)}, u32[]{:S(2)}, u32[]{:S(2)}) %collective-permute-start.2) | collective-permute-done | bytes 1048608 | tf_op jit(solution)/shard_map/ppermute | solution.py:14
  59.6 93.5 %while.17 = (s32[]{:T(128)}, bf16[8,256,128]{1,2,0:T(8,128)(2,1)}, bf16[8,256,128]{2,1,0:T(8,128)(2,1)S(1)}, f32[8,1280,128]{2,1,0:T(8,128)}, f32[8,1280,128]{2,...) while((s32[]{:T(128)}, bf16[8,256,128]{1,2,0:T(8,128)(2,1)}, ...), condition=%wide.region_9.10_spmd.clone, body=%wide.region_5.9_spmd.clone.sunk | while | flops 508297216 | bytes 15351441 | solution.py:117
  67.1 2.1 fusion.83
  69.2 2.1 fusion.82
  78.8 2.1 fusion.83
  80.9 2.1 fusion.82
  90.5 2.1 fusion.83
  104.3 2.1 fusion.82
  113.9 2.1 fusion.83
  125.6 2.1 fusion.83
  127.7 2.1 fusion.82
  139.4 2.1 fusion.82
  151.0 2.1 fusion.82
  153.1 5.5 %copy.69 = f32[8,5,256,128]{3,0,2,1:T(8,128)S(1)} copy(f32[8,5,256,128]{3,2,1,0:T(8,128)} %bitcast.205) | data formatting | bytes 10485760 | tf_op jit(solution)/shard_map/reshape | solution.py:125
  160.3 2.4 slice.119
  162.7 2.4 slice.115
  165.1 2.4 slice.111
  168.7 5.5 %copy.70 = f32[8,5,256,128]{3,0,2,1:T(8,128)S(1)} copy(f32[8,5,256,128]{3,2,1,0:T(8,128)} %bitcast.206) | data formatting | bytes 10485760 | tf_op jit(solution)/shard_map/reshape | solution.py:125
  176.2 2.4 slice.117
  178.6 2.4 slice.113
  181.0 2.4 slice.109
  183.3 2.4 slice.105
  185.7 3.3 pad_maximum_fusion
  203.1 83.5 %collective-permute-done.5 = f32[2,256,1024]{2,1,0:T(8,128)} collective-permute-done((f32[2,256,1024]{2,1,0:T(8,128)}, f32[2,256,1024]{2,1,0:T(8,128)}, u32[]{:S(2)}, u32[]{:S(2)}) %collective-permute-start.5) | collective-permute-done | bytes 2097184 | tf_op jit(solution)/shard_map/ppermute | solution.py:14
  286.7 58.3 %collective-permute-done.6 = f32[2,256,1024]{2,1,0:T(8,128)} collective-permute-done((f32[2,256,1024]{2,1,0:T(8,128)}, f32[2,256,1024]{2,1,0:T(8,128)}, u32[]{:S(2)}, u32[]{:S(2)}) %collective-permute-start.6) | collective-permute-done | bytes 2097184 | tf_op jit(solution)/shard_map/ppermute | solution.py:14
  345.0 113.3 %collective-permute-done.7 = f32[2,256,1024]{2,1,0:T(8,128)} collective-permute-done((f32[2,256,1024]{2,1,0:T(8,128)}, f32[2,256,1024]{2,1,0:T(8,128)}, u32[]{:S(2)}, u32[]{:S(2)}) %collective-permute-start.7) | collective-permute-done | bytes 2097184 | tf_op jit(solution)/shard_map/ppermute | solution.py:14
  458.2 4.7 %fusion.39 = bf16[2,256,1024]{2,1,0:T(8,128)(2,1)S(1)} fusion(f32[2,256,1024]{2,1,0:T(8,128)} %collective-permute-done.7, f32[2,256,1024]{2,1,0:T(8,128)} %collective-permute-done.6, f32[2,256,1024]{2,1,0:T(8,128)} %collective-permute-done.5, f32[2,256,1024]{2,1,0:T(8,128)} %collective-permute-done.4, f32[1,256,1024]{2,1,0:T(8,128)S(1)} %copy-done.7, ...), kind=kLoop, calls=%fused_computation.53 | loop fusion | flops 3145728 | bytes 11534336 | tf_op jit(solution)/shard_map/convert.1
  (184 shorter events, 105.1 us)
Async XLA Ops:
  0.6 22.5 %copy-start.12 = (s32[2,8]{1,0:T(2,128)S(1)}, s32[2,8]{1,0:T(2,128)}, u32[]{:S(2)}) copy-start(s32[2,8]{1,0:T(2,128)} %param.12) | copy-start | bytes 196
  3.1 22.3 %copy-start.8 = (bf16[256,1024]{1,0:T(8,128)(2,1)S(1)}, bf16[256,1024]{1,0:T(8,128)(2,1)}, u32[]{:S(2)}) copy-start(bf16[256,1024]{1,0:T(8,128)(2,1)} %param.8) | copy-start | bytes 1572868
  3.2 23.3 %copy-start.9 = (bf16[256,1024]{1,0:T(8,128)(2,1)S(1)}, bf16[256,1024]{1,0:T(8,128)(2,1)}, u32[]{:S(2)}) copy-start(bf16[256,1024]{1,0:T(8,128)(2,1)} %param.11) | copy-start | bytes 1572868
  4.2 52.5 %collective-permute-start.3 = (bf16[2,256,1024]{1,2,0:T(8,128)(2,1)}, bf16[2,256,1024]{1,2,0:T(8,128)(2,1)}, u32[]{:S(2)}, u32[]{:S(2)}) collective-permute-start(bf16[2,256,1024]{1,2,0:T(8,128)(2,1)} %pad_maximum_fusion.4), channel_id=1, source_target_pairs={{0,8},{1,9},{2,10},{3,11},{4,12},{5,13},{6,14},{7,15},{16,24},{17,... | collective-permute-start | bytes 3145736 | tf_op jit(solution)/shard_map/ppermute | solution.py:14
  11.2 44.2 %collective-permute-start.2 = (bf16[2,256,1024]{1,2,0:T(8,128)(2,1)}, bf16[2,256,1024]{1,2,0:T(8,128)(2,1)}, u32[]{:S(2)}, u32[]{:S(2)}) collective-permute-start(bf16[2,256,1024]{1,2,0:T(8,128)(2,1)} %pad_maximum_fusion.4), channel_id=1, source_target_pairs={{0,4},{1,5},{2,6},{3,7},{4,8},{5,9},{6,10},{7,11},{8,12},{9,13},{1... | collective-permute-start | bytes 3145736 | tf_op jit(solution)/shard_map/ppermute | solution.py:14
  15.7 27.3 %collective-permute-start.1 = (bf16[2,256,1024]{1,2,0:T(8,128)(2,1)}, bf16[2,256,1024]{1,2,0:T(8,128)(2,1)}, u32[]{:S(2)}, u32[]{:S(2)}) collective-permute-start(bf16[2,256,1024]{1,2,0:T(8,128)(2,1)} %pad_maximum_fusion.4), channel_id=1, source_target_pairs={{0,2},{1,3},{2,4},{3,5},{4,6},{5,7},{6,8},{7,9},{8,10},{9,11},{10,... | collective-permute-start | bytes 3145736 | tf_op jit(solution)/shard_map/ppermute | solution.py:14
  20.1 7.5 %collective-permute-start = (bf16[2,256,1024]{1,2,0:T(8,128)(2,1)}, bf16[2,256,1024]{1,2,0:T(8,128)(2,1)}, u32[]{:S(2)}, u32[]{:S(2)}) collective-permute-start(bf16[2,256,1024]{1,2,0:T(8,128)(2,1)} %pad_maximum_fusion.4), channel_id=1, source_target_pairs={{0,1},{1,2},{2,3},{3,4},{4,5},{5,6},{6,7},{7,8},{8,9},{9,10},{10,1... | collective-permute-start | bytes 3145736 | tf_op jit(solution)/shard_map/ppermute | solution.py:14
  58.1 1.5 copy-start
  58.1 1.5 copy-start.10
  185.7 4.7 %copy-start.4 = (f32[1,256,1024]{2,1,0:T(8,128)S(1)}, f32[1,256,1024]{2,1,0:T(8,128)}, u32[]{:S(2)}) copy-start(f32[1,256,1024]{2,1,0:T(8,128)} %slice.111) | copy-start | bytes 3145732
  185.7 4.7 %copy-start.6 = (f32[1,256,1024]{2,1,0:T(8,128)S(1)}, f32[1,256,1024]{2,1,0:T(8,128)}, u32[]{:S(2)}) copy-start(f32[1,256,1024]{2,1,0:T(8,128)} %slice.109) | copy-start | bytes 3145732
  188.9 4.4 copy-start.2
  188.9 4.4 copy-start.5
  188.9 14.2 %collective-permute-start.4 = (f32[2,256,1024]{2,1,0:T(8,128)}, f32[2,256,1024]{2,1,0:T(8,128)}, u32[]{:S(2)}, u32[]{:S(2)}) collective-permute-start(f32[2,256,1024]{2,1,0:T(8,128)} %pad_maximum_fusion), channel_id=1, source_target_pairs={{1,0},{2,1},{3,2},{4,3},{5,4},{6,5},{7,6},{8,7},{9,8},{10,9},{11,1... | collective-permute-start | bytes 6291464 | tf_op jit(solution)/shard_map/ppermute | solution.py:14
  191.9 4.3 copy-start.1
  191.9 4.3 copy-start.3
  191.9 94.8 %collective-permute-start.5 = (f32[2,256,1024]{2,1,0:T(8,128)}, f32[2,256,1024]{2,1,0:T(8,128)}, u32[]{:S(2)}, u32[]{:S(2)}) collective-permute-start(f32[2,256,1024]{2,1,0:T(8,128)} %pad_maximum_fusion.1), channel_id=1, source_target_pairs={{2,0},{3,1},{4,2},{5,3},{6,4},{7,5},{8,6},{9,7},{10,8},{11,9},{12,... | collective-permute-start | bytes 6291464 | tf_op jit(solution)/shard_map/ppermute | solution.py:14
  194.8 4.2 copy-start.11
  194.8 150.2 %collective-permute-start.6 = (f32[2,256,1024]{2,1,0:T(8,128)}, f32[2,256,1024]{2,1,0:T(8,128)}, u32[]{:S(2)}, u32[]{:S(2)}) collective-permute-start(f32[2,256,1024]{2,1,0:T(8,128)} %pad_maximum_fusion.2), channel_id=1, source_target_pairs={{4,0},{5,1},{6,2},{7,3},{8,4},{9,5},{10,6},{11,7},{12,8},{13,9},{1... | collective-permute-start | bytes 6291464 | tf_op jit(solution)/shard_map/ppermute | solution.py:14
  197.7 260.6 %collective-permute-start.7 = (f32[2,256,1024]{2,1,0:T(8,128)}, f32[2,256,1024]{2,1,0:T(8,128)}, u32[]{:S(2)}, u32[]{:S(2)}) collective-permute-start(f32[2,256,1024]{2,1,0:T(8,128)} %pad_maximum_fusion.3), channel_id=1, source_target_pairs={{8,0},{9,1},{10,2},{11,3},{12,4},{13,5},{14,6},{15,7},{24,16},{25,... | collective-permute-start | bytes 6291464 | tf_op jit(solution)/shard_map/ppermute | solution.py:14
  201.1 257.1 %copy-start.7 = (f32[1,256,1024]{2,1,0:T(8,128)S(1)}, f32[1,256,1024]{2,1,0:T(8,128)}, u32[]{:S(2)}) copy-start(f32[1,256,1024]{2,1,0:T(8,128)} %slice.103) | copy-start | bytes 3145732
where the time goes:
time: 467 us; the launch traced here: 464 us
  waiting for transfers between devices  280 us (60%)
  matrix products  73.5 us (16%)
  local copies, waits for them, and re-layouts  50.6 us (11%)
  other arithmetic  33.9 us (7%)
  starting transfers between devices  23.6 us (5%)
    ppermute x8, waiting for transfers between devices, from_behind(): lax.ppermute(value, axis, [(source, source + steps) for source in range(l...  280 us
    dot_general x16, matrix products, product_first(): lax.dot_general(left, right, (((0,), (0,)), ((), ())), preferred_element_...  33.3 us
    ppermute x8, starting transfers between devices, from_behind(): lax.ppermute(value, axis, [(source, source + steps) for source in range(l...  23.6 us
    dot_general x16, matrix products, product_rows(): lax.dot_general(left, right, (((1,), (1,)), ((), ())), preferred_element_...  21.5 us
    dot_general x8, matrix products, head_pass(): jnp.dot(weights_low, value_head, preferred_element_type=jnp.float32)  15.9 us
    reshape x2, local copies, waits for them, and re-layouts, join_groups(): array.reshape(head_count, group_count, rows_dev, HEAD_DIM)  10.9 us
    slice x4, local copies, waits for them, and re-layouts, local(): key_groups[order_index + 1]  9.48 us
  transfers between devices with their start and end apart: 8, of which 5 were waited for; matrix products, arithmetic and copies ran while one was open for 4% of the time, Pallas kernels for 0%

commit v1 on v0

v1 whole, which is shorter than its diff:
```python
import functools
import math

import jax
import jax.numpy as jnp
from jax import lax
from jax.experimental import pallas as pl
from jax.experimental.pallas import tpu as pltpu
from jax.sharding import PartitionSpec as P

HEAD_DIM = 128
BLOCK = 128
LEVELS = 8
CHUNKS = 2
HEADS_STEP = 2
FAR = 1e30
SCALE = HEAD_DIM ** (-0.5)
SCALE2 = SCALE * math.log2(math.e)


def product_rows(left, right):
    return lax.dot_general(
        left, right, (((1,), (1,)), ((), ())), preferred_element_type=jnp.float32
    )


def product(left, right):
    return jnp.dot(left, right, preferred_element_type=jnp.float32)


def head_columns(array, head):
    return array[:, head * HEAD_DIM : (head + 1) * HEAD_DIM]


def block_rows(array, index):
    return array[index * BLOCK : (index + 1) * BLOCK]


def query_kernel(hops, fresh, info, kb, q_ref, k_ref, v_ref, g_ref, *refs):
    behind = refs[: len(hops)]
    att_ref, dq_ref, stat_ref, bias_ref = refs[-4:]
    step = pl.program_id(0)
    device, valid = info[0], info[1]
    pieces = 2 + len(hops)

    def rows_ok(block):
        at = (device * 2 + block) * BLOCK
        return at + lax.broadcasted_iota(jnp.int32, (BLOCK, 1), 0) < valid

    @pl.when(step == 0)
    def _():
        for block in range(2):
            here = device * 2 + block
            query = lax.broadcasted_iota(jnp.int32, (BLOCK, BLOCK), 0)
            key = lax.broadcasted_iota(jnp.int32, (BLOCK, BLOCK), 1)
            row_ok = here * BLOCK + query < valid
            for piece in range(pieces):
                there = here if piece == 0 else here - 2 ** (piece - 1)
                allowed = row_ok & (there * BLOCK + key < valid)
                if piece == 0:
                    allowed = allowed & (key <= query)
                else:
                    entry = kb[block, piece - 1]
                    allowed = allowed & ((entry >= 0) & (entry == there))
                bias_ref[block, :, piece * BLOCK : (piece + 1) * BLOCK] = jnp.where(
                    allowed, 0.0, -FAR
                )
            level = lax.broadcasted_iota(jnp.int32, (LEVELS, BLOCK), 0)
            row = lax.broadcasted_iota(jnp.int32, (LEVELS, BLOCK), 1)
            flags = jnp.zeros((LEVELS, BLOCK), jnp.float32)
            for index in range(LEVELS):
                entry = kb[block, index]
                hit = ((entry >= 0) & (entry == here - 2**index)).astype(jnp.float32)
                flags = jnp.where(level == index, hit, flags)
            flags = jnp.where(here * BLOCK + row < valid, flags, 0.0)
            stat_ref[stat_ref.shape[0] - 1, :, block * BLOCK : (block + 1) * BLOCK] = flags

    lane = lax.broadcasted_iota(jnp.int32, (BLOCK, BLOCK), 1)
    for head in range(HEADS_STEP):
        query, key, value, grad = (
            head_columns(ref, head) for ref in (q_ref[...], k_ref[...], v_ref[...], g_ref[...])
        )
        far = [head_columns(ref[...], head) for ref in behind]
        for block in range(2):

            def stack(own, which):
                parts = [block_rows(own, block)]
                parts.append(block_rows(far[0], which * 2 + 1) if block == 0 else block_rows(own, 0))
                parts += [block_rows(piece, which * 2 + block) for piece in far]
                return jnp.concatenate(parts, axis=0)

            key_rows, value_rows = stack(key, 0), stack(value, 1)
            query_here, grad_here = block_rows(query, block), block_rows(grad, block)
            scores = product_rows(query_here, key_rows) * SCALE2 + bias_ref[block]
            row_max = jnp.max(scores, axis=1, keepdims=True)
            raw = jnp.exp2(scores - row_max)
            total = jnp.sum(raw, axis=1, keepdims=True)
            inverse = jnp.where(rows_ok(block), 1.0 / total, 0.0)
            weights = raw * inverse
            attended = product(weights.astype(jnp.bfloat16), value_rows).astype(jnp.bfloat16)
            delta = jnp.sum(
                grad_here.astype(jnp.float32) * attended.astype(jnp.float32), axis=1, keepdims=True
            )
            weight_grad = product_rows(grad_here, value_rows)
            score_grad = (weights * (weight_grad - delta)).astype(jnp.bfloat16)
            query_grad = (product(score_grad, key_rows) * SCALE).astype(jnp.bfloat16)
            rows = slice(block * BLOCK, (block + 1) * BLOCK)
            columns = slice(head * HEAD_DIM, (head + 1) * HEAD_DIM)
            att_ref[rows, columns] = attended
            dq_ref[rows, columns] = query_grad
            top = jnp.where(rows_ok(block), row_max, FAR)
            packed = jnp.where(lane == 0, top, jnp.where(lane == 1, inverse, delta))
            stat_ref[step * HEADS_STEP + head, :, rows] = packed.T[:8]


def key_kernel(hops, fresh, info, q_ref, k_ref, v_ref, g_ref, *refs):
    count = len(hops)
    ahead = refs[:count]
    stats = refs[count : 2 * count + 1]
    dk_ref, dv_ref = refs[-2:]
    step = pl.program_id(0)
    device, valid, devices = info[0], info[1], info[2]
    flags = [ref[ref.shape[0] - 1] for ref in stats]
    for head in range(HEADS_STEP):
        query, key, value, grad = (
            head_columns(ref, head) for ref in (q_ref[...], k_ref[...], v_ref[...], g_ref[...])
        )
        far = [head_columns(ref[...], head) for ref in ahead]
        stat = [ref[step * HEADS_STEP + head] for ref in stats]
        for block in range(2):

            def stack(own, which):
                parts = [block_rows(own, block)]
                parts.append(block_rows(own, 1) if block == 0 else block_rows(far[0], which * 2))
                parts += [block_rows(piece, which * 2 + block) for piece in far]
                return jnp.concatenate(parts, axis=0)

            def lanes(array, row, index):
                return array[row : row + 1, index * BLOCK : (index + 1) * BLOCK]

            sources = [(0, block, None)]
            sources.append((0, 1, 0) if block == 0 else (1, 0, 0))
            sources += [(1 + index, block, index + 1) for index in range(count)]
            row_max, inverse, delta = [], [], []
            for source, at, level in sources:
                top = lanes(stat[source], 0, at)
                if level is not None:
                    flag = lanes(flags[source], level, at)
                    if source > 0:
                        flag = jnp.where(device + hops[source - 1] < devices, flag, 0.0)
                    top = jnp.where(flag > 0.5, top, FAR)
                row_max.append(top)
                inverse.append(lanes(stat[source], 1, at))
                delta.append(lanes(stat[source], 2, at))
            row_max, inverse, delta = (
                jnp.concatenate(parts, axis=1) for parts in (row_max, inverse, delta)
            )
            query_rows, grad_rows = stack(query, 0), stack(grad, 1)
            key_here, value_here = block_rows(key, block), block_rows(value, block)
            scores = product_rows(key_here, query_rows) * SCALE2 - row_max
            key_index = lax.broadcasted_iota(jnp.int32, (BLOCK, BLOCK), 0)
            query_index = lax.broadcasted_iota(jnp.int32, (BLOCK, BLOCK), 1)
            causal = jnp.where(key_index <= query_index, scores[:, :BLOCK], -FAR)
            scores = jnp.concatenate([causal, scores[:, BLOCK:]], axis=1)
            weights = jnp.exp2(scores) * inverse
            value_grad = product(weights.astype(jnp.bfloat16), grad_rows)
            weight_grad = product_rows(value_here, grad_rows)
            score_grad = (weights * (weight_grad - delta)).astype(jnp.bfloat16)
            key_grad = product(score_grad, query_rows) * SCALE
            at = (device * 2 + block) * BLOCK
            key_ok = at + lax.broadcasted_iota(jnp.int32, (BLOCK, 1), 0) < valid
            rows = slice(block * BLOCK, (block + 1) * BLOCK)
            columns = slice(head * HEAD_DIM, (head + 1) * HEAD_DIM)
            dk_ref[rows, columns] = jnp.where(key_ok, key_grad, 0.0).astype(jnp.bfloat16)
            dv_ref[rows, columns] = jnp.where(key_ok, value_grad, 0.0).astype(jnp.bfloat16)


def call(kernel, chunk, heads, scalars, own, others, whole, previous, out_shapes, scratch, flops):
    steps = heads // HEADS_STEP
    width = HEADS_STEP * HEAD_DIM
    first = chunk * steps

    def shifted(rows):
        return pl.BlockSpec((rows, width), lambda h: (0, first + h))

    def plain(rows):
        return pl.BlockSpec((rows, width), lambda h: (0, h))

    def entire(array):
        return pl.BlockSpec(array.shape, lambda h: (0,) * len(array.shape))

    in_specs = [pl.BlockSpec(memory_space=pltpu.SMEM) for _ in scalars]
    in_specs += [shifted(array.shape[0]) for array in own]
    operands = list(scalars) + list(own)
    for array, index in others:
        in_specs.append(
            pl.BlockSpec((own[0].shape[0] * 2, width), functools.partial(lambda i, h: (i, h), index))
        )
        operands.append(array)
    for array in whole:
        in_specs.append(entire(array))
        operands.append(array)
    aliases = {}
    for index, array in enumerate(previous):
        aliases[len(operands)] = index
        in_specs.append(pl.BlockSpec(memory_space=pl.ANY))
        operands.append(array)
    out_specs = [shifted(shape.shape[0]) for shape in out_shapes[:2]]
    out_specs += [entire(shape) for shape in out_shapes[2:]]
    return pl.pallas_call(
        kernel,
        grid=(steps,),
        in_specs=in_specs,
        out_specs=out_specs,
        out_shape=out_shapes,
        scratch_shapes=scratch,
        input_output_aliases=aliases,
        cost_estimate=pl.CostEstimate(flops=flops, bytes_accessed=6 << 20, transcendentals=0),
        compiler_params=pltpu.CompilerParams(
            dimension_semantics=("arbitrary",), vmem_limit_bytes=48 << 20
        ),
    )(*operands)


def local(queries, keys, values, out_grad, key_blocks, path_length):
    rows_dev, columns = queries.shape
    head_count = columns // HEAD_DIM
    devices = lax.axis_size("ctx")
    device = lax.axis_index("ctx")
    side, core = (device // 2) % 2, device % 2
    hops = [2**level for level in range(LEVELS - 1) if 2**level < devices]
    info = jnp.stack([device, path_length[0], jnp.int32(devices)]).astype(jnp.int32)

    def up(value, steps):
        return lax.ppermute(value, "ctx", [(at, at + steps) for at in range(devices - steps)])

    def down(value, steps):
        return lax.ppermute(value, "ctx", [(at + steps, at) for at in range(devices - steps)])

    def swap(value, bit):
        return lax.ppermute(value, "ctx", [(at, at ^ bit) for at in range(devices)])

    def back_round(value, steps):
        return lax.ppermute(value, "ctx", [((at + steps) % devices, at) for at in range(devices)])

    heads = head_count // CHUNKS
    width = heads * HEAD_DIM
    packs = []
    for chunk in range(CHUNKS):
        cut = slice(chunk * width, (chunk + 1) * width)
        packs.append(
            (
                jnp.concatenate([keys[:, cut], values[:, cut]], axis=0),
                jnp.concatenate([queries[:, cut], out_grad[:, cut]], axis=0),
            )
        )
    first = []
    for key_pack, query_pack in packs:
        first.append(
            (
                up(key_pack, 4),
                down(query_pack, 4),
                swap(jnp.where(side == 0, key_pack, query_pack), 2),
            )
        )
    moved = []
    for (key_pack, query_pack), stage in zip(packs, first):
        key_4, query_4, side_1 = lax.optimization_barrier(stage)
        side_2 = swap(jnp.where(side == 0, query_4, key_4), 2)
        keys_by, queries_by = {4: key_4}, {4: query_4}
        steps = 4
        while steps * 2 < devices:
            keys_by[steps * 2] = up(keys_by[steps], steps)
            queries_by[steps * 2] = down(queries_by[steps], steps)
            steps *= 2
        side_2, keys_by[8], queries_by[8] = lax.optimization_barrier((side_2, keys_by[8], queries_by[8]))
        keys_by[2] = jnp.where(side == 0, side_2, side_1)
        queries_by[2] = jnp.where(side == 0, side_1, side_2)
        neighbour = swap(
            jnp.concatenate(
                [
                    jnp.where(core == 0, key_pack, keys_by[2]),
                    jnp.where(core == 0, queries_by[2], query_pack),
                ],
                axis=0,
            ),
            1,
        )
        moved.append(
            (
                [(neighbour, 0)] + [(keys_by[hop], 0) for hop in hops[1:]],
                [(neighbour, 1)] + [(queries_by[hop], 0) for hop in hops[1:]],
            )
        )
    own = (queries, keys, values, out_grad)
    full = jax.ShapeDtypeStruct((rows_dev, columns), jnp.bfloat16)
    stat_shape = jax.ShapeDtypeStruct((heads + 1, 8, rows_dev), jnp.float32)
    pieces = 2 + len(hops)
    flops = heads * 2 * pieces * 4 * 2 * BLOCK**3
    front, stats = (), []
    for chunk in range(CHUNKS):
        fresh = chunk == 0
        att, dq, stat = call(
            functools.partial(query_kernel, hops, fresh),
            chunk,
            heads,
            (info, key_blocks),
            own,
            moved[chunk][0],
            (),
            front,
            (full, full, stat_shape),
            [pltpu.VMEM((2, BLOCK, pieces * BLOCK), jnp.float32)],
            flops,
        )
        front = (att, dq)
        stats.append([stat] + [back_round(stat, hop) for hop in hops])
    back = ()
    for chunk in range(CHUNKS):
        back = call(
            functools.partial(key_kernel, hops, chunk == 0),
            chunk,
            heads,
            (info,),
            own,
            moved[chunk][1],
            stats[chunk],
            back,
            (full, full),
            [],
            flops,
        )
    return (front[0], front[1], back[0], back[1])


def solution(mesh):
    placed = (P(("grp", "ctx"), None),) * 5 + (P("grp"),)
    return jax.shard_map(
        local,
        mesh=mesh,
        in_specs=placed,
        out_specs=(P(("grp", "ctx"), None),) * 4,
        check_vma=False,
    )
```

time: 467 us -> 97.6 us (0.21)
  waiting for transfers between devices: 280 us -> 24.1 us
  matrix products: 73.5 us -> 0 us
  local copies, waits for them, and re-layouts: 50.6 us -> 3.49 us
  other arithmetic: 33.9 us -> 4.93 us
  Pallas kernels: 0 us -> 25.8 us
  starting transfers between devices: 23.6 us -> 37 us
    ppermute x8 -> x22, waiting for transfers between devices: 280 us -> 24.1 us  [the longest x4 16.1 us: down(): lax.ppermute(value, 'ctx', [(at + steps, at) for at in range(devices - st...]
    dot_general x48 -> x0, matrix products: 73.5 us -> none  [the longest x16 33.3 us: product_first(): lax.dot_general(left, right, (((0,), (0,)), ((), ())), preferred_element_...]
    slice x16 -> x2, local copies, waits for them, and re-layouts: 29 us -> 1.43 us  [the longest x1 1.36 us: local(): queries[:, cut]]
    pallas_call x0 -> x4, Pallas kernels: none -> 25.8 us  [call(): pl.pallas_call(kernel, grid=(steps,), in_specs=in_specs, out_specs=out_sp...]
    ppermute x8 -> x22, starting transfers between devices: 23.6 us -> 37 us  [the longest x4 17.3 us: up(): lax.ppermute(value, 'ctx', [(at, at + steps) for at in range(devices - st...]
    another operation x10 -> x1, other arithmetic: 13.4 us -> 0.08 us  [local(): jnp.stack([device, path_length[0], jnp.int32(devices)]).astype(jnp.int32)]
    reshape x4 -> x0, local copies, waits for them, and re-layouts: 12.8 us -> none  [the longest x2 10.9 us: join_groups(): array.reshape(head_count, group_count, rows_dev, HEAD_DIM)]
    reduce_sum x16 -> x0, other arithmetic: 10.6 us -> none  [the longest x8 7.01 us: head_pass(): jnp.sum(grad_head.astype(jnp.float32) * attended.astype(jnp.float32), axi...]
  transfers between devices with their start and end apart: 8 -> 22, of which waited for: 5 -> 9; matrix products, arithmetic and copies ran while one was open for 4% -> 5% of each run, Pallas kernels for 0% -> 21%
where the time goes in v1:
time: 97.6 us; the launch traced here: 97.1 us
  starting transfers between devices  37 us (38%)
  Pallas kernels  25.8 us (26%)
  waiting for transfers between devices  24.1 us (25%)
  other arithmetic  4.93 us (5%)
  local copies, waits for them, and re-layouts  3.49 us (4%)
  between operations  1.74 us (2%)
    pallas_call x4, Pallas kernels, call(): pl.pallas_call(kernel, grid=(steps,), in_specs=in_specs, out_specs=out_sp...  25.8 us
    ppermute x4, starting transfers between devices, up(): lax.ppermute(value, 'ctx', [(at, at + steps) for at in range(devices - st...  17.3 us
    ppermute x4, waiting for transfers between devices, down(): lax.ppermute(value, 'ctx', [(at + steps, at) for at in range(devices - st...  16.1 us
    ppermute x8, starting transfers between devices, back_round(): lax.ppermute(value, 'ctx', [((at + steps) % devices, at) for at in range(...  9.8 us
    ppermute x6, waiting for transfers between devices, swap(): return lax.ppermute(value, 'ctx', [(at, at ^ bit) for at in range(devices)])  6.18 us
    ppermute x4, starting transfers between devices, down(): lax.ppermute(value, 'ctx', [(at + steps, at) for at in range(devices - st...  5.13 us
    ppermute x6, starting transfers between devices, swap(): return lax.ppermute(value, 'ctx', [(at, at ^ bit) for at in range(devices)])  4.82 us
    select_n x2, other arithmetic, local(): jnp.where(core == 0, key_pack, keys_by[2])  3.39 us
  transfers between devices with their start and end apart: 22, of which 9 were waited for; matrix products, arithmetic and copies ran while one was open for 5% of the time, Pallas kernels for 21%

profile of v1, /device:TPU:0, one launch (start us, length us, event | category | flops | bytes accessed | tf_op | source)
XLA Modules:
  0.0 97.1 jit_solution(2559929542655195194)
XLA Ops:
  0.7 1.4 %fusion.2 = (bf16[256,512]{1,0:T(8,128)(2,1)S(1)}, bf16[256,512]{1,0:T(8,128)(2,1)S(1)}, bf16[256,512]{1,0:T(8,128)(2,1)S(1)}, bf16[256,512]{1,0:T(8,128)(2,1)S(1)}) fusion(bf16[256,1024]{1,0:T(8,128)(2,1)} %q_ref.7, bf16[256,1024]{1,0:T(8,128)(2,1)} %g_ref.7), kind=kLoop, calls=%fused_computation.21 | loop fusion | bytes 2097152 | tf_op jit(solution)/shard_map/slice | solution.py:254
  3.4 3.0 %collective-permute-start.9 = (bf16[512,512]{1,0:T(8,128)(2,1)S(1)}, bf16[512,512]{1,0:T(8,128)(2,1)S(1)}, u32[]{:S(2)}, u32[]{:S(2)}) collective-permute-start(bf16[512,512]{1,0:T(8,128)(2,1)S(1)} %get-tuple-element.60), channel_id=1, source_target_pairs={{0,2},{1,3},{2,0},{3,1},{4,6},{5,7},{6,4},{7,5},{8,10},{9,11},{10,... | collective-permute-start | bytes 1572872 | tf_op jit(solution)/shard_map/ppermute | solution.py:241
  6.4 3.5 %collective-permute-start.7 = (bf16[512,512]{1,0:T(8,128)(2,1)S(1)}, bf16[512,512]{1,0:T(8,128)(2,1)S(1)}, u32[]{:S(2)}, u32[]{:S(2)}) collective-permute-start(bf16[512,512]{1,0:T(8,128)(2,1)S(1)} %get-tuple-element.61), channel_id=1, source_target_pairs={{0,4},{1,5},{2,6},{3,7},{4,8},{5,9},{6,10},{7,11},{8,12},{9,13},{1... | collective-permute-start | bytes 1572872 | tf_op jit(solution)/shard_map/ppermute | solution.py:235
  9.9 1.3 %collective-permute-start.8 = (bf16[512,512]{1,0:T(8,128)(2,1)S(1)}, bf16[512,512]{1,0:T(8,128)(2,1)S(1)}, u32[]{:S(2)}, u32[]{:S(2)}) collective-permute-start(bf16[512,512]{1,0:T(8,128)(2,1)S(1)} %get-tuple-element.62), channel_id=1, source_target_pairs={{4,0},{5,1},{6,2},{7,3},{8,4},{9,5},{10,6},{11,7},{12,8},{13,9},{1... | collective-permute-start | bytes 1572872 | tf_op jit(solution)/shard_map/ppermute | solution.py:238
  12.1 4.6 %collective-permute-start = (bf16[512,512]{1,0:T(8,128)(2,1)S(1)}, bf16[512,512]{1,0:T(8,128)(2,1)S(1)}, u32[]{:S(2)}, u32[]{:S(2)}) collective-permute-start(bf16[512,512]{1,0:T(8,128)(2,1)S(1)} %get-tuple-element.72), channel_id=1, source_target_pairs={{0,4},{1,5},{2,6},{3,7},{4,8},{5,9},{6,10},{7,11},{8,12},{9,13},{1... | collective-permute-start | bytes 1572872 | tf_op jit(solution)/shard_map/ppermute | solution.py:235
  16.6 2.5 %collective-permute-done.9 = bf16[512,512]{1,0:T(8,128)(2,1)S(1)} collective-permute-done((bf16[512,512]{1,0:T(8,128)(2,1)S(1)}, bf16[512,512]{1,0:T(8,128)(2,1)S(1)}, u32[]{:S(2)}, u32[]{:S(2)}) %collective-permute-start.9) | collective-permute-done | bytes 524320 | tf_op jit(solution)/shard_map/ppermute | solution.py:241
  19.2 1.3 %collective-permute-start.1 = (bf16[512,512]{1,0:T(8,128)(2,1)S(1)}, bf16[512,512]{1,0:T(8,128)(2,1)S(1)}, u32[]{:S(2)}, u32[]{:S(2)}) collective-permute-start(bf16[512,512]{1,0:T(8,128)(2,1)S(1)} %get-tuple-element.73), channel_id=1, source_target_pairs={{4,0},{5,1},{6,2},{7,3},{8,4},{9,5},{10,6},{11,7},{12,8},{13,9},{1... | collective-permute-start | bytes 1572872 | tf_op jit(solution)/shard_map/ppermute | solution.py:238
  20.5 1.8 %collective-permute-done.7.refs_2_ = bf16[512,512]{1,0:T(8,128)(2,1)S(1)} collective-permute-done((bf16[512,512]{1,0:T(8,128)(2,1)S(1)}, bf16[512,512]{1,0:T(8,128)(2,1)S(1)}, u32[]{:S(2)}, u32[]{:S(2)}) %collective-permute-start.7) | collective-permute-done | bytes 524320 | tf_op jit(solution)/shard_map/ppermute | solution.py:235
  22.3 4.4 %collective-permute-done.8.refs_2_ = bf16[512,512]{1,0:T(8,128)(2,1)S(1)} collective-permute-done((bf16[512,512]{1,0:T(8,128)(2,1)S(1)}, bf16[512,512]{1,0:T(8,128)(2,1)S(1)}, u32[]{:S(2)}, u32[]{:S(2)}) %collective-permute-start.8) | collective-permute-done | bytes 524320 | tf_op jit(solution)/shard_map/ppermute | solution.py:238
  27.3 1.3 %collective-permute-start.12 = (bf16[512,512]{1,0:T(8,128)(2,1)S(1)}, bf16[512,512]{1,0:T(8,128)(2,1)}, u32[]{:S(2)}, u32[]{:S(2)}) collective-permute-start(bf16[512,512]{1,0:T(8,128)(2,1)S(1)} %collective-permute-done.8.refs_2_), channel_id=1, source_target_pairs={{4,0},{5,1},{6,2},{7,3},{8,4},{9,5},{10,6},{11,7},{12,8},{13,9},{1... | collective-permute-start | bytes 1572872 | tf_op jit(solution)/shard_map/ppermute | solution.py:238
  28.6 1.8 %collective-permute-done.2 = bf16[512,512]{1,0:T(8,128)(2,1)S(1)} collective-permute-done((bf16[512,512]{1,0:T(8,128)(2,1)S(1)}, bf16[512,512]{1,0:T(8,128)(2,1)S(1)}, u32[]{:S(2)}, u32[]{:S(2)}) %collective-permute-start.2) | collective-permute-done | bytes 524320 | tf_op jit(solution)/shard_map/ppermute | solution.py:241
  30.4 4.8 %collective-permute-start.11 = (bf16[512,512]{1,0:T(8,128)(2,1)S(1)}, bf16[512,512]{1,0:T(8,128)(2,1)}, u32[]{:S(2)}, u32[]{:S(2)}) collective-permute-start(bf16[512,512]{1,0:T(8,128)(2,1)S(1)} %collective-permute-done.7.refs_2_), channel_id=1, source_target_pairs={{0,4},{1,5},{2,6},{3,7},{4,8},{5,9},{6,10},{7,11},{8,12},{9,13},{1... | collective-permute-start | bytes 1572872 | tf_op jit(solution)/shard_map/ppermute | solution.py:235
  35.3 2.7 %collective-permute-done.1.refs_2_ = bf16[512,512]{1,0:T(8,128)(2,1)S(1)} collective-permute-done((bf16[512,512]{1,0:T(8,128)(2,1)S(1)}, bf16[512,512]{1,0:T(8,128)(2,1)S(1)}, u32[]{:S(2)}, u32[]{:S(2)}) %collective-permute-start.1) | collective-permute-done | bytes 524320 | tf_op jit(solution)/shard_map/ppermute | solution.py:238
  37.9 1.3 %collective-permute-start.5 = (bf16[512,512]{1,0:T(8,128)(2,1)S(1)}, bf16[512,512]{1,0:T(8,128)(2,1)}, u32[]{:S(2)}, u32[]{:S(2)}) collective-permute-start(bf16[512,512]{1,0:T(8,128)(2,1)S(1)} %collective-permute-done.1.refs_2_), channel_id=1, source_target_pairs={{4,0},{5,1},{6,2},{7,3},{8,4},{9,5},{10,6},{11,7},{12,8},{13,9},{1... | collective-permute-start | bytes 1572872 | tf_op jit(solution)/shard_map/ppermute | solution.py:238
  39.2 0.9 broadcast_select_fusion.6
  40.6 1.1 %collective-permute-done.10 = bf16[512,512]{1,0:T(8,128)(2,1)S(1)} collective-permute-done((bf16[512,512]{1,0:T(8,128)(2,1)S(1)}, bf16[512,512]{1,0:T(8,128)(2,1)S(1)}, u32[]{:S(2)}, u32[]{:S(2)}) %collective-permute-start.10) | collective-permute-done | bytes 524320 | tf_op jit(solution)/shard_map/ppermute | solution.py:241
  41.7 0.8 copy-done.18
  42.5 4.4 %collective-permute-start.4 = (bf16[512,512]{1,0:T(8,128)(2,1)S(1)}, bf16[512,512]{1,0:T(8,128)(2,1)}, u32[]{:S(2)}, u32[]{:S(2)}) collective-permute-start(bf16[512,512]{1,0:T(8,128)(2,1)S(1)} %collective-permute-done.refs_2_), channel_id=1, source_target_pairs={{0,4},{1,5},{2,6},{3,7},{4,8},{5,9},{6,10},{7,11},{8,12},{9,13},{1... | collective-permute-start | bytes 1572872 | tf_op jit(solution)/shard_map/ppermute | solution.py:235
  46.8 2.4 %collective-permute-done.12.refs_3_ = bf16[512,512]{1,0:T(8,128)(2,1)} collective-permute-done((bf16[512,512]{1,0:T(8,128)(2,1)S(1)}, bf16[512,512]{1,0:T(8,128)(2,1)}, u32[]{:S(2)}, u32[]{:S(2)}) %collective-permute-start.12) | collective-permute-done | bytes 524320 | tf_op jit(solution)/shard_map/ppermute | solution.py:238
  49.3 1.9 %broadcast_select_fusion.9 = (bf16[512,512]{1,0:T(8,128)(2,1)S(1)}, bf16[512,512]{1,0:T(8,128)(2,1)S(1)}, bf16[512,512]{1,0:T(8,128)(2,1)S(1)}, bf16[512,512]{1,0:T(8,128)(2,1)S(1)}) fusion(pred[]{:T(512)S(6)} %eq.7, bf16[256,512]{1,0:T(8,128)(2,1)} %copy-done.14, bf16[256,512]{1,0:T(8,128)(2,1)} %copy-done.13, bf16[512,512]{1,0:T(8,128)(2,1)} %copy-done.18, ...), kind=kLoop, calls=%fused_computation.15 | loop fusion | flops 3145728 | bytes 4194306 | tf_op jit(solution)/shard_map/jit(_where)/select_n | solution.py:282
  51.4 0.8 collective-permute-done.3
  52.2 6.6 %collective-permute-done.5.refs_3_ = bf16[512,512]{1,0:T(8,128)(2,1)} collective-permute-done((bf16[512,512]{1,0:T(8,128)(2,1)S(1)}, bf16[512,512]{1,0:T(8,128)(2,1)}, u32[]{:S(2)}, u32[]{:S(2)}) %collective-permute-start.5) | collective-permute-done | bytes 524320 | tf_op jit(solution)/shard_map/ppermute | solution.py:238
  58.8 1.5 %broadcast_select_fusion.11 = (bf16[512,512]{1,0:T(8,128)(2,1)S(1)}, bf16[512,512]{1,0:T(8,128)(2,1)S(1)}, bf16[512,512]{1,0:T(8,128)(2,1)S(1)}, bf16[512,512]{1,0:T(8,128)(2,1)S(1)}) fusion(pred[]{:T(512)S(6)} %eq.7, bf16[256,512]{1,0:T(8,128)(2,1)S(1)} %copy-done.10, bf16[256,512]{1,0:T(8,128)(2,1)S(1)} %copy-done.8, ...), kind=kLoop, calls=%fused_computation.17 | loop fusion | flops 3145728 | bytes 4194306 | tf_op jit(solution)/shard_map/jit(_where)/select_n | solution.py:282
  61.5 7.6 %shard_map.93 = (bf16[256,1024]{1,0:T(8,128)(2,1)}, bf16[256,1024]{1,0:T(8,128)(2,1)}, f32[5,8,256]{2,1,0:T(8,128)S(1)}) custom-call(s32[3]{0:T(128)S(1)} %pad_add_fusion.info, s32[2,8]{1,0:T(2,128)S(1)} %copy-done.4, bf16[256,1024]{1,0:T(8,128)(2,1)S(1)} %copy-done, bf16[256,1024]{1,0:T(8,128)(2,1)S(1)} %copy-done.1, bf16[256,1024]{1,0:T(8,128)(2,1)S(1)} %copy-done.2, ...), custom_call_target="tpu_custom_call" | custom-call | flops 805306368 | bytes 6291456 | tf_op jit(solution)/shard_map/pallas_call | solution.py:210
  69.1 2.6 %collective-permute-start.21 = (f32[5,8,256]{2,1,0:T(8,128)S(1)}, f32[5,8,256]{2,1,0:T(8,128)S(1)}, u32[]{:S(2)}, u32[]{:S(2)}) collective-permute-start(f32[5,8,256]{2,1,0:T(8,128)S(1)} %get-tuple-element.43.refs_4_), channel_id=1, source_target_pairs={{8,0},{9,1},{10,2},{11,3},{12,4},{13,5},{14,6},{15,7},{0,8},{1,9},... | collective-permute-start | bytes 122888 | tf_op jit(solution)/shard_map/ppermute | solution.py:244
  71.6 1.3 %collective-permute-start.20 = (f32[5,8,256]{2,1,0:T(8,128)S(1)}, f32[5,8,256]{2,1,0:T(8,128)S(1)}, u32[]{:S(2)}, u32[]{:S(2)}) collective-permute-start(f32[5,8,256]{2,1,0:T(8,128)S(1)} %get-tuple-element.43.refs_4_), channel_id=1, source_target_pairs={{4,0},{5,1},{6,2},{7,3},{8,4},{9,5},{10,6},{11,7},{12,8},{13,9},{1... | collective-permute-start | bytes 122888 | tf_op jit(solution)/shard_map/ppermute | solution.py:244
  73.9 7.6 %shard_map.94 = (bf16[256,1024]{1,0:T(8,128)(2,1)}, bf16[256,1024]{1,0:T(8,128)(2,1)}, f32[5,8,256]{2,1,0:T(8,128)S(1)}) custom-call(s32[3]{0:T(128)S(1)} %pad_add_fusion.info, s32[2,8]{1,0:T(2,128)S(1)} %copy-done.4, bf16[256,1024]{1,0:T(8,128)(2,1)S(1)} %copy-done, ...), custom_call_target="tpu_custom_call", output_to_operand_aliasing={{0}: (10, {}), {1}: (11, {})} | custom-call | flops 805306368 | bytes 6291456 | tf_op jit(solution)/shard_map/pallas_call | solution.py:210
  81.5 1.7 %collective-permute-start.17 = (f32[5,8,256]{2,1,0:T(8,128)S(1)}, f32[5,8,256]{2,1,0:T(8,128)S(1)}, u32[]{:S(2)}, u32[]{:S(2)}) collective-permute-start(f32[5,8,256]{2,1,0:T(8,128)S(1)} %get-tuple-element.41.refs_4_), channel_id=1, source_target_pairs={{8,0},{9,1},{10,2},{11,3},{12,4},{13,5},{14,6},{15,7},{0,8},{1,9},... | collective-permute-start | bytes 122888 | tf_op jit(solution)/shard_map/ppermute | solution.py:244
  83.2 2.2 %collective-permute-start.16 = (f32[5,8,256]{2,1,0:T(8,128)S(1)}, f32[5,8,256]{2,1,0:T(8,128)S(1)}, u32[]{:S(2)}, u32[]{:S(2)}) collective-permute-start(f32[5,8,256]{2,1,0:T(8,128)S(1)} %get-tuple-element.41.refs_4_), channel_id=1, source_target_pairs={{4,0},{5,1},{6,2},{7,3},{8,4},{9,5},{10,6},{11,7},{12,8},{13,9},{1... | collective-permute-start | bytes 122888 | tf_op jit(solution)/shard_map/ppermute | solution.py:244
  85.5 1.0 %collective-permute-start.15 = (f32[5,8,256]{2,1,0:T(8,128)S(1)}, f32[5,8,256]{2,1,0:T(8,128)S(1)}, u32[]{:S(2)}, u32[]{:S(2)}) collective-permute-start(f32[5,8,256]{2,1,0:T(8,128)S(1)} %get-tuple-element.41.refs_4_), channel_id=1, source_target_pairs={{2,0},{3,1},{4,2},{5,3},{6,4},{7,5},{8,6},{9,7},{10,8},{11,9},{12,... | collective-permute-start | bytes 122888 | tf_op jit(solution)/shard_map/ppermute | solution.py:244
  86.5 5.3 %shard_map.95 = (bf16[256,1024]{1,0:T(8,128)(2,1)}, bf16[256,1024]{1,0:T(8,128)(2,1)}) custom-call(s32[3]{0:T(128)S(1)} %pad_add_fusion.info, bf16[256,1024]{1,0:T(8,128)(2,1)S(1)} %copy-done, bf16[256,1024]{1,0:T(8,128)(2,1)S(1)} %copy-done.1, bf16[256,1024]{1,0:T(8,128)(2,1)S(1)} %copy-done.2, bf16[256,1024]{1,0:T(8,128)(2,1)S(1)} %copy-done.3, ...), custom_call_target="tpu_custom_call" | custom-call | flops 805306368 | bytes 6291456 | tf_op jit(solution)/shard_map/pallas_call | solution.py:210
  91.8 5.3 %shard_map.96 = (bf16[256,1024]{1,0:T(8,128)(2,1)}, bf16[256,1024]{1,0:T(8,128)(2,1)}) custom-call(s32[3]{0:T(128)S(1)} %pad_add_fusion.info, bf16[256,1024]{1,0:T(8,128)(2,1)S(1)} %copy-done, bf16[256,1024]{1,0:T(8,128)(2,1)S(1)} %copy-done.1, bf16[256,1024]{1,0:T(8,128)(2,1)S(1)} %copy-done.2, ...), custom_call_target="tpu_custom_call", output_to_operand_aliasing={{0}: (14, {}), {1}: (15, {})} | custom-call | flops 805306368 | bytes 6291456 | tf_op jit(solution)/shard_map/pallas_call | solution.py:210
  (65 shorter events, 4.8 us)
Async XLA Ops:
  0.7 1.5 %copy-start.2 = (bf16[256,1024]{1,0:T(8,128)(2,1)S(1)}, bf16[256,1024]{1,0:T(8,128)(2,1)}, u32[]{:S(2)}) copy-start(bf16[256,1024]{1,0:T(8,128)(2,1)} %v_ref.7) | copy-start | bytes 1572868
  2.2 9.1 %copy-start.5 = (bf16[256,512]{1,0:T(8,128)(2,1)}, bf16[256,512]{1,0:T(8,128)(2,1)S(1)}, u32[]{:S(2)}) copy-start(bf16[256,512]{1,0:T(8,128)(2,1)S(1)} %get-tuple-element.76) | copy-start | bytes 786436
  2.3 9.0 %copy-start.7 = (bf16[256,512]{1,0:T(8,128)(2,1)}, bf16[256,512]{1,0:T(8,128)(2,1)S(1)}, u32[]{:S(2)}) copy-start(bf16[256,512]{1,0:T(8,128)(2,1)S(1)} %get-tuple-element.64) | copy-start | bytes 786436
  2.3 9.0 %copy-start.9 = (bf16[256,512]{1,0:T(8,128)(2,1)}, bf16[256,512]{1,0:T(8,128)(2,1)S(1)}, u32[]{:S(2)}) copy-start(bf16[256,512]{1,0:T(8,128)(2,1)S(1)} %get-tuple-element.74) | copy-start | bytes 786436
  3.4 15.8 %collective-permute-start.9 = (bf16[512,512]{1,0:T(8,128)(2,1)S(1)}, bf16[512,512]{1,0:T(8,128)(2,1)S(1)}, u32[]{:S(2)}, u32[]{:S(2)}) collective-permute-start(bf16[512,512]{1,0:T(8,128)(2,1)S(1)} %get-tuple-element.60), channel_id=1, source_target_pairs={{0,2},{1,3},{2,0},{3,1},{4,6},{5,7},{6,4},{7,5},{8,10},{9,11},{10,... | collective-permute-start | bytes 1572872 | tf_op jit(solution)/shard_map/ppermute | solution.py:241
  6.4 15.8 %collective-permute-start.7 = (bf16[512,512]{1,0:T(8,128)(2,1)S(1)}, bf16[512,512]{1,0:T(8,128)(2,1)S(1)}, u32[]{:S(2)}, u32[]{:S(2)}) collective-permute-start(bf16[512,512]{1,0:T(8,128)(2,1)S(1)} %get-tuple-element.61), channel_id=1, source_target_pairs={{0,4},{1,5},{2,6},{3,7},{4,8},{5,9},{6,10},{7,11},{8,12},{9,13},{1... | collective-permute-start | bytes 1572872 | tf_op jit(solution)/shard_map/ppermute | solution.py:235
  9.9 16.8 %collective-permute-start.8 = (bf16[512,512]{1,0:T(8,128)(2,1)S(1)}, bf16[512,512]{1,0:T(8,128)(2,1)S(1)}, u32[]{:S(2)}, u32[]{:S(2)}) collective-permute-start(bf16[512,512]{1,0:T(8,128)(2,1)S(1)} %get-tuple-element.62), channel_id=1, source_target_pairs={{4,0},{5,1},{6,2},{7,3},{8,4},{9,5},{10,6},{11,7},{12,8},{13,9},{1... | collective-permute-start | bytes 1572872 | tf_op jit(solution)/shard_map/ppermute | solution.py:238
  11.5 18.9 %collective-permute-start.2 = (bf16[512,512]{1,0:T(8,128)(2,1)S(1)}, bf16[512,512]{1,0:T(8,128)(2,1)S(1)}, u32[]{:S(2)}, u32[]{:S(2)}) collective-permute-start(bf16[512,512]{1,0:T(8,128)(2,1)S(1)} %get-tuple-element.71), channel_id=1, source_target_pairs={{0,2},{1,3},{2,0},{3,1},{4,6},{5,7},{6,4},{7,5},{8,10},{9,11},{10,... | collective-permute-start | bytes 1572872 | tf_op jit(solution)/shard_map/ppermute | solution.py:241
  12.1 23.2 %collective-permute-start = (bf16[512,512]{1,0:T(8,128)(2,1)S(1)}, bf16[512,512]{1,0:T(8,128)(2,1)S(1)}, u32[]{:S(2)}, u32[]{:S(2)}) collective-permute-start(bf16[512,512]{1,0:T(8,128)(2,1)S(1)} %get-tuple-element.72), channel_id=1, source_target_pairs={{0,4},{1,5},{2,6},{3,7},{4,8},{5,9},{6,10},{7,11},{8,12},{9,13},{1... | collective-permute-start | bytes 1572872 | tf_op jit(solution)/shard_map/ppermute | solution.py:235
  19.2 20.9 %copy-start.17 = (bf16[512,512]{1,0:T(8,128)(2,1)}, bf16[512,512]{1,0:T(8,128)(2,1)S(1)}, u32[]{:S(2)}) copy-start(bf16[512,512]{1,0:T(8,128)(2,1)S(1)} %collective-permute-done.9) | copy-start | bytes 1572868
  19.2 18.7 %collective-permute-start.1 = (bf16[512,512]{1,0:T(8,128)(2,1)S(1)}, bf16[512,512]{1,0:T(8,128)(2,1)S(1)}, u32[]{:S(2)}, u32[]{:S(2)}) collective-permute-start(bf16[512,512]{1,0:T(8,128)(2,1)S(1)} %get-tuple-element.73), channel_id=1, source_target_pairs={{4,0},{5,1},{6,2},{7,3},{8,4},{9,5},{10,6},{11,7},{12,8},{13,9},{1... | collective-permute-start | bytes 1572872 | tf_op jit(solution)/shard_map/ppermute | solution.py:238
  26.8 14.9 %collective-permute-start.10 = (bf16[512,512]{1,0:T(8,128)(2,1)S(1)}, bf16[512,512]{1,0:T(8,128)(2,1)S(1)}, u32[]{:S(2)}, u32[]{:S(2)}) collective-permute-start(bf16[512,512]{1,0:T(8,128)(2,1)S(1)} %broadcast_select_fusion.2), channel_id=1, source_target_pairs={{0,2},{1,3},{2,0},{3,1},{4,6},{5,7},{6,4},{7,5},{8,10},{9,11},{10,... | collective-permute-start | bytes 1572872 | tf_op jit(solution)/shard_map/ppermute | solution.py:241
  27.3 21.9 %collective-permute-start.12 = (bf16[512,512]{1,0:T(8,128)(2,1)S(1)}, bf16[512,512]{1,0:T(8,128)(2,1)}, u32[]{:S(2)}, u32[]{:S(2)}) collective-permute-start(bf16[512,512]{1,0:T(8,128)(2,1)S(1)} %collective-permute-done.8.refs_2_), channel_id=1, source_target_pairs={{4,0},{5,1},{6,2},{7,3},{8,4},{9,5},{10,6},{11,7},{12,8},{13,9},{1... | collective-permute-start | bytes 1572872 | tf_op jit(solution)/shard_map/ppermute | solution.py:238
  30.4 10.2 %copy-start.15 = (bf16[512,512]{1,0:T(8,128)(2,1)}, bf16[512,512]{1,0:T(8,128)(2,1)S(1)}, u32[]{:S(2)}) copy-start(bf16[512,512]{1,0:T(8,128)(2,1)S(1)} %collective-permute-done.2) | copy-start | bytes 1572868
  30.4 18.9 %collective-permute-start.11 = (bf16[512,512]{1,0:T(8,128)(2,1)S(1)}, bf16[512,512]{1,0:T(8,128)(2,1)}, u32[]{:S(2)}, u32[]{:S(2)}) collective-permute-start(bf16[512,512]{1,0:T(8,128)(2,1)S(1)} %collective-permute-done.7.refs_2_), channel_id=1, source_target_pairs={{0,4},{1,5},{2,6},{3,7},{4,8},{5,9},{6,10},{7,11},{8,12},{9,13},{1... | collective-permute-start | bytes 1572872 | tf_op jit(solution)/shard_map/ppermute | solution.py:235
  37.9 20.8 %collective-permute-start.5 = (bf16[512,512]{1,0:T(8,128)(2,1)S(1)}, bf16[512,512]{1,0:T(8,128)(2,1)}, u32[]{:S(2)}, u32[]{:S(2)}) collective-permute-start(bf16[512,512]{1,0:T(8,128)(2,1)S(1)} %collective-permute-done.1.refs_2_), channel_id=1, source_target_pairs={{4,0},{5,1},{6,2},{7,3},{8,4},{9,5},{10,6},{11,7},{12,8},{13,9},{1... | collective-permute-start | bytes 1572872 | tf_op jit(solution)/shard_map/ppermute | solution.py:238
  40.1 12.1 %collective-permute-start.3 = (bf16[512,512]{1,0:T(8,128)(2,1)}, bf16[512,512]{1,0:T(8,128)(2,1)}, u32[]{:S(2)}, u32[]{:S(2)}) collective-permute-start(bf16[512,512]{1,0:T(8,128)(2,1)} %broadcast_select_fusion.6), channel_id=1, source_target_pairs={{0,2},{1,3},{2,0},{3,1},{4,6},{5,7},{6,4},{7,5},{8,10},{9,11},{10,... | collective-permute-start | bytes 1572872 | tf_op jit(solution)/shard_map/ppermute | solution.py:241
  42.5 16.3 %collective-permute-start.4 = (bf16[512,512]{1,0:T(8,128)(2,1)S(1)}, bf16[512,512]{1,0:T(8,128)(2,1)}, u32[]{:S(2)}, u32[]{:S(2)}) collective-permute-start(bf16[512,512]{1,0:T(8,128)(2,1)S(1)} %collective-permute-done.refs_2_), channel_id=1, source_target_pairs={{0,4},{1,5},{2,6},{3,7},{4,8},{5,9},{6,10},{7,11},{8,12},{9,13},{1... | collective-permute-start | bytes 1572872 | tf_op jit(solution)/shard_map/ppermute | solution.py:235
  51.2 7.5 %copy-start.6 = (bf16[256,512]{1,0:T(8,128)(2,1)S(1)}, bf16[256,512]{1,0:T(8,128)(2,1)}, u32[]{:S(2)}) copy-start(bf16[256,512]{1,0:T(8,128)(2,1)} %copy-done.5) | copy-start | bytes 786436
  51.2 7.5 %copy-start.8 = (bf16[256,512]{1,0:T(8,128)(2,1)S(1)}, bf16[256,512]{1,0:T(8,128)(2,1)}, u32[]{:S(2)}) copy-start(bf16[256,512]{1,0:T(8,128)(2,1)} %copy-done.7) | copy-start | bytes 786436
  51.2 7.5 %copy-start.10 = (bf16[256,512]{1,0:T(8,128)(2,1)S(1)}, bf16[256,512]{1,0:T(8,128)(2,1)}, u32[]{:S(2)}) copy-start(bf16[256,512]{1,0:T(8,128)(2,1)} %copy-done.9) | copy-start | bytes 786436
  51.2 7.5 %copy-start.16 = (bf16[512,512]{1,0:T(8,128)(2,1)S(1)}, bf16[512,512]{1,0:T(8,128)(2,1)}, u32[]{:S(2)}) copy-start(bf16[512,512]{1,0:T(8,128)(2,1)} %copy-done.15) | copy-start | bytes 1572868
  51.3 9.9 %collective-permute-start.13 = (bf16[1024,512]{1,0:T(8,128)(2,1)S(1)}, bf16[1024,512]{1,0:T(8,128)(2,1)S(1)}, u32[]{:S(2)}, u32[]{:S(2)}) collective-permute-start(bf16[1024,512]{1,0:T(8,128)(2,1)S(1)} %pad_maximum_fusion.1), channel_id=1, source_target_pairs={{0,1},{1,0},{2,3},{3,2},{4,5},{5,4},{6,7},{7,6},{8,9},{9,8},{10,11... | collective-permute-start | bytes 3145736 | tf_op jit(solution)/shard_map/ppermute | solution.py:241
  60.4 13.6 %collective-permute-start.6 = (bf16[1024,512]{1,0:T(8,128)(2,1)S(1)}, bf16[1024,512]{1,0:T(8,128)(2,1)S(1)}, u32[]{:S(2)}, u32[]{:S(2)}) collective-permute-start(bf16[1024,512]{1,0:T(8,128)(2,1)S(1)} %pad_maximum_fusion), channel_id=1, source_target_pairs={{0,1},{1,0},{2,3},{3,2},{4,5},{5,4},{6,7},{7,6},{8,9},{9,8},{10,11... | collective-permute-start | bytes 3145736 | tf_op jit(solution)/shard_map/ppermute | solution.py:241
  69.1 14.1 %collective-permute-start.21 = (f32[5,8,256]{2,1,0:T(8,128)S(1)}, f32[5,8,256]{2,1,0:T(8,128)S(1)}, u32[]{:S(2)}, u32[]{:S(2)}) collective-permute-start(f32[5,8,256]{2,1,0:T(8,128)S(1)} %get-tuple-element.43.refs_4_), channel_id=1, source_target_pairs={{8,0},{9,1},{10,2},{11,3},{12,4},{13,5},{14,6},{15,7},{0,8},{1,9},... | collective-permute-start | bytes 122888 | tf_op jit(solution)/shard_map/ppermute | solution.py:244
  71.6 13.8 %collective-permute-start.20 = (f32[5,8,256]{2,1,0:T(8,128)S(1)}, f32[5,8,256]{2,1,0:T(8,128)S(1)}, u32[]{:S(2)}, u32[]{:S(2)}) collective-permute-start(f32[5,8,256]{2,1,0:T(8,128)S(1)} %get-tuple-element.43.refs_4_), channel_id=1, source_target_pairs={{4,0},{5,1},{6,2},{7,3},{8,4},{9,5},{10,6},{11,7},{12,8},{13,9},{1... | collective-permute-start | bytes 122888 | tf_op jit(solution)/shard_map/ppermute | solution.py:244
  73.0 13.5 %collective-permute-start.19 = (f32[5,8,256]{2,1,0:T(8,128)S(1)}, f32[5,8,256]{2,1,0:T(8,128)S(1)}, u32[]{:S(2)}, u32[]{:S(2)}) collective-permute-start(f32[5,8,256]{2,1,0:T(8,128)S(1)} %get-tuple-element.43.refs_4_), channel_id=1, source_target_pairs={{2,0},{3,1},{4,2},{5,3},{6,4},{7,5},{8,6},{9,7},{10,8},{11,9},{12,... | collective-permute-start | bytes 122888 | tf_op jit(solution)/shard_map/ppermute | solution.py:244
  73.4 13.1 %collective-permute-start.18 = (f32[5,8,256]{2,1,0:T(8,128)S(1)}, f32[5,8,256]{2,1,0:T(8,128)S(1)}, u32[]{:S(2)}, u32[]{:S(2)}) collective-permute-start(f32[5,8,256]{2,1,0:T(8,128)S(1)} %get-tuple-element.43.refs_4_), channel_id=1, source_target_pairs={{1,0},{2,1},{3,2},{4,3},{5,4},{6,5},{7,6},{8,7},{9,8},{10,9},{11,1... | collective-permute-start | bytes 122888 | tf_op jit(solution)/shard_map/ppermute | solution.py:244
  81.5 10.2 %collective-permute-start.17 = (f32[5,8,256]{2,1,0:T(8,128)S(1)}, f32[5,8,256]{2,1,0:T(8,128)S(1)}, u32[]{:S(2)}, u32[]{:S(2)}) collective-permute-start(f32[5,8,256]{2,1,0:T(8,128)S(1)} %get-tuple-element.41.refs_4_), channel_id=1, source_target_pairs={{8,0},{9,1},{10,2},{11,3},{12,4},{13,5},{14,6},{15,7},{0,8},{1,9},... | collective-permute-start | bytes 122888 | tf_op jit(solution)/shard_map/ppermute | solution.py:244
  83.2 8.6 %collective-permute-start.16 = (f32[5,8,256]{2,1,0:T(8,128)S(1)}, f32[5,8,256]{2,1,0:T(8,128)S(1)}, u32[]{:S(2)}, u32[]{:S(2)}) collective-permute-start(f32[5,8,256]{2,1,0:T(8,128)S(1)} %get-tuple-element.41.refs_4_), channel_id=1, source_target_pairs={{4,0},{5,1},{6,2},{7,3},{8,4},{9,5},{10,6},{11,7},{12,8},{13,9},{1... | collective-permute-start | bytes 122888 | tf_op jit(solution)/shard_map/ppermute | solution.py:244
  85.5 6.3 %collective-permute-start.15 = (f32[5,8,256]{2,1,0:T(8,128)S(1)}, f32[5,8,256]{2,1,0:T(8,128)S(1)}, u32[]{:S(2)}, u32[]{:S(2)}) collective-permute-start(f32[5,8,256]{2,1,0:T(8,128)S(1)} %get-tuple-element.41.refs_4_), channel_id=1, source_target_pairs={{2,0},{3,1},{4,2},{5,3},{6,4},{7,5},{8,6},{9,7},{10,8},{11,9},{12,... | collective-permute-start | bytes 122888 | tf_op jit(solution)/shard_map/ppermute | solution.py:244
  86.5 5.3 %collective-permute-start.14 = (f32[5,8,256]{2,1,0:T(8,128)S(1)}, f32[5,8,256]{2,1,0:T(8,128)S(1)}, u32[]{:S(2)}, u32[]{:S(2)}) collective-permute-start(f32[5,8,256]{2,1,0:T(8,128)S(1)} %get-tuple-element.41.refs_4_), channel_id=1, source_target_pairs={{1,0},{2,1},{3,2},{4,3},{5,4},{6,5},{7,6},{8,7},{9,8},{10,9},{11,1... | collective-permute-start | bytes 122888 | tf_op jit(solution)/shard_map/ppermute | solution.py:244
  (9 other events, 9.6 us)

commit v2 on v1

--- a/solution.py
+++ b/solution.py
@@ -12,7 +12,9 @@
 BLOCK = 128
 LEVELS = 8
 CHUNKS = 2
-HEADS_STEP = 2
+HEADS_STEP = 4
+QUERY_LAG = (0, 1, 2, 3)
+KEY_LAG = (0, 1, 1)
 FAR = 1e30
 SCALE = HEAD_DIM ** (-0.5)
 SCALE2 = SCALE * math.log2(math.e)
@@ -28,12 +30,11 @@
     return jnp.dot(left, right, preferred_element_type=jnp.float32)
 
 
-def head_columns(array, head):
-    return array[:, head * HEAD_DIM : (head + 1) * HEAD_DIM]
-
-
-def block_rows(array, index):
-    return array[index * BLOCK : (index + 1) * BLOCK]
+def staged(units, stages, lags):
+    for turn in range(len(units) + max(lags)):
+        for stage, lag in zip(stages, lags):
+            if 0 <= turn - lag < len(units):
+                stage(units[turn - lag])
 
 
 def query_kernel(hops, fresh, info, kb, q_ref, k_ref, v_ref, g_ref, *refs):
@@ -76,41 +77,67 @@
             stat_ref[stat_ref.shape[0] - 1, :, block * BLOCK : (block + 1) * BLOCK] = flags
 
     lane = lax.broadcasted_iota(jnp.int32, (BLOCK, BLOCK), 1)
-    for head in range(HEADS_STEP):
-        query, key, value, grad = (
-            head_columns(ref, head) for ref in (q_ref[...], k_ref[...], v_ref[...], g_ref[...])
-        )
-        far = [head_columns(ref[...], head) for ref in behind]
-        for block in range(2):
-
-            def stack(own, which):
-                parts = [block_rows(own, block)]
-                parts.append(block_rows(far[0], which * 2 + 1) if block == 0 else block_rows(own, 0))
-                parts += [block_rows(piece, which * 2 + block) for piece in far]
-                return jnp.concatenate(parts, axis=0)
-
-            key_rows, value_rows = stack(key, 0), stack(value, 1)
-            query_here, grad_here = block_rows(query, block), block_rows(grad, block)
-            scores = product_rows(query_here, key_rows) * SCALE2 + bias_ref[block]
-            row_max = jnp.max(scores, axis=1, keepdims=True)
-            raw = jnp.exp2(scores - row_max)
-            total = jnp.sum(raw, axis=1, keepdims=True)
-            inverse = jnp.where(rows_ok(block), 1.0 / total, 0.0)
-            weights = raw * inverse
-            attended = product(weights.astype(jnp.bfloat16), value_rows).astype(jnp.bfloat16)
-            delta = jnp.sum(
-                grad_here.astype(jnp.float32) * attended.astype(jnp.float32), axis=1, keepdims=True
-            )
-            weight_grad = product_rows(grad_here, value_rows)
-            score_grad = (weights * (weight_grad - delta)).astype(jnp.bfloat16)
-            query_grad = (product(score_grad, key_rows) * SCALE).astype(jnp.bfloat16)
-            rows = slice(block * BLOCK, (block + 1) * BLOCK)
-            columns = slice(head * HEAD_DIM, (head + 1) * HEAD_DIM)
-            att_ref[rows, columns] = attended
-            dq_ref[rows, columns] = query_grad
-            top = jnp.where(rows_ok(block), row_max, FAR)
-            packed = jnp.where(lane == 0, top, jnp.where(lane == 1, inverse, delta))
-            stat_ref[step * HEADS_STEP + head, :, rows] = packed.T[:8]
+    units = [(head, block) for head in range(HEADS_STEP) for block in range(2)]
+    held = {}
+
+    def stack(unit, own_ref, which):
+        head, block = unit
+        columns = slice(head * HEAD_DIM, (head + 1) * HEAD_DIM)
+
+        def part(ref, index):
+            return ref[index * BLOCK : (index + 1) * BLOCK, columns]
+
+        parts = [part(own_ref, block)]
+        parts.append(part(behind[0], which * 2 + 1) if block == 0 else part(own_ref, 0))
+        parts += [part(ref, which * 2 + block) for ref in behind]
+        return jnp.concatenate(parts, axis=0)
+
+    def place(unit):
+        head, block = unit
+        return (
+            slice(block * BLOCK, (block + 1) * BLOCK),
+            slice(head * HEAD_DIM, (head + 1) * HEAD_DIM),
+        )
+
+    def products(unit):
+        rows, columns = place(unit)
+        scores = product_rows(q_ref[rows, columns], stack(unit, k_ref, 0))
+        weight_grad = product_rows(g_ref[rows, columns], stack(unit, v_ref, 1))
+        held[unit] = (scores, weight_grad)
+
+    def soften(unit):
+        scores, weight_grad = held[unit]
+        scores = scores * SCALE2 + bias_ref[unit[1]]
+        row_max = jnp.max(scores, axis=1, keepdims=True)
+        raw = jnp.exp2(scores - row_max)
+        total = jnp.sum(raw, axis=1, keepdims=True)
+        inverse = jnp.where(rows_ok(unit[1]), 1.0 / total, 0.0)
+        weights = raw * inverse
+        held[unit] = (weights, weight_grad, row_max, inverse)
+
+    def attend(unit):
+        weights, weight_grad, row_max, inverse = held[unit]
+        rows, columns = place(unit)
+        attended = product(weights.astype(jnp.bfloat16), stack(unit, v_ref, 1)).astype(jnp.bfloat16)
+        grad_here = g_ref[rows, columns]
+        delta = jnp.sum(
+            grad_here.astype(jnp.float32) * attended.astype(jnp.float32), axis=1, keepdims=True
+        )
+        att_ref[rows, columns] = attended
+        top = jnp.where(rows_ok(unit[1]), row_max, FAR)
+        packed = jnp.where(lane == 0, top, jnp.where(lane == 1, inverse, delta))
+        stat_ref[step * HEADS_STEP + unit[0], :, rows] = packed.T[:8]
+        held[unit] = (weights, weight_grad, delta)
+
+    def finish(unit):
+        weights, weight_grad, delta = held[unit]
+        rows, columns = place(unit)
+        score_grad = (weights * (weight_grad - delta)).astype(jnp.bfloat16)
+        dq_ref[rows, columns] = (product(score_grad, stack(unit, k_ref, 0)) * SCALE).astype(
+            jnp.bfloat16
+        )
+
+    staged(units, (products, soften, attend, finish), QUERY_LAG)
 
 
 def key_kernel(hops, fresh, info, q_ref, k_ref, v_ref, g_ref, *refs):
@@ -121,58 +148,78 @@
     step = pl.program_id(0)
     device, valid, devices = info[0], info[1], info[2]
     flags = [ref[ref.shape[0] - 1] for ref in stats]
-    for head in range(HEADS_STEP):
-        query, key, value, grad = (
-            head_columns(ref, head) for ref in (q_ref[...], k_ref[...], v_ref[...], g_ref[...])
-        )
-        far = [head_columns(ref[...], head) for ref in ahead]
+    units = [(head, block) for head in range(HEADS_STEP) for block in range(2)]
+    held = {}
+
+    def stack(unit, own_ref, which):
+        head, block = unit
+        columns = slice(head * HEAD_DIM, (head + 1) * HEAD_DIM)
+
+        def part(ref, index):
+            return ref[index * BLOCK : (index + 1) * BLOCK, columns]
+
+        parts = [part(own_ref, block)]
+        parts.append(part(own_ref, 1) if block == 0 else part(ahead[0], which * 2))
+        parts += [part(ref, which * 2 + block) for ref in ahead]
+        return jnp.concatenate(parts, axis=0)
+
+    def place(unit):
+        head, block = unit
+        return (
+            slice(block * BLOCK, (block + 1) * BLOCK),
+            slice(head * HEAD_DIM, (head + 1) * HEAD_DIM),
+        )
+
+    def lanes(array, row, index):
+        return array[row : row + 1, index * BLOCK : (index + 1) * BLOCK]
+
+    def products(unit):
+        rows, columns = place(unit)
+        scores = product_rows(k_ref[rows, columns], stack(unit, q_ref, 0))
+        weight_grad = product_rows(v_ref[rows, columns], stack(unit, g_ref, 1))
+        held[unit] = (scores, weight_grad)
+
+    def soften(unit):
+        head, block = unit
+        scores, weight_grad = held[unit]
         stat = [ref[step * HEADS_STEP + head] for ref in stats]
-        for block in range(2):
-
-            def stack(own, which):
-                parts = [block_rows(own, block)]
-                parts.append(block_rows(own, 1) if block == 0 else block_rows(far[0], which * 2))
-                parts += [block_rows(piece, which * 2 + block) for piece in far]
-                return jnp.concatenate(parts, axis=0)
-
-            def lanes(array, row, index):
-                return array[row : row + 1, index * BLOCK : (index + 1) * BLOCK]
-
-            sources = [(0, block, None)]
-            sources.append((0, 1, 0) if block == 0 else (1, 0, 0))
-            sources += [(1 + index, block, index + 1) for index in range(count)]
-            row_max, inverse, delta = [], [], []
-            for source, at, level in sources:
-                top = lanes(stat[source], 0, at)
-                if level is not None:
-                    flag = lanes(flags[source], level, at)
-                    if source > 0:
-                        flag = jnp.where(device + hops[source - 1] < devices, flag, 0.0)
-                    top = jnp.where(flag > 0.5, top, FAR)
-                row_max.append(top)
-                inverse.append(lanes(stat[source], 1, at))
-                delta.append(lanes(stat[source], 2, at))
-            row_max, inverse, delta = (
-                jnp.concatenate(parts, axis=1) for parts in (row_max, inverse, delta)
-            )
-            query_rows, grad_rows = stack(query, 0), stack(grad, 1)
-            key_here, value_here = block_rows(key, block), block_rows(value, block)
-            scores = product_rows(key_here, query_rows) * SCALE2 - row_max
-            key_index = lax.broadcasted_iota(jnp.int32, (BLOCK, BLOCK), 0)
-            query_index = lax.broadcasted_iota(jnp.int32, (BLOCK, BLOCK), 1)
-            causal = jnp.where(key_index <= query_index, scores[:, :BLOCK], -FAR)
-            scores = jnp.concatenate([causal, scores[:, BLOCK:]], axis=1)
-            weights = jnp.exp2(scores) * inverse
-            value_grad = product(weights.astype(jnp.bfloat16), grad_rows)
-            weight_grad = product_rows(value_here, grad_rows)
-            score_grad = (weights * (weight_grad - delta)).astype(jnp.bfloat16)
-            key_grad = product(score_grad, query_rows) * SCALE
-            at = (device * 2 + block) * BLOCK
-            key_ok = at + lax.broadcasted_iota(jnp.int32, (BLOCK, 1), 0) < valid
-            rows = slice(block * BLOCK, (block + 1) * BLOCK)
-            columns = slice(head * HEAD_DIM, (head + 1) * HEAD_DIM)
-            dk_ref[rows, columns] = jnp.where(key_ok, key_grad, 0.0).astype(jnp.bfloat16)
-            dv_ref[rows, columns] = jnp.where(key_ok, value_grad, 0.0).astype(jnp.bfloat16)
+        sources = [(0, block, None)]
+        sources.append((0, 1, 0) if block == 0 else (1, 0, 0))
+        sources += [(1 + index, block, index + 1) for index in range(count)]
+        row_max, inverse, delta = [], [], []
+        for source, at, level in sources:
+            top = lanes(stat[source], 0, at)
+            if level is not None:
+                flag = lanes(flags[source], level, at)
+                if source > 0:
+                    flag = jnp.where(device + hops[source - 1] < devices, flag, 0.0)
+                top = jnp.where(flag > 0.5, top, FAR)
+            row_max.append(top)
+            inverse.append(lanes(stat[source], 1, at))
+            delta.append(lanes(stat[source], 2, at))
+        row_max, inverse, delta = (
+            jnp.concatenate(parts, axis=1) for parts in (row_max, inverse, delta)
+        )
+        scores = scores * SCALE2 - row_max
+        key_index = lax.broadcasted_iota(jnp.int32, (BLOCK, BLOCK), 0)
+        query_index = lax.broadcasted_iota(jnp.int32, (BLOCK, BLOCK), 1)
+        causal = jnp.where(key_index <= query_index, scores[:, :BLOCK], -FAR)
+        scores = jnp.concatenate([causal, scores[:, BLOCK:]], axis=1)
+        weights = jnp.exp2(scores) * inverse
+        score_grad = (weights * (weight_grad - delta)).astype(jnp.bfloat16)
+        held[unit] = (weights.astype(jnp.bfloat16), score_grad)
+
+    def finish(unit):
+        weights_low, score_grad = held[unit]
+        rows, columns = place(unit)
+        value_grad = product(weights_low, stack(unit, g_ref, 1))
+        key_grad = product(score_grad, stack(unit, q_ref, 0)) * SCALE
+        at = (device * 2 + unit[1]) * BLOCK
+        key_ok = at + lax.broadcasted_iota(jnp.int32, (BLOCK, 1), 0) < valid
+        dk_ref[rows, columns] = jnp.where(key_ok, key_grad, 0.0).astype(jnp.bfloat16)
+        dv_ref[rows, columns] = jnp.where(key_ok, value_grad, 0.0).astype(jnp.bfloat16)
+
+    staged(units, (products, soften, finish), KEY_LAG)
 
 
 def call(kernel, chunk, heads, scalars, own, others, whole, previous, out_shapes, scratch, flops):
@@ -263,7 +310,13 @@
                 swap(jnp.where(side == 0, key_pack, query_pack), 2),
             )
         )
-    moved = []
+    own = (queries, keys, values, out_grad)
+    full = jax.ShapeDtypeStruct((rows_dev, columns), jnp.bfloat16)
+    stat_shape = jax.ShapeDtypeStruct((heads + 1, 8, rows_dev), jnp.float32)
+    pieces = 2 + len(hops)
+    flops = heads * 2 * pieces * 4 * 2 * BLOCK**3
+
+    middle = []
     for (key_pack, query_pack), stage in zip(packs, first):
         key_4, query_4, side_1 = lax.optimization_barrier(stage)
         side_2 = swap(jnp.where(side == 0, query_4, key_4), 2)
@@ -273,6 +326,11 @@
             keys_by[steps * 2] = up(keys_by[steps], steps)
             queries_by[steps * 2] = down(queries_by[steps], steps)
             steps *= 2
+        middle.append((side_1, side_2, keys_by, queries_by))
+
+    front, stats, moved = (), [], []
+    for chunk in range(CHUNKS):
+        (key_pack, query_pack), (side_1, side_2, keys_by, queries_by) = packs[chunk], middle[chunk]
         side_2, keys_by[8], queries_by[8] = lax.optimization_barrier((side_2, keys_by[8], queries_by[8]))
         keys_by[2] = jnp.where(side == 0, side_2, side_1)
         queries_by[2] = jnp.where(side == 0, side_1, side_2)
@@ -292,16 +350,8 @@
                 [(neighbour, 1)] + [(queries_by[hop], 0) for hop in hops[1:]],
             )
         )
-    own = (queries, keys, values, out_grad)
-    full = jax.ShapeDtypeStruct((rows_dev, columns), jnp.bfloat16)
-    stat_shape = jax.ShapeDtypeStruct((heads + 1, 8, rows_dev), jnp.float32)
-    pieces = 2 + len(hops)
-    flops = heads * 2 * pieces * 4 * 2 * BLOCK**3
-    front, stats = (), []
-    for chunk in range(CHUNKS):
-        fresh = chunk == 0
         att, dq, stat = call(
-            functools.partial(query_kernel, hops, fresh),
+            functools.partial(query_kernel, hops, chunk == 0),
             chunk,
             heads,
             (info, key_blocks),

time: 97.6 us -> 88.8 us (0.910)
  Pallas kernels: 25.8 us -> 16.8 us
    pallas_call x4, Pallas kernels: 25.8 us -> 16.8 us  [call(): pl.pallas_call(kernel, grid=(steps,), in_specs=in_specs, out_specs=out_sp...]
  transfers between devices with their start and end apart: 22 -> 22, of which waited for: 9 -> 9; matrix products, arithmetic and copies ran while one was open for 5% -> 5% of each run, Pallas kernels for 21% -> 15%
where the time goes in v2:
time: 88.8 us; the launch traced here: 88.1 us
  starting transfers between devices  37 us (42%)
  waiting for transfers between devices  24.1 us (27%)
  Pallas kernels  16.8 us (19%)
  other arithmetic  4.93 us (6%)
  local copies, waits for them, and re-layouts  3.49 us (4%)
  between operations  1.74 us (2%)
    ppermute x4, starting transfers between devices, up(): lax.ppermute(value, 'ctx', [(at, at + steps) for at in range(devices - st...  17.3 us
    pallas_call x4, Pallas kernels, call(): pl.pallas_call(kernel, grid=(steps,), in_specs=in_specs, out_specs=out_sp...  16.8 us
    ppermute x4, waiting for transfers between devices, down(): lax.ppermute(value, 'ctx', [(at + steps, at) for at in range(devices - st...  16.1 us
    ppermute x8, starting transfers between devices, back_round(): lax.ppermute(value, 'ctx', [((at + steps) % devices, at) for at in range(...  9.76 us
    ppermute x6, waiting for transfers between devices, swap(): return lax.ppermute(value, 'ctx', [(at, at ^ bit) for at in range(devices)])  6.18 us
    ppermute x4, starting transfers between devices, down(): lax.ppermute(value, 'ctx', [(at + steps, at) for at in range(devices - st...  5.13 us
    ppermute x6, starting transfers between devices, swap(): return lax.ppermute(value, 'ctx', [(at, at ^ bit) for at in range(devices)])  4.82 us
    select_n x2, other arithmetic, local(): jnp.where(core == 0, key_pack, keys_by[2])  3.39 us
  transfers between devices with their start and end apart: 22, of which 9 were waited for; matrix products, arithmetic and copies ran while one was open for 5% of the time, Pallas kernels for 15%

profile of v2, /device:TPU:0, one launch (start us, length us, event | category | flops | bytes accessed | tf_op | source)
XLA Modules:
  0.0 88.1 jit_solution(12586298456733509395)
XLA Ops:
  0.7 1.4 %fusion.2 = (bf16[256,512]{1,0:T(8,128)(2,1)S(1)}, bf16[256,512]{1,0:T(8,128)(2,1)S(1)}, bf16[256,512]{1,0:T(8,128)(2,1)S(1)}, bf16[256,512]{1,0:T(8,128)(2,1)S(1)}) fusion(bf16[256,1024]{1,0:T(8,128)(2,1)} %q_ref.7, bf16[256,1024]{1,0:T(8,128)(2,1)} %g_ref.7), kind=kLoop, calls=%fused_computation.21 | loop fusion | bytes 2097152 | tf_op jit(solution)/shard_map/slice | solution.py:301
  3.4 3.0 %collective-permute-start.9 = (bf16[512,512]{1,0:T(8,128)(2,1)S(1)}, bf16[512,512]{1,0:T(8,128)(2,1)S(1)}, u32[]{:S(2)}, u32[]{:S(2)}) collective-permute-start(bf16[512,512]{1,0:T(8,128)(2,1)S(1)} %get-tuple-element.60), channel_id=1, source_target_pairs={{0,2},{1,3},{2,0},{3,1},{4,6},{5,7},{6,4},{7,5},{8,10},{9,11},{10,... | collective-permute-start | bytes 1572872 | tf_op jit(solution)/shard_map/ppermute | solution.py:288
  6.4 3.5 %collective-permute-start.7 = (bf16[512,512]{1,0:T(8,128)(2,1)S(1)}, bf16[512,512]{1,0:T(8,128)(2,1)S(1)}, u32[]{:S(2)}, u32[]{:S(2)}) collective-permute-start(bf16[512,512]{1,0:T(8,128)(2,1)S(1)} %get-tuple-element.61), channel_id=1, source_target_pairs={{0,4},{1,5},{2,6},{3,7},{4,8},{5,9},{6,10},{7,11},{8,12},{9,13},{1... | collective-permute-start | bytes 1572872 | tf_op jit(solution)/shard_map/ppermute | solution.py:282
  9.9 1.3 %collective-permute-start.8 = (bf16[512,512]{1,0:T(8,128)(2,1)S(1)}, bf16[512,512]{1,0:T(8,128)(2,1)S(1)}, u32[]{:S(2)}, u32[]{:S(2)}) collective-permute-start(bf16[512,512]{1,0:T(8,128)(2,1)S(1)} %get-tuple-element.62), channel_id=1, source_target_pairs={{4,0},{5,1},{6,2},{7,3},{8,4},{9,5},{10,6},{11,7},{12,8},{13,9},{1... | collective-permute-start | bytes 1572872 | tf_op jit(solution)/shard_map/ppermute | solution.py:285
  12.1 4.6 %collective-permute-start = (bf16[512,512]{1,0:T(8,128)(2,1)S(1)}, bf16[512,512]{1,0:T(8,128)(2,1)S(1)}, u32[]{:S(2)}, u32[]{:S(2)}) collective-permute-start(bf16[512,512]{1,0:T(8,128)(2,1)S(1)} %get-tuple-element.72), channel_id=1, source_target_pairs={{0,4},{1,5},{2,6},{3,7},{4,8},{5,9},{6,10},{7,11},{8,12},{9,13},{1... | collective-permute-start | bytes 1572872 | tf_op jit(solution)/shard_map/ppermute | solution.py:282
  16.6 2.5 %collective-permute-done.9 = bf16[512,512]{1,0:T(8,128)(2,1)S(1)} collective-permute-done((bf16[512,512]{1,0:T(8,128)(2,1)S(1)}, bf16[512,512]{1,0:T(8,128)(2,1)S(1)}, u32[]{:S(2)}, u32[]{:S(2)}) %collective-permute-start.9) | collective-permute-done | bytes 524320 | tf_op jit(solution)/shard_map/ppermute | solution.py:288
  19.2 1.3 %collective-permute-start.1 = (bf16[512,512]{1,0:T(8,128)(2,1)S(1)}, bf16[512,512]{1,0:T(8,128)(2,1)S(1)}, u32[]{:S(2)}, u32[]{:S(2)}) collective-permute-start(bf16[512,512]{1,0:T(8,128)(2,1)S(1)} %get-tuple-element.73), channel_id=1, source_target_pairs={{4,0},{5,1},{6,2},{7,3},{8,4},{9,5},{10,6},{11,7},{12,8},{13,9},{1... | collective-permute-start | bytes 1572872 | tf_op jit(solution)/shard_map/ppermute | solution.py:285
  20.5 1.8 %collective-permute-done.7.refs_2_ = bf16[512,512]{1,0:T(8,128)(2,1)S(1)} collective-permute-done((bf16[512,512]{1,0:T(8,128)(2,1)S(1)}, bf16[512,512]{1,0:T(8,128)(2,1)S(1)}, u32[]{:S(2)}, u32[]{:S(2)}) %collective-permute-start.7) | collective-permute-done | bytes 524320 | tf_op jit(solution)/shard_map/ppermute | solution.py:282
  22.3 4.4 %collective-permute-done.8.refs_2_ = bf16[512,512]{1,0:T(8,128)(2,1)S(1)} collective-permute-done((bf16[512,512]{1,0:T(8,128)(2,1)S(1)}, bf16[512,512]{1,0:T(8,128)(2,1)S(1)}, u32[]{:S(2)}, u32[]{:S(2)}) %collective-permute-start.8) | collective-permute-done | bytes 524320 | tf_op jit(solution)/shard_map/ppermute | solution.py:285
  27.3 1.3 %collective-permute-start.12 = (bf16[512,512]{1,0:T(8,128)(2,1)S(1)}, bf16[512,512]{1,0:T(8,128)(2,1)}, u32[]{:S(2)}, u32[]{:S(2)}) collective-permute-start(bf16[512,512]{1,0:T(8,128)(2,1)S(1)} %collective-permute-done.8.refs_2_), channel_id=1, source_target_pairs={{4,0},{5,1},{6,2},{7,3},{8,4},{9,5},{10,6},{11,7},{12,8},{13,9},{1... | collective-permute-start | bytes 1572872 | tf_op jit(solution)/shard_map/ppermute | solution.py:285
  28.6 1.8 %collective-permute-done.2 = bf16[512,512]{1,0:T(8,128)(2,1)S(1)} collective-permute-done((bf16[512,512]{1,0:T(8,128)(2,1)S(1)}, bf16[512,512]{1,0:T(8,128)(2,1)S(1)}, u32[]{:S(2)}, u32[]{:S(2)}) %collective-permute-start.2) | collective-permute-done | bytes 524320 | tf_op jit(solution)/shard_map/ppermute | solution.py:288
  30.4 4.8 %collective-permute-start.11 = (bf16[512,512]{1,0:T(8,128)(2,1)S(1)}, bf16[512,512]{1,0:T(8,128)(2,1)}, u32[]{:S(2)}, u32[]{:S(2)}) collective-permute-start(bf16[512,512]{1,0:T(8,128)(2,1)S(1)} %collective-permute-done.7.refs_2_), channel_id=1, source_target_pairs={{0,4},{1,5},{2,6},{3,7},{4,8},{5,9},{6,10},{7,11},{8,12},{9,13},{1... | collective-permute-start | bytes 1572872 | tf_op jit(solution)/shard_map/ppermute | solution.py:282
  35.3 2.7 %collective-permute-done.1.refs_2_ = bf16[512,512]{1,0:T(8,128)(2,1)S(1)} collective-permute-done((bf16[512,512]{1,0:T(8,128)(2,1)S(1)}, bf16[512,512]{1,0:T(8,128)(2,1)S(1)}, u32[]{:S(2)}, u32[]{:S(2)}) %collective-permute-start.1) | collective-permute-done | bytes 524320 | tf_op jit(solution)/shard_map/ppermute | solution.py:285
  37.9 1.3 %collective-permute-start.5 = (bf16[512,512]{1,0:T(8,128)(2,1)S(1)}, bf16[512,512]{1,0:T(8,128)(2,1)}, u32[]{:S(2)}, u32[]{:S(2)}) collective-permute-start(bf16[512,512]{1,0:T(8,128)(2,1)S(1)} %collective-permute-done.1.refs_2_), channel_id=1, source_target_pairs={{4,0},{5,1},{6,2},{7,3},{8,4},{9,5},{10,6},{11,7},{12,8},{13,9},{1... | collective-permute-start | bytes 1572872 | tf_op jit(solution)/shard_map/ppermute | solution.py:285
  39.2 0.9 broadcast_select_fusion.6
  40.6 1.1 %collective-permute-done.10 = bf16[512,512]{1,0:T(8,128)(2,1)S(1)} collective-permute-done((bf16[512,512]{1,0:T(8,128)(2,1)S(1)}, bf16[512,512]{1,0:T(8,128)(2,1)S(1)}, u32[]{:S(2)}, u32[]{:S(2)}) %collective-permute-start.10) | collective-permute-done | bytes 524320 | tf_op jit(solution)/shard_map/ppermute | solution.py:288
  41.7 0.8 copy-done.18
  42.5 4.4 %collective-permute-start.4 = (bf16[512,512]{1,0:T(8,128)(2,1)S(1)}, bf16[512,512]{1,0:T(8,128)(2,1)}, u32[]{:S(2)}, u32[]{:S(2)}) collective-permute-start(bf16[512,512]{1,0:T(8,128)(2,1)S(1)} %collective-permute-done.refs_2_), channel_id=1, source_target_pairs={{0,4},{1,5},{2,6},{3,7},{4,8},{5,9},{6,10},{7,11},{8,12},{9,13},{1... | collective-permute-start | bytes 1572872 | tf_op jit(solution)/shard_map/ppermute | solution.py:282
  46.8 2.4 %collective-permute-done.12.refs_3_ = bf16[512,512]{1,0:T(8,128)(2,1)} collective-permute-done((bf16[512,512]{1,0:T(8,128)(2,1)S(1)}, bf16[512,512]{1,0:T(8,128)(2,1)}, u32[]{:S(2)}, u32[]{:S(2)}) %collective-permute-start.12) | collective-permute-done | bytes 524320 | tf_op jit(solution)/shard_map/ppermute | solution.py:285
  49.3 1.9 %broadcast_select_fusion.9 = (bf16[512,512]{1,0:T(8,128)(2,1)S(1)}, bf16[512,512]{1,0:T(8,128)(2,1)S(1)}, bf16[512,512]{1,0:T(8,128)(2,1)S(1)}, bf16[512,512]{1,0:T(8,128)(2,1)S(1)}) fusion(pred[]{:T(512)S(6)} %eq.7, bf16[256,512]{1,0:T(8,128)(2,1)} %copy-done.14, bf16[256,512]{1,0:T(8,128)(2,1)} %copy-done.13, bf16[512,512]{1,0:T(8,128)(2,1)} %copy-done.18, ...), kind=kLoop, calls=%fused_computation.15 | loop fusion | flops 3145728 | bytes 4194306 | tf_op jit(solution)/shard_map/jit(_where)/select_n | solution.py:340
  51.4 0.8 collective-permute-done.3
  52.2 6.6 %collective-permute-done.5.refs_3_ = bf16[512,512]{1,0:T(8,128)(2,1)} collective-permute-done((bf16[512,512]{1,0:T(8,128)(2,1)S(1)}, bf16[512,512]{1,0:T(8,128)(2,1)}, u32[]{:S(2)}, u32[]{:S(2)}) %collective-permute-start.5) | collective-permute-done | bytes 524320 | tf_op jit(solution)/shard_map/ppermute | solution.py:285
  58.8 1.5 %broadcast_select_fusion.11 = (bf16[512,512]{1,0:T(8,128)(2,1)S(1)}, bf16[512,512]{1,0:T(8,128)(2,1)S(1)}, bf16[512,512]{1,0:T(8,128)(2,1)S(1)}, bf16[512,512]{1,0:T(8,128)(2,1)S(1)}) fusion(pred[]{:T(512)S(6)} %eq.7, bf16[256,512]{1,0:T(8,128)(2,1)S(1)} %copy-done.10, bf16[256,512]{1,0:T(8,128)(2,1)S(1)} %copy-done.8, ...), kind=kLoop, calls=%fused_computation.17 | loop fusion | flops 3145728 | bytes 4194306 | tf_op jit(solution)/shard_map/jit(_where)/select_n | solution.py:340
  61.5 4.5 %shard_map.93 = (bf16[256,1024]{1,0:T(8,128)(2,1)}, bf16[256,1024]{1,0:T(8,128)(2,1)}, f32[5,8,256]{2,1,0:T(8,128)S(1)}) custom-call(s32[3]{0:T(128)S(1)} %pad_add_fusion.info, s32[2,8]{1,0:T(2,128)S(1)} %copy-done.4, bf16[256,1024]{1,0:T(8,128)(2,1)S(1)} %copy-done, bf16[256,1024]{1,0:T(8,128)(2,1)S(1)} %copy-done.1, bf16[256,1024]{1,0:T(8,128)(2,1)S(1)} %copy-done.2, ...), custom_call_target="tpu_custom_call" | custom-call | flops 805306368 | bytes 6291456 | tf_op jit(solution)/shard_map/pallas_call | solution.py:257
  66.0 2.6 %collective-permute-start.21 = (f32[5,8,256]{2,1,0:T(8,128)S(1)}, f32[5,8,256]{2,1,0:T(8,128)S(1)}, u32[]{:S(2)}, u32[]{:S(2)}) collective-permute-start(f32[5,8,256]{2,1,0:T(8,128)S(1)} %get-tuple-element.43.refs_4_), channel_id=1, source_target_pairs={{8,0},{9,1},{10,2},{11,3},{12,4},{13,5},{14,6},{15,7},{0,8},{1,9},... | collective-permute-start | bytes 122888 | tf_op jit(solution)/shard_map/ppermute | solution.py:291
  68.6 1.3 %collective-permute-start.20 = (f32[5,8,256]{2,1,0:T(8,128)S(1)}, f32[5,8,256]{2,1,0:T(8,128)S(1)}, u32[]{:S(2)}, u32[]{:S(2)}) collective-permute-start(f32[5,8,256]{2,1,0:T(8,128)S(1)} %get-tuple-element.43.refs_4_), channel_id=1, source_target_pairs={{4,0},{5,1},{6,2},{7,3},{8,4},{9,5},{10,6},{11,7},{12,8},{13,9},{1... | collective-permute-start | bytes 122888 | tf_op jit(solution)/shard_map/ppermute | solution.py:291
  70.9 4.5 %shard_map.94 = (bf16[256,1024]{1,0:T(8,128)(2,1)}, bf16[256,1024]{1,0:T(8,128)(2,1)}, f32[5,8,256]{2,1,0:T(8,128)S(1)}) custom-call(s32[3]{0:T(128)S(1)} %pad_add_fusion.info, s32[2,8]{1,0:T(2,128)S(1)} %copy-done.4, bf16[256,1024]{1,0:T(8,128)(2,1)S(1)} %copy-done, ...), custom_call_target="tpu_custom_call", output_to_operand_aliasing={{0}: (10, {}), {1}: (11, {})} | custom-call | flops 805306368 | bytes 6291456 | tf_op jit(solution)/shard_map/pallas_call | solution.py:257
  75.4 1.7 %collective-permute-start.17 = (f32[5,8,256]{2,1,0:T(8,128)S(1)}, f32[5,8,256]{2,1,0:T(8,128)S(1)}, u32[]{:S(2)}, u32[]{:S(2)}) collective-permute-start(f32[5,8,256]{2,1,0:T(8,128)S(1)} %get-tuple-element.41.refs_4_), channel_id=1, source_target_pairs={{8,0},{9,1},{10,2},{11,3},{12,4},{13,5},{14,6},{15,7},{0,8},{1,9},... | collective-permute-start | bytes 122888 | tf_op jit(solution)/shard_map/ppermute | solution.py:291
  77.1 2.3 %collective-permute-start.16 = (f32[5,8,256]{2,1,0:T(8,128)S(1)}, f32[5,8,256]{2,1,0:T(8,128)S(1)}, u32[]{:S(2)}, u32[]{:S(2)}) collective-permute-start(f32[5,8,256]{2,1,0:T(8,128)S(1)} %get-tuple-element.41.refs_4_), channel_id=1, source_target_pairs={{4,0},{5,1},{6,2},{7,3},{8,4},{9,5},{10,6},{11,7},{12,8},{13,9},{1... | collective-permute-start | bytes 122888 | tf_op jit(solution)/shard_map/ppermute | solution.py:291
  79.3 1.0 %collective-permute-start.15 = (f32[5,8,256]{2,1,0:T(8,128)S(1)}, f32[5,8,256]{2,1,0:T(8,128)S(1)}, u32[]{:S(2)}, u32[]{:S(2)}) collective-permute-start(f32[5,8,256]{2,1,0:T(8,128)S(1)} %get-tuple-element.41.refs_4_), channel_id=1, source_target_pairs={{2,0},{3,1},{4,2},{5,3},{6,4},{7,5},{8,6},{9,7},{10,8},{11,9},{12,... | collective-permute-start | bytes 122888 | tf_op jit(solution)/shard_map/ppermute | solution.py:291
  80.4 3.9 %shard_map.95 = (bf16[256,1024]{1,0:T(8,128)(2,1)}, bf16[256,1024]{1,0:T(8,128)(2,1)}) custom-call(s32[3]{0:T(128)S(1)} %pad_add_fusion.info, bf16[256,1024]{1,0:T(8,128)(2,1)S(1)} %copy-done, bf16[256,1024]{1,0:T(8,128)(2,1)S(1)} %copy-done.1, bf16[256,1024]{1,0:T(8,128)(2,1)S(1)} %copy-done.2, bf16[256,1024]{1,0:T(8,128)(2,1)S(1)} %copy-done.3, ...), custom_call_target="tpu_custom_call" | custom-call | flops 805306368 | bytes 6291456 | tf_op jit(solution)/shard_map/pallas_call | solution.py:257
  84.2 3.8 %shard_map.96 = (bf16[256,1024]{1,0:T(8,128)(2,1)}, bf16[256,1024]{1,0:T(8,128)(2,1)}) custom-call(s32[3]{0:T(128)S(1)} %pad_add_fusion.info, bf16[256,1024]{1,0:T(8,128)(2,1)S(1)} %copy-done, bf16[256,1024]{1,0:T(8,128)(2,1)S(1)} %copy-done.1, bf16[256,1024]{1,0:T(8,128)(2,1)S(1)} %copy-done.2, ...), custom_call_target="tpu_custom_call", output_to_operand_aliasing={{0}: (14, {}), {1}: (15, {})} | custom-call | flops 805306368 | bytes 6291456 | tf_op jit(solution)/shard_map/pallas_call | solution.py:257
  (65 shorter events, 4.8 us)
Async XLA Ops:
  0.7 1.5 %copy-start.2 = (bf16[256,1024]{1,0:T(8,128)(2,1)S(1)}, bf16[256,1024]{1,0:T(8,128)(2,1)}, u32[]{:S(2)}) copy-start(bf16[256,1024]{1,0:T(8,128)(2,1)} %v_ref.7) | copy-start | bytes 1572868
  2.2 9.1 %copy-start.5 = (bf16[256,512]{1,0:T(8,128)(2,1)}, bf16[256,512]{1,0:T(8,128)(2,1)S(1)}, u32[]{:S(2)}) copy-start(bf16[256,512]{1,0:T(8,128)(2,1)S(1)} %get-tuple-element.76) | copy-start | bytes 786436
  2.3 9.0 %copy-start.7 = (bf16[256,512]{1,0:T(8,128)(2,1)}, bf16[256,512]{1,0:T(8,128)(2,1)S(1)}, u32[]{:S(2)}) copy-start(bf16[256,512]{1,0:T(8,128)(2,1)S(1)} %get-tuple-element.64) | copy-start | bytes 786436
  2.3 9.0 %copy-start.9 = (bf16[256,512]{1,0:T(8,128)(2,1)}, bf16[256,512]{1,0:T(8,128)(2,1)S(1)}, u32[]{:S(2)}) copy-start(bf16[256,512]{1,0:T(8,128)(2,1)S(1)} %get-tuple-element.74) | copy-start | bytes 786436
  3.4 15.8 %collective-permute-start.9 = (bf16[512,512]{1,0:T(8,128)(2,1)S(1)}, bf16[512,512]{1,0:T(8,128)(2,1)S(1)}, u32[]{:S(2)}, u32[]{:S(2)}) collective-permute-start(bf16[512,512]{1,0:T(8,128)(2,1)S(1)} %get-tuple-element.60), channel_id=1, source_target_pairs={{0,2},{1,3},{2,0},{3,1},{4,6},{5,7},{6,4},{7,5},{8,10},{9,11},{10,... | collective-permute-start | bytes 1572872 | tf_op jit(solution)/shard_map/ppermute | solution.py:288
  6.4 15.8 %collective-permute-start.7 = (bf16[512,512]{1,0:T(8,128)(2,1)S(1)}, bf16[512,512]{1,0:T(8,128)(2,1)S(1)}, u32[]{:S(2)}, u32[]{:S(2)}) collective-permute-start(bf16[512,512]{1,0:T(8,128)(2,1)S(1)} %get-tuple-element.61), channel_id=1, source_target_pairs={{0,4},{1,5},{2,6},{3,7},{4,8},{5,9},{6,10},{7,11},{8,12},{9,13},{1... | collective-permute-start | bytes 1572872 | tf_op jit(solution)/shard_map/ppermute | solution.py:282
  9.9 16.8 %collective-permute-start.8 = (bf16[512,512]{1,0:T(8,128)(2,1)S(1)}, bf16[512,512]{1,0:T(8,128)(2,1)S(1)}, u32[]{:S(2)}, u32[]{:S(2)}) collective-permute-start(bf16[512,512]{1,0:T(8,128)(2,1)S(1)} %get-tuple-element.62), channel_id=1, source_target_pairs={{4,0},{5,1},{6,2},{7,3},{8,4},{9,5},{10,6},{11,7},{12,8},{13,9},{1... | collective-permute-start | bytes 1572872 | tf_op jit(solution)/shard_map/ppermute | solution.py:285
  11.5 18.9 %collective-permute-start.2 = (bf16[512,512]{1,0:T(8,128)(2,1)S(1)}, bf16[512,512]{1,0:T(8,128)(2,1)S(1)}, u32[]{:S(2)}, u32[]{:S(2)}) collective-permute-start(bf16[512,512]{1,0:T(8,128)(2,1)S(1)} %get-tuple-element.71), channel_id=1, source_target_pairs={{0,2},{1,3},{2,0},{3,1},{4,6},{5,7},{6,4},{7,5},{8,10},{9,11},{10,... | collective-permute-start | bytes 1572872 | tf_op jit(solution)/shard_map/ppermute | solution.py:288
  12.1 23.2 %collective-permute-start = (bf16[512,512]{1,0:T(8,128)(2,1)S(1)}, bf16[512,512]{1,0:T(8,128)(2,1)S(1)}, u32[]{:S(2)}, u32[]{:S(2)}) collective-permute-start(bf16[512,512]{1,0:T(8,128)(2,1)S(1)} %get-tuple-element.72), channel_id=1, source_target_pairs={{0,4},{1,5},{2,6},{3,7},{4,8},{5,9},{6,10},{7,11},{8,12},{9,13},{1... | collective-permute-start | bytes 1572872 | tf_op jit(solution)/shard_map/ppermute | solution.py:282
  19.2 20.9 %copy-start.17 = (bf16[512,512]{1,0:T(8,128)(2,1)}, bf16[512,512]{1,0:T(8,128)(2,1)S(1)}, u32[]{:S(2)}) copy-start(bf16[512,512]{1,0:T(8,128)(2,1)S(1)} %collective-permute-done.9) | copy-start | bytes 1572868
  19.2 18.7 %collective-permute-start.1 = (bf16[512,512]{1,0:T(8,128)(2,1)S(1)}, bf16[512,512]{1,0:T(8,128)(2,1)S(1)}, u32[]{:S(2)}, u32[]{:S(2)}) collective-permute-start(bf16[512,512]{1,0:T(8,128)(2,1)S(1)} %get-tuple-element.73), channel_id=1, source_target_pairs={{4,0},{5,1},{6,2},{7,3},{8,4},{9,5},{10,6},{11,7},{12,8},{13,9},{1... | collective-permute-start | bytes 1572872 | tf_op jit(solution)/shard_map/ppermute | solution.py:285
  26.8 14.9 %collective-permute-start.10 = (bf16[512,512]{1,0:T(8,128)(2,1)S(1)}, bf16[512,512]{1,0:T(8,128)(2,1)S(1)}, u32[]{:S(2)}, u32[]{:S(2)}) collective-permute-start(bf16[512,512]{1,0:T(8,128)(2,1)S(1)} %broadcast_select_fusion.2), channel_id=1, source_target_pairs={{0,2},{1,3},{2,0},{3,1},{4,6},{5,7},{6,4},{7,5},{8,10},{9,11},{10,... | collective-permute-start | bytes 1572872 | tf_op jit(solution)/shard_map/ppermute | solution.py:288
  27.3 21.9 %collective-permute-start.12 = (bf16[512,512]{1,0:T(8,128)(2,1)S(1)}, bf16[512,512]{1,0:T(8,128)(2,1)}, u32[]{:S(2)}, u32[]{:S(2)}) collective-permute-start(bf16[512,512]{1,0:T(8,128)(2,1)S(1)} %collective-permute-done.8.refs_2_), channel_id=1, source_target_pairs={{4,0},{5,1},{6,2},{7,3},{8,4},{9,5},{10,6},{11,7},{12,8},{13,9},{1... | collective-permute-start | bytes 1572872 | tf_op jit(solution)/shard_map/ppermute | solution.py:285
  30.4 10.2 %copy-start.15 = (bf16[512,512]{1,0:T(8,128)(2,1)}, bf16[512,512]{1,0:T(8,128)(2,1)S(1)}, u32[]{:S(2)}) copy-start(bf16[512,512]{1,0:T(8,128)(2,1)S(1)} %collective-permute-done.2) | copy-start | bytes 1572868
  30.4 18.9 %collective-permute-start.11 = (bf16[512,512]{1,0:T(8,128)(2,1)S(1)}, bf16[512,512]{1,0:T(8,128)(2,1)}, u32[]{:S(2)}, u32[]{:S(2)}) collective-permute-start(bf16[512,512]{1,0:T(8,128)(2,1)S(1)} %collective-permute-done.7.refs_2_), channel_id=1, source_target_pairs={{0,4},{1,5},{2,6},{3,7},{4,8},{5,9},{6,10},{7,11},{8,12},{9,13},{1... | collective-permute-start | bytes 1572872 | tf_op jit(solution)/shard_map/ppermute | solution.py:282
  37.9 20.8 %collective-permute-start.5 = (bf16[512,512]{1,0:T(8,128)(2,1)S(1)}, bf16[512,512]{1,0:T(8,128)(2,1)}, u32[]{:S(2)}, u32[]{:S(2)}) collective-permute-start(bf16[512,512]{1,0:T(8,128)(2,1)S(1)} %collective-permute-done.1.refs_2_), channel_id=1, source_target_pairs={{4,0},{5,1},{6,2},{7,3},{8,4},{9,5},{10,6},{11,7},{12,8},{13,9},{1... | collective-permute-start | bytes 1572872 | tf_op jit(solution)/shard_map/ppermute | solution.py:285
  40.1 12.1 %collective-permute-start.3 = (bf16[512,512]{1,0:T(8,128)(2,1)}, bf16[512,512]{1,0:T(8,128)(2,1)}, u32[]{:S(2)}, u32[]{:S(2)}) collective-permute-start(bf16[512,512]{1,0:T(8,128)(2,1)} %broadcast_select_fusion.6), channel_id=1, source_target_pairs={{0,2},{1,3},{2,0},{3,1},{4,6},{5,7},{6,4},{7,5},{8,10},{9,11},{10,... | collective-permute-start | bytes 1572872 | tf_op jit(solution)/shard_map/ppermute | solution.py:288
  42.5 16.3 %collective-permute-start.4 = (bf16[512,512]{1,0:T(8,128)(2,1)S(1)}, bf16[512,512]{1,0:T(8,128)(2,1)}, u32[]{:S(2)}, u32[]{:S(2)}) collective-permute-start(bf16[512,512]{1,0:T(8,128)(2,1)S(1)} %collective-permute-done.refs_2_), channel_id=1, source_target_pairs={{0,4},{1,5},{2,6},{3,7},{4,8},{5,9},{6,10},{7,11},{8,12},{9,13},{1... | collective-permute-start | bytes 1572872 | tf_op jit(solution)/shard_map/ppermute | solution.py:282
  51.2 7.5 %copy-start.6 = (bf16[256,512]{1,0:T(8,128)(2,1)S(1)}, bf16[256,512]{1,0:T(8,128)(2,1)}, u32[]{:S(2)}) copy-start(bf16[256,512]{1,0:T(8,128)(2,1)} %copy-done.5) | copy-start | bytes 786436
  51.2 7.5 %copy-start.8 = (bf16[256,512]{1,0:T(8,128)(2,1)S(1)}, bf16[256,512]{1,0:T(8,128)(2,1)}, u32[]{:S(2)}) copy-start(bf16[256,512]{1,0:T(8,128)(2,1)} %copy-done.7) | copy-start | bytes 786436
  51.2 7.5 %copy-start.10 = (bf16[256,512]{1,0:T(8,128)(2,1)S(1)}, bf16[256,512]{1,0:T(8,128)(2,1)}, u32[]{:S(2)}) copy-start(bf16[256,512]{1,0:T(8,128)(2,1)} %copy-done.9) | copy-start | bytes 786436
  51.2 7.5 %copy-start.16 = (bf16[512,512]{1,0:T(8,128)(2,1)S(1)}, bf16[512,512]{1,0:T(8,128)(2,1)}, u32[]{:S(2)}) copy-start(bf16[512,512]{1,0:T(8,128)(2,1)} %copy-done.15) | copy-start | bytes 1572868
  51.3 9.9 %collective-permute-start.13 = (bf16[1024,512]{1,0:T(8,128)(2,1)S(1)}, bf16[1024,512]{1,0:T(8,128)(2,1)S(1)}, u32[]{:S(2)}, u32[]{:S(2)}) collective-permute-start(bf16[1024,512]{1,0:T(8,128)(2,1)S(1)} %pad_maximum_fusion.1), channel_id=1, source_target_pairs={{0,1},{1,0},{2,3},{3,2},{4,5},{5,4},{6,7},{7,6},{8,9},{9,8},{10,11... | collective-permute-start | bytes 3145736 | tf_op jit(solution)/shard_map/ppermute | solution.py:288
  60.4 10.5 %collective-permute-start.6 = (bf16[1024,512]{1,0:T(8,128)(2,1)S(1)}, bf16[1024,512]{1,0:T(8,128)(2,1)S(1)}, u32[]{:S(2)}, u32[]{:S(2)}) collective-permute-start(bf16[1024,512]{1,0:T(8,128)(2,1)S(1)} %pad_maximum_fusion), channel_id=1, source_target_pairs={{0,1},{1,0},{2,3},{3,2},{4,5},{5,4},{6,7},{7,6},{8,9},{9,8},{10,11... | collective-permute-start | bytes 3145736 | tf_op jit(solution)/shard_map/ppermute | solution.py:288
  66.0 11.0 %collective-permute-start.21 = (f32[5,8,256]{2,1,0:T(8,128)S(1)}, f32[5,8,256]{2,1,0:T(8,128)S(1)}, u32[]{:S(2)}, u32[]{:S(2)}) collective-permute-start(f32[5,8,256]{2,1,0:T(8,128)S(1)} %get-tuple-element.43.refs_4_), channel_id=1, source_target_pairs={{8,0},{9,1},{10,2},{11,3},{12,4},{13,5},{14,6},{15,7},{0,8},{1,9},... | collective-permute-start | bytes 122888 | tf_op jit(solution)/shard_map/ppermute | solution.py:291
  68.6 10.7 %collective-permute-start.20 = (f32[5,8,256]{2,1,0:T(8,128)S(1)}, f32[5,8,256]{2,1,0:T(8,128)S(1)}, u32[]{:S(2)}, u32[]{:S(2)}) collective-permute-start(f32[5,8,256]{2,1,0:T(8,128)S(1)} %get-tuple-element.43.refs_4_), channel_id=1, source_target_pairs={{4,0},{5,1},{6,2},{7,3},{8,4},{9,5},{10,6},{11,7},{12,8},{13,9},{1... | collective-permute-start | bytes 122888 | tf_op jit(solution)/shard_map/ppermute | solution.py:291
  69.9 10.4 %collective-permute-start.19 = (f32[5,8,256]{2,1,0:T(8,128)S(1)}, f32[5,8,256]{2,1,0:T(8,128)S(1)}, u32[]{:S(2)}, u32[]{:S(2)}) collective-permute-start(f32[5,8,256]{2,1,0:T(8,128)S(1)} %get-tuple-element.43.refs_4_), channel_id=1, source_target_pairs={{2,0},{3,1},{4,2},{5,3},{6,4},{7,5},{8,6},{9,7},{10,8},{11,9},{12,... | collective-permute-start | bytes 122888 | tf_op jit(solution)/shard_map/ppermute | solution.py:291
  70.4 10.0 %collective-permute-start.18 = (f32[5,8,256]{2,1,0:T(8,128)S(1)}, f32[5,8,256]{2,1,0:T(8,128)S(1)}, u32[]{:S(2)}, u32[]{:S(2)}) collective-permute-start(f32[5,8,256]{2,1,0:T(8,128)S(1)} %get-tuple-element.43.refs_4_), channel_id=1, source_target_pairs={{1,0},{2,1},{3,2},{4,3},{5,4},{6,5},{7,6},{8,7},{9,8},{10,9},{11,1... | collective-permute-start | bytes 122888 | tf_op jit(solution)/shard_map/ppermute | solution.py:291
  75.4 8.8 %collective-permute-start.17 = (f32[5,8,256]{2,1,0:T(8,128)S(1)}, f32[5,8,256]{2,1,0:T(8,128)S(1)}, u32[]{:S(2)}, u32[]{:S(2)}) collective-permute-start(f32[5,8,256]{2,1,0:T(8,128)S(1)} %get-tuple-element.41.refs_4_), channel_id=1, source_target_pairs={{8,0},{9,1},{10,2},{11,3},{12,4},{13,5},{14,6},{15,7},{0,8},{1,9},... | collective-permute-start | bytes 122888 | tf_op jit(solution)/shard_map/ppermute | solution.py:291
  77.1 7.1 %collective-permute-start.16 = (f32[5,8,256]{2,1,0:T(8,128)S(1)}, f32[5,8,256]{2,1,0:T(8,128)S(1)}, u32[]{:S(2)}, u32[]{:S(2)}) collective-permute-start(f32[5,8,256]{2,1,0:T(8,128)S(1)} %get-tuple-element.41.refs_4_), channel_id=1, source_target_pairs={{4,0},{5,1},{6,2},{7,3},{8,4},{9,5},{10,6},{11,7},{12,8},{13,9},{1... | collective-permute-start | bytes 122888 | tf_op jit(solution)/shard_map/ppermute | solution.py:291
  79.3 4.9 %collective-permute-start.15 = (f32[5,8,256]{2,1,0:T(8,128)S(1)}, f32[5,8,256]{2,1,0:T(8,128)S(1)}, u32[]{:S(2)}, u32[]{:S(2)}) collective-permute-start(f32[5,8,256]{2,1,0:T(8,128)S(1)} %get-tuple-element.41.refs_4_), channel_id=1, source_target_pairs={{2,0},{3,1},{4,2},{5,3},{6,4},{7,5},{8,6},{9,7},{10,8},{11,9},{12,... | collective-permute-start | bytes 122888 | tf_op jit(solution)/shard_map/ppermute | solution.py:291
  80.3 3.9 %collective-permute-start.14 = (f32[5,8,256]{2,1,0:T(8,128)S(1)}, f32[5,8,256]{2,1,0:T(8,128)S(1)}, u32[]{:S(2)}, u32[]{:S(2)}) collective-permute-start(f32[5,8,256]{2,1,0:T(8,128)S(1)} %get-tuple-element.41.refs_4_), channel_id=1, source_target_pairs={{1,0},{2,1},{3,2},{4,3},{5,4},{6,5},{7,6},{8,7},{9,8},{10,9},{11,1... | collective-permute-start | bytes 122888 | tf_op jit(solution)/shard_map/ppermute | solution.py:291
  (9 other events, 9.6 us)

commit v3 on v2

v3 whole, which is shorter than its diff:
```python
import functools
import math

import jax
import jax.numpy as jnp
from jax import lax
from jax.experimental import pallas as pl
from jax.experimental.pallas import tpu as pltpu
from jax.sharding import PartitionSpec as P

HEAD_DIM = 128
BLOCK = 128
LEVELS = 8
CHUNKS = 2
QUERY_LAG = (0, 1, 2, 3)
KEY_LAG = (0, 1, 1)
FAR = 1e30
SCALE = HEAD_DIM ** (-0.5)
SCALE2 = SCALE * math.log2(math.e)


def product_rows(left, right):
    return lax.dot_general(
        left, right, (((1,), (1,)), ((), ())), preferred_element_type=jnp.float32
    )


def product(left, right):
    return jnp.dot(left, right, preferred_element_type=jnp.float32)


def two_heads(left):
    first, second = left[:, :HEAD_DIM], left[:, HEAD_DIM:]
    empty = jnp.zeros_like(first)
    return jnp.concatenate(
        [
            jnp.concatenate([first, empty], axis=1),
            jnp.concatenate([empty, second], axis=1),
        ],
        axis=0,
    )


def pair_rows(left, right):
    both = product_rows(two_heads(left), right)
    return [both[:BLOCK], both[BLOCK:]]


def pair_product(left, right):
    both = product(jnp.concatenate(left, axis=0), right)
    return [both[:BLOCK, :HEAD_DIM], both[BLOCK:, HEAD_DIM:]]


def staged(units, stages, lags):
    for turn in range(len(units) + max(lags)):
        for stage, lag in zip(stages, lags):
            if 0 <= turn - lag < len(units):
                stage(units[turn - lag])


def send_head(copies, head, first, pairs, sems):
    for index, (source, target) in enumerate(pairs):
        copy = pltpu.make_async_copy(
            source.at[:, pl.ds(head * HEAD_DIM, HEAD_DIM)],
            target.at[:, pl.ds((first + head) * HEAD_DIM, HEAD_DIM)],
            sems.at[index, head],
        )
        copy.start()
        copies.append(copy)


def query_kernel(hops, first, info, kb, q_ref, k_ref, v_ref, g_ref, *refs):
    behind = refs[: len(hops) + (first > 0)]
    att_out, dq_out, stat_ref, att_ref, dq_ref, sems, bias_ref = refs[-7:]
    heads = att_ref.shape[1] // HEAD_DIM
    base = first
    device, valid = info[0], info[1]
    pieces = 2 + len(hops)

    def rows_ok(block):
        at = (device * 2 + block) * BLOCK
        return at + lax.broadcasted_iota(jnp.int32, (BLOCK, 1), 0) < valid

    if True:
        for block in range(2):
            here = device * 2 + block
            query = lax.broadcasted_iota(jnp.int32, (BLOCK, BLOCK), 0)
            key = lax.broadcasted_iota(jnp.int32, (BLOCK, BLOCK), 1)
            row_ok = here * BLOCK + query < valid
            for piece in range(pieces):
                there = here if piece == 0 else here - 2 ** (piece - 1)
                allowed = row_ok & (there * BLOCK + key < valid)
                if piece == 0:
                    allowed = allowed & (key <= query)
                else:
                    entry = kb[block, piece - 1]
                    allowed = allowed & ((entry >= 0) & (entry == there))
                bias_ref[block, :, piece * BLOCK : (piece + 1) * BLOCK] = jnp.where(
                    allowed, 0.0, -FAR
                )
            level = lax.broadcasted_iota(jnp.int32, (LEVELS, BLOCK), 0)
            row = lax.broadcasted_iota(jnp.int32, (LEVELS, BLOCK), 1)
            flags = jnp.zeros((LEVELS, BLOCK), jnp.float32)
            for index in range(LEVELS):
                entry = kb[block, index]
                hit = ((entry >= 0) & (entry == here - 2**index)).astype(jnp.float32)
                flags = jnp.where(level == index, hit, flags)
            flags = jnp.where(here * BLOCK + row < valid, flags, 0.0)
            stat_ref[3, :, block * BLOCK : (block + 1) * BLOCK] = flags
        if first:
            stat_ref[:3] = behind[-1][:3]

    lane = lax.broadcasted_iota(jnp.int32, (BLOCK, BLOCK), 1)
    units = [(pair, block) for pair in range(heads // 2) for block in range(2)]
    held = {}

    def stack(unit, own_ref, which):
        pair, block = unit

        def part(ref, index):
            shift = first * HEAD_DIM if ref is own_ref else 0
            return ref[
                index * BLOCK : (index + 1) * BLOCK, pl.ds(shift + pair * 2 * HEAD_DIM, 2 * HEAD_DIM)
            ]

        parts = [part(own_ref, block)]
        parts.append(part(behind[0], which * 2 + 1) if block == 0 else part(own_ref, 0))
        parts += [part(ref, which * 2 + block) for ref in behind[: len(hops)]]
        return jnp.concatenate(parts, axis=0)

    def place(unit, shift=0):
        pair, block = unit
        return (
            slice(block * BLOCK, (block + 1) * BLOCK),
            slice((shift + 2 * pair) * HEAD_DIM, (shift + 2 * pair + 2) * HEAD_DIM),
        )

    def products(unit):
        rows, columns = place(unit, first)
        scores = pair_rows(q_ref[rows, columns], stack(unit, k_ref, 0))
        weight_grad = pair_rows(g_ref[rows, columns], stack(unit, v_ref, 1))
        held[unit] = (scores, weight_grad)

    def soften(unit):
        both, weight_grad = held[unit]
        weights, top, inverses = [], [], []
        for scores in both:
            scores = scores * SCALE2 + bias_ref[unit[1]]
            row_max = jnp.max(scores, axis=1, keepdims=True)
            raw = jnp.exp2(scores - row_max)
            total = jnp.sum(raw, axis=1, keepdims=True)
            inverse = jnp.where(rows_ok(unit[1]), 1.0 / total, 0.0)
            weights.append(raw * inverse)
            top.append(jnp.where(rows_ok(unit[1]), row_max, FAR))
            inverses.append(inverse)
        held[unit] = (weights, weight_grad, top, inverses)

    def attend(unit):
        weights, weight_grad, top, inverse = held[unit]
        rows, columns = place(unit)
        attended = pair_product([w.astype(jnp.bfloat16) for w in weights], stack(unit, v_ref, 1))
        attended = jnp.concatenate(attended, axis=1).astype(jnp.bfloat16)
        att_ref[rows, columns] = attended
        terms = g_ref[place(unit, first)].astype(jnp.float32) * attended.astype(jnp.float32)
        deltas = []
        for index in range(2):
            delta = jnp.sum(
                terms[:, index * HEAD_DIM : (index + 1) * HEAD_DIM], axis=1, keepdims=True
            )
            packed = jnp.where(lane == 0, top[index], jnp.where(lane == 1, inverse[index], delta))
            turned = packed.T
            for kind in range(3):
                at = base + 2 * unit[0] + index
                stat_ref[kind, at : at + 1, rows] = turned[kind : kind + 1]
            deltas.append(delta)
        held[unit] = (weights, weight_grad, deltas)

    def finish(unit):
        score_grad = [
            (w * (wg - d)).astype(jnp.bfloat16) for w, wg, d in zip(*held[unit])
        ]
        query_grad = pair_product(score_grad, stack(unit, k_ref, 0))
        dq_ref[place(unit)] = (jnp.concatenate(query_grad, axis=1) * SCALE).astype(jnp.bfloat16)
        if unit[1] == 1:
            for head in (2 * unit[0], 2 * unit[0] + 1):
                send_head(copies, head, first, ((att_ref, att_out), (dq_ref, dq_out)), sems)

    copies = []
    staged(units, (products, soften, attend, finish), QUERY_LAG)
    for copy in copies:
        copy.wait()


def key_kernel(hops, chunks, info, q_ref, k_ref, v_ref, g_ref, *refs):
    count = len(hops)
    ahead_all = [refs[chunk * count : (chunk + 1) * count] for chunk in range(chunks)]
    stats = refs[chunks * count : (chunks + 1) * count + 1]
    dk_out, dv_out, dk_ref, dv_ref, sems = refs[-5:]
    heads = dk_ref.shape[1] // HEAD_DIM
    device, valid, devices = info[0], info[1], info[2]
    flags = [ref[3] for ref in stats]
    units = [(pair, block) for pair in range(heads // 2) for block in range(2)]
    held = {}

    def stack(unit, own_ref, which):
        pair, block = unit
        chunk = pair * chunks * 2 // heads
        ahead = ahead_all[chunk]

        def part(ref, index):
            shift = 0 if ref is own_ref else -chunk * heads // chunks * HEAD_DIM
            return ref[
                index * BLOCK : (index + 1) * BLOCK, pl.ds(shift + pair * 2 * HEAD_DIM, 2 * HEAD_DIM)
            ]

        parts = [part(own_ref, block)]
        parts.append(part(own_ref, 1) if block == 0 else part(ahead[0], 4 + which * 2))
        parts += [
            part(ref, which * 2 + block + (4 if index == 0 else 0)) for index, ref in enumerate(ahead)
        ]
        return jnp.concatenate(parts, axis=0)

    def place(unit, shift=0):
        pair, block = unit
        return (
            slice(block * BLOCK, (block + 1) * BLOCK),
            slice((shift + 2 * pair) * HEAD_DIM, (shift + 2 * pair + 2) * HEAD_DIM),
        )

    def lanes(array, row, index):
        return array[row : row + 1, index * BLOCK : (index + 1) * BLOCK]

    def products(unit):
        rows, columns = place(unit)
        scores = pair_rows(k_ref[rows, columns], stack(unit, q_ref, 0))
        weight_grad = pair_rows(v_ref[rows, columns], stack(unit, g_ref, 1))
        held[unit] = (scores, weight_grad)

    def soften(unit):
        pair, block = unit
        held[unit] = [
            soften_head(2 * pair + index, block, held[unit][0][index], held[unit][1][index])
            for index in range(2)
        ]

    def soften_head(head, block, scores, weight_grad):
        stat = [
            [ref[kind, head : head + 1, :] for kind in range(3)] for ref in stats
        ]
        sources = [(0, block, None)]
        sources.append((0, 1, 0) if block == 0 else (1, 0, 0))
        sources += [(1 + index, block, index + 1) for index in range(count)]
        row_max, inverse, delta = [], [], []
        for source, at, level in sources:
            top = lanes(stat[source][0], 0, at)
            if level is not None:
                flag = lanes(flags[source], level, at)
                if source > 0:
                    flag = jnp.where(device + hops[source - 1] < devices, flag, 0.0)
                top = jnp.where(flag > 0.5, top, FAR)
            row_max.append(top)
            inverse.append(lanes(stat[source][1], 0, at))
            delta.append(lanes(stat[source][2], 0, at))
        row_max, inverse, delta = (
            jnp.concatenate(parts, axis=1) for parts in (row_max, inverse, delta)
        )
        scores = scores * SCALE2 - row_max
        key_index = lax.broadcasted_iota(jnp.int32, (BLOCK, BLOCK), 0)
        query_index = lax.broadcasted_iota(jnp.int32, (BLOCK, BLOCK), 1)
        causal = jnp.where(key_index <= query_index, scores[:, :BLOCK], -FAR)
        scores = jnp.concatenate([causal, scores[:, BLOCK:]], axis=1)
        weights = jnp.exp2(scores) * inverse
        score_grad = (weights * (weight_grad - delta)).astype(jnp.bfloat16)
        return (weights.astype(jnp.bfloat16), score_grad)

    def finish(unit):
        weights_low, score_grad = zip(*held[unit])
        rows, columns = place(unit)
        value_grad = jnp.concatenate(pair_product(weights_low, stack(unit, g_ref, 1)), axis=1)
        key_grad = jnp.concatenate(pair_product(score_grad, stack(unit, q_ref, 0)), axis=1) * SCALE
        at = (device * 2 + unit[1]) * BLOCK
        key_ok = at + lax.broadcasted_iota(jnp.int32, (BLOCK, 1), 0) < valid
        dk_ref[rows, columns] = jnp.where(key_ok, key_grad, 0.0).astype(jnp.bfloat16)
        dv_ref[rows, columns] = jnp.where(key_ok, value_grad, 0.0).astype(jnp.bfloat16)
        if unit[1] == 1:
            for head in (2 * unit[0], 2 * unit[0] + 1):
                send_head(copies, head, 0, ((dk_ref, dk_out), (dv_ref, dv_out)), sems)

    copies = []
    staged(units, (products, soften, finish), KEY_LAG)
    for copy in copies:
        copy.wait()


def call(kernel, heads, scalars, arrays, previous, out_shapes, scratch, flops):
    width = heads * HEAD_DIM
    in_specs = [pl.BlockSpec(memory_space=pltpu.SMEM) for _ in scalars]
    in_specs += [pl.BlockSpec(memory_space=pltpu.VMEM) for _ in arrays]
    in_specs += [pl.BlockSpec(memory_space=pl.ANY) for _ in previous]
    before = len(scalars) + len(arrays)
    out_specs = [pl.BlockSpec(memory_space=pl.ANY)] * 2
    out_specs += [pl.BlockSpec(memory_space=pltpu.VMEM)] * (len(out_shapes) - 2)
    rows = out_shapes[0].shape[0]
    return pl.pallas_call(
        kernel,
        in_specs=in_specs,
        out_specs=out_specs,
        out_shape=out_shapes,
        scratch_shapes=[
            pltpu.VMEM((rows, width), jnp.bfloat16),
            pltpu.VMEM((rows, width), jnp.bfloat16),
            pltpu.SemaphoreType.DMA((2, heads)),
        ]
        + scratch,
        input_output_aliases={before + index: index for index in range(len(previous))},
        cost_estimate=pl.CostEstimate(flops=flops, bytes_accessed=6 << 20, transcendentals=0),
        compiler_params=pltpu.CompilerParams(vmem_limit_bytes=24 << 20),
    )(*scalars, *arrays, *previous)


def local(queries, keys, values, out_grad, key_blocks, path_length):
    rows_dev, columns = queries.shape
    head_count = columns // HEAD_DIM
    devices = lax.axis_size("ctx")
    device = lax.axis_index("ctx")
    side, core = (device // 2) % 2, device % 2
    hops = [2**level for level in range(LEVELS - 1) if 2**level < devices]
    info = jnp.stack([device, path_length[0], jnp.int32(devices)]).astype(jnp.int32)

    def up(value, steps):
        return lax.ppermute(value, "ctx", [(at, at + steps) for at in range(devices - steps)])

    def down(value, steps):
        return lax.ppermute(value, "ctx", [(at + steps, at) for at in range(devices - steps)])

    def swap(value, bit):
        return lax.ppermute(value, "ctx", [(at, at ^ bit) for at in range(devices)])

    def back_round(value, steps):
        return lax.ppermute(value, "ctx", [((at + steps) % devices, at) for at in range(devices)])

    heads = head_count // CHUNKS
    width = heads * HEAD_DIM
    packs = []
    for chunk in range(CHUNKS):
        cut = slice(chunk * width, (chunk + 1) * width)
        packs.append(
            (
                jnp.concatenate([keys[:, cut], values[:, cut]], axis=0),
                jnp.concatenate([queries[:, cut], out_grad[:, cut]], axis=0),
            )
        )
    first = []
    for key_pack, query_pack in packs:
        first.append(
            (
                up(key_pack, 4),
                down(query_pack, 4),
                swap(jnp.where(side == 0, key_pack, query_pack), 2),
            )
        )
    own = (queries, keys, values, out_grad)
    full = jax.ShapeDtypeStruct((rows_dev, columns), jnp.bfloat16)
    stat_shape = jax.ShapeDtypeStruct((4, max(head_count, LEVELS), rows_dev), jnp.float32)
    pieces = 2 + len(hops)
    flops = heads * 2 * pieces * 4 * 2 * BLOCK**3

    middle = []
    for (key_pack, query_pack), stage in zip(packs, first):
        key_4, query_4, side_1 = lax.optimization_barrier(stage)
        side_2 = swap(jnp.where(side == 0, query_4, key_4), 2)
        keys_by, queries_by = {4: key_4}, {4: query_4}
        steps = 4
        while steps * 2 < devices:
            keys_by[steps * 2] = up(keys_by[steps], steps)
            queries_by[steps * 2] = down(queries_by[steps], steps)
            steps *= 2
        middle.append((side_1, side_2, keys_by, queries_by))

    front, stats, moved = (), [], []
    for chunk in range(CHUNKS):
        (key_pack, query_pack), (side_1, side_2, keys_by, queries_by) = packs[chunk], middle[chunk]
        side_2, keys_by[8], queries_by[8] = lax.optimization_barrier((side_2, keys_by[8], queries_by[8]))
        keys_by[2] = jnp.where(side == 0, side_2, side_1)
        queries_by[2] = jnp.where(side == 0, side_1, side_2)
        neighbour = swap(
            jnp.concatenate(
                [
                    jnp.where(core == 0, key_pack, keys_by[2]),
                    jnp.where(core == 0, queries_by[2], query_pack),
                ],
                axis=0,
            ),
            1,
        )
        moved.append(
            (
                [neighbour] + [keys_by[hop] for hop in hops[1:]],
                [neighbour] + [queries_by[hop] for hop in hops[1:]],
            )
        )
        att, dq, stat = call(
            functools.partial(query_kernel, hops, chunk * heads),
            heads,
            (info, key_blocks),
            own + tuple(moved[chunk][0]) + tuple(stats[-1:]),
            front,
            (full, full, stat_shape),
            [pltpu.VMEM((2, BLOCK, pieces * BLOCK), jnp.float32)],
            flops,
        )
        front = (att, dq)
        stats.append(stat)
    stats = [stat] + [back_round(stat, hop) for hop in hops]
    back = call(
        functools.partial(key_kernel, hops, CHUNKS),
        head_count,
        (info,),
        own + sum((tuple(pair[1]) for pair in moved), ()) + tuple(stats),
        (),
        (full, full),
        [],
        2 * flops,
    )
    return (front[0], front[1], back[0], back[1])


def solution(mesh):
    placed = (P(("grp", "ctx"), None),) * 5 + (P("grp"),)
    return jax.shard_map(
        local,
        mesh=mesh,
        in_specs=placed,
        out_specs=(P(("grp", "ctx"), None),) * 4,
        check_vma=False,
    )
```

time: 88.8 us -> 84.6 us (0.953)
  starting transfers between devices: 37 us -> 32.1 us
  waiting for transfers between devices: 24.1 us -> 27.1 us
  Pallas kernels: 16.8 us -> 14.7 us
    ppermute x8 -> x4, starting transfers between devices: 9.76 us -> 4.9 us  [back_round(): lax.ppermute(value, 'ctx', [((at + steps) % devices, at) for at in range(...]
    ppermute x8 -> x4, waiting for transfers between devices: 0.02 us -> 2.99 us  [back_round(): lax.ppermute(value, 'ctx', [((at + steps) % devices, at) for at in range(...]
    pallas_call x4 -> x3, Pallas kernels: 16.8 us -> 14.7 us  [call(): pl.pallas_call(kernel, in_specs=in_specs, out_specs=out_specs, out_shape=...]
  transfers between devices with their start and end apart: 22 -> 18, of which waited for: 9 -> 12; matrix products, arithmetic and copies ran while one was open for 5% -> 6% of each run, Pallas kernels for 15% -> 5%
where the time goes in v3:
time: 84.6 us; the launch traced here: 84 us
  starting transfers between devices  32.1 us (38%)
  waiting for transfers between devices  27.1 us (32%)
  Pallas kernels  14.7 us (17%)
  other arithmetic  4.91 us (6%)
  local copies, waits for them, and re-layouts  3.29 us (4%)
  between operations  1.9 us (2%)
    ppermute x4, starting transfers between devices, up(): lax.ppermute(value, 'ctx', [(at, at + steps) for at in range(devices - st...  17.3 us
    ppermute x4, waiting for transfers between devices, down(): lax.ppermute(value, 'ctx', [(at + steps, at) for at in range(devices - st...  16.2 us
    pallas_call x3, Pallas kernels, call(): pl.pallas_call(kernel, in_specs=in_specs, out_specs=out_specs, out_shape=...  14.7 us
    ppermute x6, waiting for transfers between devices, swap(): return lax.ppermute(value, 'ctx', [(at, at ^ bit) for at in range(devices)])  6.18 us
    ppermute x4, starting transfers between devices, down(): lax.ppermute(value, 'ctx', [(at + steps, at) for at in range(devices - st...  5.13 us
    ppermute x4, starting transfers between devices, back_round(): lax.ppermute(value, 'ctx', [((at + steps) % devices, at) for at in range(...  4.9 us
    ppermute x6, starting transfers between devices, swap(): return lax.ppermute(value, 'ctx', [(at, at ^ bit) for at in range(devices)])  4.82 us
    select_n x2, other arithmetic, local(): jnp.where(core == 0, key_pack, keys_by[2])  3.38 us
  transfers between devices with their start and end apart: 18, of which 12 were waited for; matrix products, arithmetic and copies ran while one was open for 6% of the time, Pallas kernels for 5%

profile of v3, /device:TPU:0, one launch (start us, length us, event | category | flops | bytes accessed | tf_op | source)
XLA Modules:
  0.0 84.0 jit_solution(5722780715031930704)
XLA Ops:
  0.7 1.3 %fusion.2 = (bf16[256,512]{1,0:T(8,128)(2,1)S(1)}, bf16[256,512]{1,0:T(8,128)(2,1)S(1)}, bf16[256,512]{1,0:T(8,128)(2,1)S(1)}, bf16[256,512]{1,0:T(8,128)(2,1)S(1)}) fusion(bf16[256,1024]{1,0:T(8,128)(2,1)} %q_ref.5, bf16[256,1024]{1,0:T(8,128)(2,1)} %g_ref.5), kind=kLoop, calls=%fused_computation.21 | loop fusion | bytes 2097152 | tf_op jit(solution)/shard_map/slice | solution.py:350
  3.2 3.0 %collective-permute-start.9 = (bf16[512,512]{1,0:T(8,128)(2,1)S(1)}, bf16[512,512]{1,0:T(8,128)(2,1)S(1)}, u32[]{:S(2)}, u32[]{:S(2)}) collective-permute-start(bf16[512,512]{1,0:T(8,128)(2,1)S(1)} %get-tuple-element.56), channel_id=1, source_target_pairs={{0,2},{1,3},{2,0},{3,1},{4,6},{5,7},{6,4},{7,5},{8,10},{9,11},{10,... | collective-permute-start | bytes 1572872 | tf_op jit(solution)/shard_map/ppermute | solution.py:337
  6.2 3.5 %collective-permute-start.7 = (bf16[512,512]{1,0:T(8,128)(2,1)S(1)}, bf16[512,512]{1,0:T(8,128)(2,1)S(1)}, u32[]{:S(2)}, u32[]{:S(2)}) collective-permute-start(bf16[512,512]{1,0:T(8,128)(2,1)S(1)} %get-tuple-element.57), channel_id=1, source_target_pairs={{0,4},{1,5},{2,6},{3,7},{4,8},{5,9},{6,10},{7,11},{8,12},{9,13},{1... | collective-permute-start | bytes 1572872 | tf_op jit(solution)/shard_map/ppermute | solution.py:331
  9.7 1.3 %collective-permute-start.8 = (bf16[512,512]{1,0:T(8,128)(2,1)S(1)}, bf16[512,512]{1,0:T(8,128)(2,1)S(1)}, u32[]{:S(2)}, u32[]{:S(2)}) collective-permute-start(bf16[512,512]{1,0:T(8,128)(2,1)S(1)} %get-tuple-element.58), channel_id=1, source_target_pairs={{4,0},{5,1},{6,2},{7,3},{8,4},{9,5},{10,6},{11,7},{12,8},{13,9},{1... | collective-permute-start | bytes 1572872 | tf_op jit(solution)/shard_map/ppermute | solution.py:334
  11.3 0.6 collective-permute-start.2
  11.8 4.6 %collective-permute-start = (bf16[512,512]{1,0:T(8,128)(2,1)S(1)}, bf16[512,512]{1,0:T(8,128)(2,1)S(1)}, u32[]{:S(2)}, u32[]{:S(2)}) collective-permute-start(bf16[512,512]{1,0:T(8,128)(2,1)S(1)} %get-tuple-element.68), channel_id=1, source_target_pairs={{0,4},{1,5},{2,6},{3,7},{4,8},{5,9},{6,10},{7,11},{8,12},{9,13},{1... | collective-permute-start | bytes 1572872 | tf_op jit(solution)/shard_map/ppermute | solution.py:331
  16.4 2.6 %collective-permute-done.9 = bf16[512,512]{1,0:T(8,128)(2,1)S(1)} collective-permute-done((bf16[512,512]{1,0:T(8,128)(2,1)S(1)}, bf16[512,512]{1,0:T(8,128)(2,1)S(1)}, u32[]{:S(2)}, u32[]{:S(2)}) %collective-permute-start.9) | collective-permute-done | bytes 524320 | tf_op jit(solution)/shard_map/ppermute | solution.py:337
  19.0 1.3 %collective-permute-start.1 = (bf16[512,512]{1,0:T(8,128)(2,1)S(1)}, bf16[512,512]{1,0:T(8,128)(2,1)S(1)}, u32[]{:S(2)}, u32[]{:S(2)}) collective-permute-start(bf16[512,512]{1,0:T(8,128)(2,1)S(1)} %get-tuple-element.69), channel_id=1, source_target_pairs={{4,0},{5,1},{6,2},{7,3},{8,4},{9,5},{10,6},{11,7},{12,8},{13,9},{1... | collective-permute-start | bytes 1572872 | tf_op jit(solution)/shard_map/ppermute | solution.py:334
  20.3 1.8 %collective-permute-done.7.refs_2_ = bf16[512,512]{1,0:T(8,128)(2,1)S(1)} collective-permute-done((bf16[512,512]{1,0:T(8,128)(2,1)S(1)}, bf16[512,512]{1,0:T(8,128)(2,1)S(1)}, u32[]{:S(2)}, u32[]{:S(2)}) %collective-permute-start.7) | collective-permute-done | bytes 524320 | tf_op jit(solution)/shard_map/ppermute | solution.py:331
  22.0 4.4 %collective-permute-done.8.refs_2_ = bf16[512,512]{1,0:T(8,128)(2,1)S(1)} collective-permute-done((bf16[512,512]{1,0:T(8,128)(2,1)S(1)}, bf16[512,512]{1,0:T(8,128)(2,1)S(1)}, u32[]{:S(2)}, u32[]{:S(2)}) %collective-permute-start.8) | collective-permute-done | bytes 524320 | tf_op jit(solution)/shard_map/ppermute | solution.py:334
  26.6 0.6 collective-permute-start.10
  27.1 1.3 %collective-permute-start.12 = (bf16[512,512]{1,0:T(8,128)(2,1)S(1)}, bf16[512,512]{1,0:T(8,128)(2,1)}, u32[]{:S(2)}, u32[]{:S(2)}) collective-permute-start(bf16[512,512]{1,0:T(8,128)(2,1)S(1)} %collective-permute-done.8.refs_2_), channel_id=1, source_target_pairs={{4,0},{5,1},{6,2},{7,3},{8,4},{9,5},{10,6},{11,7},{12,8},{13,9},{1... | collective-permute-start | bytes 1572872 | tf_op jit(solution)/shard_map/ppermute | solution.py:334
  28.4 1.8 %collective-permute-done.2 = bf16[512,512]{1,0:T(8,128)(2,1)S(1)} collective-permute-done((bf16[512,512]{1,0:T(8,128)(2,1)S(1)}, bf16[512,512]{1,0:T(8,128)(2,1)S(1)}, u32[]{:S(2)}, u32[]{:S(2)}) %collective-permute-start.2) | collective-permute-done | bytes 524320 | tf_op jit(solution)/shard_map/ppermute | solution.py:337
  30.2 4.8 %collective-permute-start.11 = (bf16[512,512]{1,0:T(8,128)(2,1)S(1)}, bf16[512,512]{1,0:T(8,128)(2,1)}, u32[]{:S(2)}, u32[]{:S(2)}) collective-permute-start(bf16[512,512]{1,0:T(8,128)(2,1)S(1)} %collective-permute-done.7.refs_2_), channel_id=1, source_target_pairs={{0,4},{1,5},{2,6},{3,7},{4,8},{5,9},{6,10},{7,11},{8,12},{9,13},{1... | collective-permute-start | bytes 1572872 | tf_op jit(solution)/shard_map/ppermute | solution.py:331
  35.0 2.7 %collective-permute-done.1.refs_6_ = bf16[512,512]{1,0:T(8,128)(2,1)S(1)} collective-permute-done((bf16[512,512]{1,0:T(8,128)(2,1)S(1)}, bf16[512,512]{1,0:T(8,128)(2,1)S(1)}, u32[]{:S(2)}, u32[]{:S(2)}) %collective-permute-start.1) | collective-permute-done | bytes 524320 | tf_op jit(solution)/shard_map/ppermute | solution.py:334
  37.7 1.3 %collective-permute-start.5 = (bf16[512,512]{1,0:T(8,128)(2,1)S(1)}, bf16[512,512]{1,0:T(8,128)(2,1)}, u32[]{:S(2)}, u32[]{:S(2)}) collective-permute-start(bf16[512,512]{1,0:T(8,128)(2,1)S(1)} %collective-permute-done.1.refs_6_), channel_id=1, source_target_pairs={{4,0},{5,1},{6,2},{7,3},{8,4},{9,5},{10,6},{11,7},{12,8},{13,9},{1... | collective-permute-start | bytes 1572872 | tf_op jit(solution)/shard_map/ppermute | solution.py:334
  39.0 0.9 %broadcast_select_fusion.6 = bf16[512,512]{1,0:T(8,128)(2,1)} fusion(bf16[512,512]{1,0:T(8,128)(2,1)S(1)} %collective-permute-done.1.refs_6_, bf16[512,512]{1,0:T(8,128)(2,1)S(1)} %collective-permute-done.refs_2_, pred[]{:T(512)S(6)} %eq.8), kind=kLoop, calls=%fused_computation.12 | loop fusion | flops 262144 | bytes 1572865 | tf_op jit(solution)/shard_map/jit(_where)/select_n | solution.py:371
  40.4 1.1 %collective-permute-done.10 = bf16[512,512]{1,0:T(8,128)(2,1)S(1)} collective-permute-done((bf16[512,512]{1,0:T(8,128)(2,1)S(1)}, bf16[512,512]{1,0:T(8,128)(2,1)S(1)}, u32[]{:S(2)}, u32[]{:S(2)}) %collective-permute-start.10) | collective-permute-done | bytes 524320 | tf_op jit(solution)/shard_map/ppermute | solution.py:337
  41.4 0.8 copy-done.18
  42.2 4.4 %collective-permute-start.4 = (bf16[512,512]{1,0:T(8,128)(2,1)S(1)}, bf16[512,512]{1,0:T(8,128)(2,1)}, u32[]{:S(2)}, u32[]{:S(2)}) collective-permute-start(bf16[512,512]{1,0:T(8,128)(2,1)S(1)} %collective-permute-done.refs_2_), channel_id=1, source_target_pairs={{0,4},{1,5},{2,6},{3,7},{4,8},{5,9},{6,10},{7,11},{8,12},{9,13},{1... | collective-permute-start | bytes 1572872 | tf_op jit(solution)/shard_map/ppermute | solution.py:331
  46.6 2.4 %collective-permute-done.12.refs_3_ = bf16[512,512]{1,0:T(8,128)(2,1)} collective-permute-done((bf16[512,512]{1,0:T(8,128)(2,1)S(1)}, bf16[512,512]{1,0:T(8,128)(2,1)}, u32[]{:S(2)}, u32[]{:S(2)}) %collective-permute-start.12) | collective-permute-done | bytes 524320 | tf_op jit(solution)/shard_map/ppermute | solution.py:334
  49.1 1.9 %broadcast_select_fusion.9 = (bf16[512,512]{1,0:T(8,128)(2,1)S(1)}, bf16[512,512]{1,0:T(8,128)(2,1)S(1)}, bf16[512,512]{1,0:T(8,128)(2,1)S(1)}, bf16[512,512]{1,0:T(8,128)(2,1)S(1)}) fusion(pred[]{:T(512)S(6)} %eq.7, bf16[256,512]{1,0:T(8,128)(2,1)} %copy-done.14, bf16[256,512]{1,0:T(8,128)(2,1)} %copy-done.13, bf16[512,512]{1,0:T(8,128)(2,1)} %copy-done.18, ...), kind=kLoop, calls=%fused_computation.15 | loop fusion | flops 3145728 | bytes 4194306 | tf_op jit(solution)/shard_map/jit(_where)/select_n | solution.py:389
  51.2 0.8 collective-permute-done.3
  52.0 6.6 %collective-permute-done.5.refs_7_ = bf16[512,512]{1,0:T(8,128)(2,1)} collective-permute-done((bf16[512,512]{1,0:T(8,128)(2,1)S(1)}, bf16[512,512]{1,0:T(8,128)(2,1)}, u32[]{:S(2)}, u32[]{:S(2)}) %collective-permute-start.5) | collective-permute-done | bytes 524320 | tf_op jit(solution)/shard_map/ppermute | solution.py:334
  58.6 1.5 %broadcast_select_fusion.11 = (bf16[512,512]{1,0:T(8,128)(2,1)S(1)}, bf16[512,512]{1,0:T(8,128)(2,1)S(1)}, bf16[512,512]{1,0:T(8,128)(2,1)S(1)}, bf16[512,512]{1,0:T(8,128)(2,1)S(1)}) fusion(pred[]{:T(512)S(6)} %eq.7, bf16[256,512]{1,0:T(8,128)(2,1)S(1)} %copy-done.10, bf16[256,512]{1,0:T(8,128)(2,1)S(1)} %copy-done.8, ...), kind=kLoop, calls=%fused_computation.17 | loop fusion | flops 3145728 | bytes 4194306 | tf_op jit(solution)/shard_map/jit(_where)/select_n | solution.py:389
  61.3 4.4 %shard_map.93 = (bf16[256,1024]{1,0:T(8,128)(2,1)}, bf16[256,1024]{1,0:T(8,128)(2,1)}, f32[4,8,256]{2,1,0:T(8,128)S(1)}) custom-call(s32[3]{0:T(128)S(1)} %pad_add_fusion.info, s32[2,8]{1,0:T(2,128)S(1)} %copy-done.4, bf16[256,1024]{1,0:T(8,128)(2,1)S(1)} %copy-done, bf16[256,1024]{1,0:T(8,128)(2,1)S(1)} %copy-done.1, bf16[256,1024]{1,0:T(8,128)(2,1)S(1)} %copy-done.2, ...), custom_call_target="tpu_custom_call" | custom-call | flops 805306368 | bytes 6291456 | tf_op jit(solution)/shard_map/pallas_call | solution.py:304
  65.7 4.4 %shard_map.94 = (bf16[256,1024]{1,0:T(8,128)(2,1)}, bf16[256,1024]{1,0:T(8,128)(2,1)}, f32[4,8,256]{2,1,0:T(8,128)S(1)}) custom-call(s32[3]{0:T(128)S(1)} %pad_add_fusion.info, s32[2,8]{1,0:T(2,128)S(1)} %copy-done.4, bf16[256,1024]{1,0:T(8,128)(2,1)S(1)} %copy-done, ...), custom_call_target="tpu_custom_call", output_to_operand_aliasing={{0}: (11, {}), {1}: (12, {})} | custom-call | flops 805306368 | bytes 6291456 | tf_op jit(solution)/shard_map/pallas_call | solution.py:304
  70.2 2.6 %collective-permute-start.17 = (f32[4,8,256]{2,1,0:T(8,128)S(1)}, f32[4,8,256]{2,1,0:T(8,128)S(1)}, u32[]{:S(2)}, u32[]{:S(2)}) collective-permute-start(f32[4,8,256]{2,1,0:T(8,128)S(1)} %get-tuple-element.41.refs_8_), channel_id=1, source_target_pairs={{8,0},{9,1},{10,2},{11,3},{12,4},{13,5},{14,6},{15,7},{0,8},{1,9},... | collective-permute-start | bytes 98312 | tf_op jit(solution)/shard_map/ppermute | solution.py:340
  72.8 1.3 %collective-permute-start.16 = (f32[4,8,256]{2,1,0:T(8,128)S(1)}, f32[4,8,256]{2,1,0:T(8,128)S(1)}, u32[]{:S(2)}, u32[]{:S(2)}) collective-permute-start(f32[4,8,256]{2,1,0:T(8,128)S(1)} %get-tuple-element.41.refs_8_), channel_id=1, source_target_pairs={{4,0},{5,1},{6,2},{7,3},{8,4},{9,5},{10,6},{11,7},{12,8},{13,9},{1... | collective-permute-start | bytes 98312 | tf_op jit(solution)/shard_map/ppermute | solution.py:340
  75.4 1.6 %collective-permute-done.16.refs_11_ = f32[4,8,256]{2,1,0:T(8,128)S(1)} collective-permute-done((f32[4,8,256]{2,1,0:T(8,128)S(1)}, f32[4,8,256]{2,1,0:T(8,128)S(1)}, u32[]{:S(2)}, u32[]{:S(2)}) %collective-permute-start.16) | collective-permute-done | bytes 32800 | tf_op jit(solution)/shard_map/ppermute | solution.py:340
  77.0 1.0 %collective-permute-done.15.refs_10_ = f32[4,8,256]{2,1,0:T(8,128)S(1)} collective-permute-done((f32[4,8,256]{2,1,0:T(8,128)S(1)}, f32[4,8,256]{2,1,0:T(8,128)S(1)}, u32[]{:S(2)}, u32[]{:S(2)}) %collective-permute-start.15) | collective-permute-done | bytes 32800 | tf_op jit(solution)/shard_map/ppermute | solution.py:340
  78.1 5.8 %shard_map.95 = (bf16[256,1024]{1,0:T(8,128)(2,1)}, bf16[256,1024]{1,0:T(8,128)(2,1)}) custom-call(s32[3]{0:T(128)S(1)} %pad_add_fusion.info, bf16[256,1024]{1,0:T(8,128)(2,1)S(1)} %copy-done, bf16[256,1024]{1,0:T(8,128)(2,1)S(1)} %copy-done.1, bf16[256,1024]{1,0:T(8,128)(2,1)S(1)} %copy-done.2, bf16[256,1024]{1,0:T(8,128)(2,1)S(1)} %copy-done.3, ...), custom_call_target="tpu_custom_call" | custom-call | flops 1610612736 | bytes 6291456 | tf_op jit(solution)/shard_map/pallas_call | solution.py:304
  (56 shorter events, 3.7 us)
Async XLA Ops:
  0.7 1.4 %copy-start.1 = (bf16[256,1024]{1,0:T(8,128)(2,1)S(1)}, bf16[256,1024]{1,0:T(8,128)(2,1)}, u32[]{:S(2)}) copy-start(bf16[256,1024]{1,0:T(8,128)(2,1)} %k_ref.5) | copy-start | bytes 1572868
  0.7 1.5 %copy-start.2 = (bf16[256,1024]{1,0:T(8,128)(2,1)S(1)}, bf16[256,1024]{1,0:T(8,128)(2,1)}, u32[]{:S(2)}) copy-start(bf16[256,1024]{1,0:T(8,128)(2,1)} %v_ref.5) | copy-start | bytes 1572868
  2.2 8.9 %copy-start.5 = (bf16[256,512]{1,0:T(8,128)(2,1)}, bf16[256,512]{1,0:T(8,128)(2,1)S(1)}, u32[]{:S(2)}) copy-start(bf16[256,512]{1,0:T(8,128)(2,1)S(1)} %get-tuple-element.72) | copy-start | bytes 786436
  2.3 8.8 %copy-start.7 = (bf16[256,512]{1,0:T(8,128)(2,1)}, bf16[256,512]{1,0:T(8,128)(2,1)S(1)}, u32[]{:S(2)}) copy-start(bf16[256,512]{1,0:T(8,128)(2,1)S(1)} %get-tuple-element.60) | copy-start | bytes 786436
  2.3 8.8 %copy-start.9 = (bf16[256,512]{1,0:T(8,128)(2,1)}, bf16[256,512]{1,0:T(8,128)(2,1)S(1)}, u32[]{:S(2)}) copy-start(bf16[256,512]{1,0:T(8,128)(2,1)S(1)} %get-tuple-element.70) | copy-start | bytes 786436
  3.2 15.8 %collective-permute-start.9 = (bf16[512,512]{1,0:T(8,128)(2,1)S(1)}, bf16[512,512]{1,0:T(8,128)(2,1)S(1)}, u32[]{:S(2)}, u32[]{:S(2)}) collective-permute-start(bf16[512,512]{1,0:T(8,128)(2,1)S(1)} %get-tuple-element.56), channel_id=1, source_target_pairs={{0,2},{1,3},{2,0},{3,1},{4,6},{5,7},{6,4},{7,5},{8,10},{9,11},{10,... | collective-permute-start | bytes 1572872 | tf_op jit(solution)/shard_map/ppermute | solution.py:337
  6.2 15.8 %collective-permute-start.7 = (bf16[512,512]{1,0:T(8,128)(2,1)S(1)}, bf16[512,512]{1,0:T(8,128)(2,1)S(1)}, u32[]{:S(2)}, u32[]{:S(2)}) collective-permute-start(bf16[512,512]{1,0:T(8,128)(2,1)S(1)} %get-tuple-element.57), channel_id=1, source_target_pairs={{0,4},{1,5},{2,6},{3,7},{4,8},{5,9},{6,10},{7,11},{8,12},{9,13},{1... | collective-permute-start | bytes 1572872 | tf_op jit(solution)/shard_map/ppermute | solution.py:331
  9.7 16.8 %collective-permute-start.8 = (bf16[512,512]{1,0:T(8,128)(2,1)S(1)}, bf16[512,512]{1,0:T(8,128)(2,1)S(1)}, u32[]{:S(2)}, u32[]{:S(2)}) collective-permute-start(bf16[512,512]{1,0:T(8,128)(2,1)S(1)} %get-tuple-element.58), channel_id=1, source_target_pairs={{4,0},{5,1},{6,2},{7,3},{8,4},{9,5},{10,6},{11,7},{12,8},{13,9},{1... | collective-permute-start | bytes 1572872 | tf_op jit(solution)/shard_map/ppermute | solution.py:334
  11.3 18.9 %collective-permute-start.2 = (bf16[512,512]{1,0:T(8,128)(2,1)S(1)}, bf16[512,512]{1,0:T(8,128)(2,1)S(1)}, u32[]{:S(2)}, u32[]{:S(2)}) collective-permute-start(bf16[512,512]{1,0:T(8,128)(2,1)S(1)} %get-tuple-element.67), channel_id=1, source_target_pairs={{0,2},{1,3},{2,0},{3,1},{4,6},{5,7},{6,4},{7,5},{8,10},{9,11},{10,... | collective-permute-start | bytes 1572872 | tf_op jit(solution)/shard_map/ppermute | solution.py:337
  11.8 23.2 %collective-permute-start = (bf16[512,512]{1,0:T(8,128)(2,1)S(1)}, bf16[512,512]{1,0:T(8,128)(2,1)S(1)}, u32[]{:S(2)}, u32[]{:S(2)}) collective-permute-start(bf16[512,512]{1,0:T(8,128)(2,1)S(1)} %get-tuple-element.68), channel_id=1, source_target_pairs={{0,4},{1,5},{2,6},{3,7},{4,8},{5,9},{6,10},{7,11},{8,12},{9,13},{1... | collective-permute-start | bytes 1572872 | tf_op jit(solution)/shard_map/ppermute | solution.py:331
  19.0 20.9 %copy-start.17 = (bf16[512,512]{1,0:T(8,128)(2,1)}, bf16[512,512]{1,0:T(8,128)(2,1)S(1)}, u32[]{:S(2)}) copy-start(bf16[512,512]{1,0:T(8,128)(2,1)S(1)} %collective-permute-done.9) | copy-start | bytes 1572868
  19.0 18.7 %collective-permute-start.1 = (bf16[512,512]{1,0:T(8,128)(2,1)S(1)}, bf16[512,512]{1,0:T(8,128)(2,1)S(1)}, u32[]{:S(2)}, u32[]{:S(2)}) collective-permute-start(bf16[512,512]{1,0:T(8,128)(2,1)S(1)} %get-tuple-element.69), channel_id=1, source_target_pairs={{4,0},{5,1},{6,2},{7,3},{8,4},{9,5},{10,6},{11,7},{12,8},{13,9},{1... | collective-permute-start | bytes 1572872 | tf_op jit(solution)/shard_map/ppermute | solution.py:334
  26.6 14.9 %collective-permute-start.10 = (bf16[512,512]{1,0:T(8,128)(2,1)S(1)}, bf16[512,512]{1,0:T(8,128)(2,1)S(1)}, u32[]{:S(2)}, u32[]{:S(2)}) collective-permute-start(bf16[512,512]{1,0:T(8,128)(2,1)S(1)} %broadcast_select_fusion.2), channel_id=1, source_target_pairs={{0,2},{1,3},{2,0},{3,1},{4,6},{5,7},{6,4},{7,5},{8,10},{9,11},{10,... | collective-permute-start | bytes 1572872 | tf_op jit(solution)/shard_map/ppermute | solution.py:337
  27.1 21.9 %collective-permute-start.12 = (bf16[512,512]{1,0:T(8,128)(2,1)S(1)}, bf16[512,512]{1,0:T(8,128)(2,1)}, u32[]{:S(2)}, u32[]{:S(2)}) collective-permute-start(bf16[512,512]{1,0:T(8,128)(2,1)S(1)} %collective-permute-done.8.refs_2_), channel_id=1, source_target_pairs={{4,0},{5,1},{6,2},{7,3},{8,4},{9,5},{10,6},{11,7},{12,8},{13,9},{1... | collective-permute-start | bytes 1572872 | tf_op jit(solution)/shard_map/ppermute | solution.py:334
  30.2 10.2 %copy-start.15 = (bf16[512,512]{1,0:T(8,128)(2,1)}, bf16[512,512]{1,0:T(8,128)(2,1)S(1)}, u32[]{:S(2)}) copy-start(bf16[512,512]{1,0:T(8,128)(2,1)S(1)} %collective-permute-done.2) | copy-start | bytes 1572868
  30.2 18.9 %collective-permute-start.11 = (bf16[512,512]{1,0:T(8,128)(2,1)S(1)}, bf16[512,512]{1,0:T(8,128)(2,1)}, u32[]{:S(2)}, u32[]{:S(2)}) collective-permute-start(bf16[512,512]{1,0:T(8,128)(2,1)S(1)} %collective-permute-done.7.refs_2_), channel_id=1, source_target_pairs={{0,4},{1,5},{2,6},{3,7},{4,8},{5,9},{6,10},{7,11},{8,12},{9,13},{1... | collective-permute-start | bytes 1572872 | tf_op jit(solution)/shard_map/ppermute | solution.py:331
  37.7 20.8 %collective-permute-start.5 = (bf16[512,512]{1,0:T(8,128)(2,1)S(1)}, bf16[512,512]{1,0:T(8,128)(2,1)}, u32[]{:S(2)}, u32[]{:S(2)}) collective-permute-start(bf16[512,512]{1,0:T(8,128)(2,1)S(1)} %collective-permute-done.1.refs_6_), channel_id=1, source_target_pairs={{4,0},{5,1},{6,2},{7,3},{8,4},{9,5},{10,6},{11,7},{12,8},{13,9},{1... | collective-permute-start | bytes 1572872 | tf_op jit(solution)/shard_map/ppermute | solution.py:334
  39.9 12.1 %collective-permute-start.3 = (bf16[512,512]{1,0:T(8,128)(2,1)}, bf16[512,512]{1,0:T(8,128)(2,1)}, u32[]{:S(2)}, u32[]{:S(2)}) collective-permute-start(bf16[512,512]{1,0:T(8,128)(2,1)} %broadcast_select_fusion.6), channel_id=1, source_target_pairs={{0,2},{1,3},{2,0},{3,1},{4,6},{5,7},{6,4},{7,5},{8,10},{9,11},{10,... | collective-permute-start | bytes 1572872 | tf_op jit(solution)/shard_map/ppermute | solution.py:337
  42.2 16.3 %collective-permute-start.4 = (bf16[512,512]{1,0:T(8,128)(2,1)S(1)}, bf16[512,512]{1,0:T(8,128)(2,1)}, u32[]{:S(2)}, u32[]{:S(2)}) collective-permute-start(bf16[512,512]{1,0:T(8,128)(2,1)S(1)} %collective-permute-done.refs_2_), channel_id=1, source_target_pairs={{0,4},{1,5},{2,6},{3,7},{4,8},{5,9},{6,10},{7,11},{8,12},{9,13},{1... | collective-permute-start | bytes 1572872 | tf_op jit(solution)/shard_map/ppermute | solution.py:331
  51.0 7.5 %copy-start.6 = (bf16[256,512]{1,0:T(8,128)(2,1)S(1)}, bf16[256,512]{1,0:T(8,128)(2,1)}, u32[]{:S(2)}) copy-start(bf16[256,512]{1,0:T(8,128)(2,1)} %copy-done.5) | copy-start | bytes 786436
  51.0 7.5 %copy-start.8 = (bf16[256,512]{1,0:T(8,128)(2,1)S(1)}, bf16[256,512]{1,0:T(8,128)(2,1)}, u32[]{:S(2)}) copy-start(bf16[256,512]{1,0:T(8,128)(2,1)} %copy-done.7) | copy-start | bytes 786436
  51.0 7.5 %copy-start.10 = (bf16[256,512]{1,0:T(8,128)(2,1)S(1)}, bf16[256,512]{1,0:T(8,128)(2,1)}, u32[]{:S(2)}) copy-start(bf16[256,512]{1,0:T(8,128)(2,1)} %copy-done.9) | copy-start | bytes 786436
  51.0 7.5 %copy-start.16 = (bf16[512,512]{1,0:T(8,128)(2,1)S(1)}, bf16[512,512]{1,0:T(8,128)(2,1)}, u32[]{:S(2)}) copy-start(bf16[512,512]{1,0:T(8,128)(2,1)} %copy-done.15) | copy-start | bytes 1572868
  51.1 9.9 %collective-permute-start.13 = (bf16[1024,512]{1,0:T(8,128)(2,1)S(1)}, bf16[1024,512]{1,0:T(8,128)(2,1)S(1)}, u32[]{:S(2)}, u32[]{:S(2)}) collective-permute-start(bf16[1024,512]{1,0:T(8,128)(2,1)S(1)} %pad_maximum_fusion.1), channel_id=1, source_target_pairs={{0,1},{1,0},{2,3},{3,2},{4,5},{5,4},{6,7},{7,6},{8,9},{9,8},{10,11... | collective-permute-start | bytes 3145736 | tf_op jit(solution)/shard_map/ppermute | solution.py:337
  60.0 1.0 %copy-start = (bf16[256,1024]{1,0:T(8,128)(2,1)S(1)}, bf16[256,1024]{1,0:T(8,128)(2,1)}, u32[]{:S(2)}) copy-start(bf16[256,1024]{1,0:T(8,128)(2,1)} %q_ref.5) | copy-start | bytes 1572868
  60.0 1.2 %copy-start.3 = (bf16[256,1024]{1,0:T(8,128)(2,1)S(1)}, bf16[256,1024]{1,0:T(8,128)(2,1)}, u32[]{:S(2)}) copy-start(bf16[256,1024]{1,0:T(8,128)(2,1)} %g_ref.5) | copy-start | bytes 1572868
  60.1 1.2 %copy-start.4 = (s32[2,8]{1,0:T(2,128)S(1)}, s32[2,8]{1,0:T(2,128)}, u32[]{:S(2)}) copy-start(s32[2,8]{1,0:T(2,128)} %kb.3) | copy-start | bytes 196
  60.1 5.5 %collective-permute-start.6 = (bf16[1024,512]{1,0:T(8,128)(2,1)S(1)}, bf16[1024,512]{1,0:T(8,128)(2,1)S(1)}, u32[]{:S(2)}, u32[]{:S(2)}) collective-permute-start(bf16[1024,512]{1,0:T(8,128)(2,1)S(1)} %pad_maximum_fusion), channel_id=1, source_target_pairs={{0,1},{1,0},{2,3},{3,2},{4,5},{5,4},{6,7},{7,6},{8,9},{9,8},{10,11... | collective-permute-start | bytes 3145736 | tf_op jit(solution)/shard_map/ppermute | solution.py:337
  70.2 5.2 %collective-permute-start.17 = (f32[4,8,256]{2,1,0:T(8,128)S(1)}, f32[4,8,256]{2,1,0:T(8,128)S(1)}, u32[]{:S(2)}, u32[]{:S(2)}) collective-permute-start(f32[4,8,256]{2,1,0:T(8,128)S(1)} %get-tuple-element.41.refs_8_), channel_id=1, source_target_pairs={{8,0},{9,1},{10,2},{11,3},{12,4},{13,5},{14,6},{15,7},{0,8},{1,9},... | collective-permute-start | bytes 98312 | tf_op jit(solution)/shard_map/ppermute | solution.py:340
  72.8 4.2 %collective-permute-start.16 = (f32[4,8,256]{2,1,0:T(8,128)S(1)}, f32[4,8,256]{2,1,0:T(8,128)S(1)}, u32[]{:S(2)}, u32[]{:S(2)}) collective-permute-start(f32[4,8,256]{2,1,0:T(8,128)S(1)} %get-tuple-element.41.refs_8_), channel_id=1, source_target_pairs={{4,0},{5,1},{6,2},{7,3},{8,4},{9,5},{10,6},{11,7},{12,8},{13,9},{1... | collective-permute-start | bytes 98312 | tf_op jit(solution)/shard_map/ppermute | solution.py:340
  74.1 3.9 %collective-permute-start.15 = (f32[4,8,256]{2,1,0:T(8,128)S(1)}, f32[4,8,256]{2,1,0:T(8,128)S(1)}, u32[]{:S(2)}, u32[]{:S(2)}) collective-permute-start(f32[4,8,256]{2,1,0:T(8,128)S(1)} %get-tuple-element.41.refs_8_), channel_id=1, source_target_pairs={{2,0},{3,1},{4,2},{5,3},{6,4},{7,5},{8,6},{9,7},{10,8},{11,9},{12,... | collective-permute-start | bytes 98312 | tf_op jit(solution)/shard_map/ppermute | solution.py:340
  74.6 3.5 %collective-permute-start.14 = (f32[4,8,256]{2,1,0:T(8,128)S(1)}, f32[4,8,256]{2,1,0:T(8,128)S(1)}, u32[]{:S(2)}, u32[]{:S(2)}) collective-permute-start(f32[4,8,256]{2,1,0:T(8,128)S(1)} %get-tuple-element.41.refs_8_), channel_id=1, source_target_pairs={{1,0},{2,1},{3,2},{4,3},{5,4},{6,5},{7,6},{8,7},{9,8},{10,9},{11,1... | collective-permute-start | bytes 98312 | tf_op jit(solution)/shard_map/ppermute | solution.py:340
  (5 other events, 4.1 us)

commit v4 on v3

--- a/solution.py
+++ b/solution.py
@@ -13,7 +13,7 @@
 LEVELS = 8
 CHUNKS = 2
 QUERY_LAG = (0, 1, 2, 3)
-KEY_LAG = (0, 1, 1)
+KEY_LAG = (0, 1)
 FAR = 1e30
 SCALE = HEAD_DIM ** (-0.5)
 SCALE2 = SCALE * math.log2(math.e)
@@ -191,9 +191,48 @@
         copy.wait()
 
 
-def key_kernel(hops, chunks, info, q_ref, k_ref, v_ref, g_ref, *refs):
+def key_stack(hops, chunks, heads, refs):
     count = len(hops)
-    ahead_all = [refs[chunk * count : (chunk + 1) * count] for chunk in range(chunks)]
+
+    def stack(unit, own_ref, which):
+        pair, block = unit
+        chunk = pair * chunks * 2 // heads
+        ahead = refs[chunk * count : (chunk + 1) * count]
+
+        def part(ref, index):
+            shift = 0 if ref is own_ref else -chunk * heads // chunks * HEAD_DIM
+            return ref[
+                index * BLOCK : (index + 1) * BLOCK, pl.ds(shift + pair * 2 * HEAD_DIM, 2 * HEAD_DIM)
+            ]
+
+        parts = [part(own_ref, block)]
+        parts.append(part(own_ref, 1) if block == 0 else part(ahead[0], 4 + which * 2))
+        parts += [
+            part(ref, which * 2 + block + (4 if index == 0 else 0)) for index, ref in enumerate(ahead)
+        ]
+        return jnp.concatenate(parts, axis=0)
+
+    return stack
+
+
+def product_kernel(hops, chunks, q_ref, k_ref, v_ref, g_ref, *refs):
+    score_ref, grad_ref = refs[-2:]
+    heads = q_ref.shape[1] // HEAD_DIM
+    stack = key_stack(hops, chunks, heads, refs)
+    for pair in range(heads // 2):
+        for block in range(2):
+            rows = slice(block * BLOCK, (block + 1) * BLOCK)
+            columns = slice(2 * pair * HEAD_DIM, (2 * pair + 2) * HEAD_DIM)
+            unit = (pair, block)
+            scores = pair_rows(k_ref[rows, columns], stack(unit, q_ref, 0))
+            weight_grad = pair_rows(v_ref[rows, columns], stack(unit, g_ref, 1))
+            for index in range(2):
+                score_ref[2 * pair + index, rows] = scores[index]
+                grad_ref[2 * pair + index, rows] = weight_grad[index]
+
+
+def key_kernel(hops, chunks, info, score_ref, grad_ref, q_ref, g_ref, *refs):
+    count = len(hops)
     stats = refs[chunks * count : (chunks + 1) * count + 1]
     dk_out, dv_out, dk_ref, dv_ref, sems = refs[-5:]
     heads = dk_ref.shape[1] // HEAD_DIM
@@ -201,24 +240,7 @@
     flags = [ref[3] for ref in stats]
     units = [(pair, block) for pair in range(heads // 2) for block in range(2)]
     held = {}
-
-    def stack(unit, own_ref, which):
-        pair, block = unit
-        chunk = pair * chunks * 2 // heads
-        ahead = ahead_all[chunk]
-
-        def part(ref, index):
-            shift = 0 if ref is own_ref else -chunk * heads // chunks * HEAD_DIM
-            return ref[
-                index * BLOCK : (index + 1) * BLOCK, pl.ds(shift + pair * 2 * HEAD_DIM, 2 * HEAD_DIM)
-            ]
-
-        parts = [part(own_ref, block)]
-        parts.append(part(own_ref, 1) if block == 0 else part(ahead[0], 4 + which * 2))
-        parts += [
-            part(ref, which * 2 + block + (4 if index == 0 else 0)) for index, ref in enumerate(ahead)
-        ]
-        return jnp.concatenate(parts, axis=0)
+    stack = key_stack(hops, chunks, heads, refs)
 
     def place(unit, shift=0):
         pair, block = unit
@@ -230,20 +252,16 @@
     def lanes(array, row, index):
         return array[row : row + 1, index * BLOCK : (index + 1) * BLOCK]
 
-    def products(unit):
-        rows, columns = place(unit)
-        scores = pair_rows(k_ref[rows, columns], stack(unit, q_ref, 0))
-        weight_grad = pair_rows(v_ref[rows, columns], stack(unit, g_ref, 1))
-        held[unit] = (scores, weight_grad)
-
     def soften(unit):
         pair, block = unit
         held[unit] = [
-            soften_head(2 * pair + index, block, held[unit][0][index], held[unit][1][index])
+            soften_head(2 * pair + index, block)
             for index in range(2)
         ]
 
-    def soften_head(head, block, scores, weight_grad):
+    def soften_head(head, block):
+        scores = score_ref[head, block * BLOCK : (block + 1) * BLOCK]
+        weight_grad = grad_ref[head, block * BLOCK : (block + 1) * BLOCK]
         stat = [
             [ref[kind, head : head + 1, :] for kind in range(3)] for ref in stats
         ]
@@ -287,7 +305,7 @@
                 send_head(copies, head, 0, ((dk_ref, dk_out), (dv_ref, dv_out)), sems)
 
     copies = []
-    staged(units, (products, soften, finish), KEY_LAG)
+    staged(units, (soften, finish), KEY_LAG)
     for copy in copies:
         copy.wait()
 
@@ -314,7 +332,7 @@
         + scratch,
         input_output_aliases={before + index: index for index in range(len(previous))},
         cost_estimate=pl.CostEstimate(flops=flops, bytes_accessed=6 << 20, transcendentals=0),
-        compiler_params=pltpu.CompilerParams(vmem_limit_bytes=24 << 20),
+        compiler_params=pltpu.CompilerParams(vmem_limit_bytes=16 << 20),
     )(*scalars, *arrays, *previous)
 
 
@@ -412,11 +430,21 @@
         front = (att, dq)
         stats.append(stat)
     stats = [stat] + [back_round(stat, hop) for hop in hops]
+    ahead = sum((tuple(pair[1]) for pair in moved), ())
+    raw_shape = jax.ShapeDtypeStruct((head_count, rows_dev, pieces * BLOCK), jnp.float32)
+    raw = pl.pallas_call(
+        functools.partial(product_kernel, hops, CHUNKS),
+        in_specs=[pl.BlockSpec(memory_space=pltpu.VMEM)] * (len(own) + len(ahead)),
+        out_specs=[pl.BlockSpec(memory_space=pltpu.VMEM)] * 2,
+        out_shape=(raw_shape, raw_shape),
+        cost_estimate=pl.CostEstimate(flops=2 * flops, bytes_accessed=6 << 20, transcendentals=0),
+        compiler_params=pltpu.CompilerParams(vmem_limit_bytes=16 << 20),
+    )(*own, *ahead)
     back = call(
         functools.partial(key_kernel, hops, CHUNKS),
         head_count,
         (info,),
-        own + sum((tuple(pair[1]) for pair in moved), ()) + tuple(stats),
+        tuple(raw) + (queries, out_grad) + ahead + tuple(stats),
         (),
         (full, full),
         [],

time: 84.6 us -> 82.3 us (0.973)
  waiting for transfers between devices: 27.1 us -> 23.7 us
  starting transfers between devices: 32.1 us -> 33.5 us
    ppermute x6, waiting for transfers between devices: 6.18 us -> 2.55 us  [swap(): return lax.ppermute(value, 'ctx', [(at, at ^ bit) for at in range(devices)])]
    ppermute x4, waiting for transfers between devices: 2.99 us -> 0.36 us  [back_round(): lax.ppermute(value, 'ctx', [((at + steps) % devices, at) for at in range(...]
    ppermute x6, starting transfers between devices: 4.82 us -> 6.84 us  [swap(): return lax.ppermute(value, 'ctx', [(at, at ^ bit) for at in range(devices)])]
    pallas_call x3, Pallas kernels: 14.7 us -> 12.7 us  [call(): pl.pallas_call(kernel, in_specs=in_specs, out_specs=out_specs, out_shape=...]
    ppermute x4, waiting for transfers between devices: 16.2 us -> 18 us  [down(): lax.ppermute(value, 'ctx', [(at + steps, at) for at in range(devices - st...]
    pallas_call x0 -> x1, Pallas kernels: none -> 1.83 us  [local(): pl.pallas_call(functools.partial(product_kernel, hops, CHUNKS), in_specs=...]
    slice x1, local copies, waits for them, and re-layouts: 0.07 us -> 1.34 us  [local(): keys[:, cut]]
    slice x1, local copies, waits for them, and re-layouts: 1.34 us -> 0.07 us  [local(): queries[:, cut]]
  transfers between devices with their start and end apart: 18 -> 18, of which waited for: 12 -> 9; matrix products, arithmetic and copies ran while one was open for 6% -> 6% of each run, Pallas kernels for 5% -> 8%
where the time goes in v4:
time: 82.3 us; the launch traced here: 81.7 us
  starting transfers between devices  33.5 us (41%)
  waiting for transfers between devices  23.7 us (29%)
  Pallas kernels  14.5 us (18%)
  other arithmetic  5.08 us (6%)
  local copies, waits for them, and re-layouts  3.05 us (4%)
  between operations  1.91 us (2%)
    ppermute x4, waiting for transfers between devices, down(): lax.ppermute(value, 'ctx', [(at + steps, at) for at in range(devices - st...  18 us
    ppermute x4, starting transfers between devices, up(): lax.ppermute(value, 'ctx', [(at, at + steps) for at in range(devices - st...  16.6 us
    pallas_call x3, Pallas kernels, call(): pl.pallas_call(kernel, in_specs=in_specs, out_specs=out_specs, out_shape=...  12.7 us
    ppermute x6, starting transfers between devices, swap(): return lax.ppermute(value, 'ctx', [(at, at ^ bit) for at in range(devices)])  6.84 us
    ppermute x4, starting transfers between devices, down(): lax.ppermute(value, 'ctx', [(at + steps, at) for at in range(devices - st...  5.12 us
    ppermute x4, starting transfers between devices, back_round(): lax.ppermute(value, 'ctx', [((at + steps) % devices, at) for at in range(...  4.9 us
    select_n x2, other arithmetic, local(): jnp.where(core == 0, key_pack, keys_by[2])  3.53 us
    ppermute x4, waiting for transfers between devices, up(): lax.ppermute(value, 'ctx', [(at, at + steps) for at in range(devices - st...  2.79 us
  transfers between devices with their start and end apart: 18, of which 9 were waited for; matrix products, arithmetic and copies ran while one was open for 6% of the time, Pallas kernels for 8%

profile of v4, /device:TPU:0, one launch (start us, length us, event | category | flops | bytes accessed | tf_op | source)
XLA Modules:
  0.0 81.7 jit_solution(4373357088452013023)
XLA Ops:
  0.7 1.3 %fusion = (bf16[256,512]{1,0:T(8,128)(2,1)S(1)}, bf16[256,512]{1,0:T(8,128)(2,1)S(1)}, bf16[256,512]{1,0:T(8,128)(2,1)S(1)}, bf16[256,512]{1,0:T(8,128)(2,1)S(1)}) fusion(bf16[256,1024]{1,0:T(8,128)(2,1)} %k_ref.5, bf16[256,1024]{1,0:T(8,128)(2,1)} %v_ref.5), kind=kLoop, calls=%fused_computation.19 | loop fusion | bytes 2097152 | tf_op jit(solution)/shard_map/slice | solution.py:367
  2.9 3.0 %collective-permute-start.9 = (bf16[512,512]{1,0:T(8,128)(2,1)S(1)}, bf16[512,512]{1,0:T(8,128)(2,1)S(1)}, u32[]{:S(2)}, u32[]{:S(2)}) collective-permute-start(bf16[512,512]{1,0:T(8,128)(2,1)S(1)} %get-tuple-element.60), channel_id=1, source_target_pairs={{0,2},{1,3},{2,0},{3,1},{4,6},{5,7},{6,4},{7,5},{8,10},{9,11},{10,... | collective-permute-start | bytes 1572872 | tf_op jit(solution)/shard_map/ppermute | solution.py:355
  5.9 4.3 %collective-permute-start.7 = (bf16[512,512]{1,0:T(8,128)(2,1)S(1)}, bf16[512,512]{1,0:T(8,128)(2,1)}, u32[]{:S(2)}, u32[]{:S(2)}) collective-permute-start(bf16[512,512]{1,0:T(8,128)(2,1)S(1)} %get-tuple-element.61), channel_id=1, source_target_pairs={{0,4},{1,5},{2,6},{3,7},{4,8},{5,9},{6,10},{7,11},{8,12},{9,13},{1... | collective-permute-start | bytes 1572872 | tf_op jit(solution)/shard_map/ppermute | solution.py:349
  10.2 1.3 %collective-permute-start.8 = (bf16[512,512]{1,0:T(8,128)(2,1)S(1)}, bf16[512,512]{1,0:T(8,128)(2,1)S(1)}, u32[]{:S(2)}, u32[]{:S(2)}) collective-permute-start(bf16[512,512]{1,0:T(8,128)(2,1)S(1)} %get-tuple-element.62), channel_id=1, source_target_pairs={{4,0},{5,1},{6,2},{7,3},{8,4},{9,5},{10,6},{11,7},{12,8},{13,9},{1... | collective-permute-start | bytes 1572872 | tf_op jit(solution)/shard_map/ppermute | solution.py:352
  11.8 0.6 collective-permute-start.2
  12.3 5.3 %collective-permute-start = (bf16[512,512]{1,0:T(8,128)(2,1)S(1)}, bf16[512,512]{1,0:T(8,128)(2,1)}, u32[]{:S(2)}, u32[]{:S(2)}) collective-permute-start(bf16[512,512]{1,0:T(8,128)(2,1)S(1)} %get-tuple-element.72), channel_id=1, source_target_pairs={{0,4},{1,5},{2,6},{3,7},{4,8},{5,9},{6,10},{7,11},{8,12},{9,13},{1... | collective-permute-start | bytes 1572872 | tf_op jit(solution)/shard_map/ppermute | solution.py:349
  17.7 1.0 %collective-permute-done.9 = bf16[512,512]{1,0:T(8,128)(2,1)S(1)} collective-permute-done((bf16[512,512]{1,0:T(8,128)(2,1)S(1)}, bf16[512,512]{1,0:T(8,128)(2,1)S(1)}, u32[]{:S(2)}, u32[]{:S(2)}) %collective-permute-start.9) | collective-permute-done | bytes 524320 | tf_op jit(solution)/shard_map/ppermute | solution.py:355
  18.7 1.3 %collective-permute-start.1 = (bf16[512,512]{1,0:T(8,128)(2,1)S(1)}, bf16[512,512]{1,0:T(8,128)(2,1)S(1)}, u32[]{:S(2)}, u32[]{:S(2)}) collective-permute-start(bf16[512,512]{1,0:T(8,128)(2,1)S(1)} %get-tuple-element.73), channel_id=1, source_target_pairs={{4,0},{5,1},{6,2},{7,3},{8,4},{9,5},{10,6},{11,7},{12,8},{13,9},{1... | collective-permute-start | bytes 1572872 | tf_op jit(solution)/shard_map/ppermute | solution.py:352
  20.0 1.8 %collective-permute-done.7.refs_2_ = bf16[512,512]{1,0:T(8,128)(2,1)} collective-permute-done((bf16[512,512]{1,0:T(8,128)(2,1)S(1)}, bf16[512,512]{1,0:T(8,128)(2,1)}, u32[]{:S(2)}, u32[]{:S(2)}) %collective-permute-start.7) | collective-permute-done | bytes 524320 | tf_op jit(solution)/shard_map/ppermute | solution.py:349
  21.7 5.2 %collective-permute-done.8.refs_2_ = bf16[512,512]{1,0:T(8,128)(2,1)S(1)} collective-permute-done((bf16[512,512]{1,0:T(8,128)(2,1)S(1)}, bf16[512,512]{1,0:T(8,128)(2,1)S(1)}, u32[]{:S(2)}, u32[]{:S(2)}) %collective-permute-start.8) | collective-permute-done | bytes 524320 | tf_op jit(solution)/shard_map/ppermute | solution.py:352
  27.0 1.6 %collective-permute-start.10 = (bf16[512,512]{1,0:T(8,128)(2,1)S(1)}, bf16[512,512]{1,0:T(8,128)(2,1)S(1)}, u32[]{:S(2)}, u32[]{:S(2)}) collective-permute-start(bf16[512,512]{1,0:T(8,128)(2,1)S(1)} %broadcast_select_fusion.2), channel_id=1, source_target_pairs={{0,2},{1,3},{2,0},{3,1},{4,6},{5,7},{6,4},{7,5},{8,10},{9,11},{10,... | collective-permute-start | bytes 1572872 | tf_op jit(solution)/shard_map/ppermute | solution.py:355
  28.6 3.5 %collective-permute-start.11 = (bf16[512,512]{1,0:T(8,128)(2,1)}, bf16[512,512]{1,0:T(8,128)(2,1)}, u32[]{:S(2)}, u32[]{:S(2)}) collective-permute-start(bf16[512,512]{1,0:T(8,128)(2,1)} %collective-permute-done.7.refs_2_), channel_id=1, source_target_pairs={{0,4},{1,5},{2,6},{3,7},{4,8},{5,9},{6,10},{7,11},{8,12},{9,13},{1... | collective-permute-start | bytes 1572872 | tf_op jit(solution)/shard_map/ppermute | solution.py:349
  32.1 1.3 %collective-permute-start.12 = (bf16[512,512]{1,0:T(8,128)(2,1)S(1)}, bf16[512,512]{1,0:T(8,128)(2,1)S(1)}, u32[]{:S(2)}, u32[]{:S(2)}) collective-permute-start(bf16[512,512]{1,0:T(8,128)(2,1)S(1)} %collective-permute-done.8.refs_2_), channel_id=1, source_target_pairs={{4,0},{5,1},{6,2},{7,3},{8,4},{9,5},{10,6},{11,7},{12,8},{13,9},{1... | collective-permute-start | bytes 1572872 | tf_op jit(solution)/shard_map/ppermute | solution.py:352
  33.4 4.8 %collective-permute-done.1.refs_6_ = bf16[512,512]{1,0:T(8,128)(2,1)S(1)} collective-permute-done((bf16[512,512]{1,0:T(8,128)(2,1)S(1)}, bf16[512,512]{1,0:T(8,128)(2,1)S(1)}, u32[]{:S(2)}, u32[]{:S(2)}) %collective-permute-start.1) | collective-permute-done | bytes 524320 | tf_op jit(solution)/shard_map/ppermute | solution.py:352
  38.2 3.5 %collective-permute-start.4 = (bf16[512,512]{1,0:T(8,128)(2,1)}, bf16[512,512]{1,0:T(8,128)(2,1)}, u32[]{:S(2)}, u32[]{:S(2)}) collective-permute-start(bf16[512,512]{1,0:T(8,128)(2,1)} %collective-permute-done.refs_2_), channel_id=1, source_target_pairs={{0,4},{1,5},{2,6},{3,7},{4,8},{5,9},{6,10},{7,11},{8,12},{9,13},{1... | collective-permute-start | bytes 1572872 | tf_op jit(solution)/shard_map/ppermute | solution.py:349
  41.7 0.9 %broadcast_select_fusion.6 = bf16[512,512]{1,0:T(8,128)(2,1)} fusion(bf16[512,512]{1,0:T(8,128)(2,1)S(1)} %collective-permute-done.1.refs_6_, bf16[512,512]{1,0:T(8,128)(2,1)} %collective-permute-done.refs_2_, pred[]{:T(512)S(6)} %eq.8), kind=kLoop, calls=%fused_computation.12 | loop fusion | flops 262144 | bytes 1572865 | tf_op jit(solution)/shard_map/jit(_where)/select_n | solution.py:389
  42.5 1.5 %collective-permute-start.3 = (bf16[512,512]{1,0:T(8,128)(2,1)}, bf16[512,512]{1,0:T(8,128)(2,1)}, u32[]{:S(2)}, u32[]{:S(2)}) collective-permute-start(bf16[512,512]{1,0:T(8,128)(2,1)} %broadcast_select_fusion.6), channel_id=1, source_target_pairs={{0,2},{1,3},{2,0},{3,1},{4,6},{5,7},{6,4},{7,5},{8,10},{9,11},{10,... | collective-permute-start | bytes 1572872 | tf_op jit(solution)/shard_map/ppermute | solution.py:355
  44.1 0.8 copy-done.16
  44.9 1.3 %collective-permute-start.5 = (bf16[512,512]{1,0:T(8,128)(2,1)S(1)}, bf16[512,512]{1,0:T(8,128)(2,1)S(1)}, u32[]{:S(2)}, u32[]{:S(2)}) collective-permute-start(bf16[512,512]{1,0:T(8,128)(2,1)S(1)} %collective-permute-done.1.refs_6_), channel_id=1, source_target_pairs={{4,0},{5,1},{6,2},{7,3},{8,4},{9,5},{10,6},{11,7},{12,8},{13,9},{1... | collective-permute-start | bytes 1572872 | tf_op jit(solution)/shard_map/ppermute | solution.py:352
  46.2 3.2 %collective-permute-done.12.refs_3_ = bf16[512,512]{1,0:T(8,128)(2,1)S(1)} collective-permute-done((bf16[512,512]{1,0:T(8,128)(2,1)S(1)}, bf16[512,512]{1,0:T(8,128)(2,1)S(1)}, u32[]{:S(2)}, u32[]{:S(2)}) %collective-permute-start.12) | collective-permute-done | bytes 524320 | tf_op jit(solution)/shard_map/ppermute | solution.py:352
  49.4 1.9 %broadcast_select_fusion.9 = (bf16[512,512]{1,0:T(8,128)(2,1)S(1)}, bf16[512,512]{1,0:T(8,128)(2,1)S(1)}, bf16[512,512]{1,0:T(8,128)(2,1)S(1)}, bf16[512,512]{1,0:T(8,128)(2,1)S(1)}) fusion(pred[]{:T(512)S(6)} %eq.7, bf16[256,512]{1,0:T(8,128)(2,1)} %copy-done.12, bf16[256,512]{1,0:T(8,128)(2,1)} %copy-done.11, bf16[512,512]{1,0:T(8,128)(2,1)} %copy-done.16, ...), kind=kLoop, calls=%fused_computation.15 | loop fusion | flops 3145728 | bytes 4194306 | tf_op jit(solution)/shard_map/jit(_where)/select_n | solution.py:407
  51.5 1.6 %collective-permute-done.3 = bf16[512,512]{1,0:T(8,128)(2,1)} collective-permute-done((bf16[512,512]{1,0:T(8,128)(2,1)}, bf16[512,512]{1,0:T(8,128)(2,1)}, u32[]{:S(2)}, u32[]{:S(2)}) %collective-permute-start.3) | collective-permute-done | bytes 524320 | tf_op jit(solution)/shard_map/ppermute | solution.py:355
  53.1 1.0 %collective-permute-done.4.refs_3_ = bf16[512,512]{1,0:T(8,128)(2,1)} collective-permute-done((bf16[512,512]{1,0:T(8,128)(2,1)}, bf16[512,512]{1,0:T(8,128)(2,1)}, u32[]{:S(2)}, u32[]{:S(2)}) %collective-permute-start.4) | collective-permute-done | bytes 524320 | tf_op jit(solution)/shard_map/ppermute | solution.py:349
  54.1 4.8 %collective-permute-done.5.refs_7_ = bf16[512,512]{1,0:T(8,128)(2,1)S(1)} collective-permute-done((bf16[512,512]{1,0:T(8,128)(2,1)S(1)}, bf16[512,512]{1,0:T(8,128)(2,1)S(1)}, u32[]{:S(2)}, u32[]{:S(2)}) %collective-permute-start.5) | collective-permute-done | bytes 524320 | tf_op jit(solution)/shard_map/ppermute | solution.py:352
  58.9 1.6 %broadcast_select_fusion.11 = (bf16[512,512]{1,0:T(8,128)(2,1)S(1)}, bf16[512,512]{1,0:T(8,128)(2,1)S(1)}, bf16[512,512]{1,0:T(8,128)(2,1)S(1)}, bf16[512,512]{1,0:T(8,128)(2,1)S(1)}) fusion(pred[]{:T(512)S(6)} %eq.7, bf16[256,512]{1,0:T(8,128)(2,1)S(1)} %copy-done.6, bf16[256,512]{1,0:T(8,128)(2,1)S(1)} %get-tuple-element.64, ...), kind=kLoop, calls=%fused_computation.17 | loop fusion | flops 3145728 | bytes 4194306 | tf_op jit(solution)/shard_map/jit(_where)/select_n | solution.py:407
  61.8 4.6 %shard_map.93 = (bf16[256,1024]{1,0:T(8,128)(2,1)}, bf16[256,1024]{1,0:T(8,128)(2,1)}, f32[4,8,256]{2,1,0:T(8,128)S(1)}) custom-call(s32[3]{0:T(128)S(1)} %pad_add_fusion.info, s32[2,8]{1,0:T(2,128)S(1)} %copy-done.4, bf16[256,1024]{1,0:T(8,128)(2,1)S(1)} %copy-done, bf16[256,1024]{1,0:T(8,128)(2,1)S(1)} %copy-done.2, bf16[256,1024]{1,0:T(8,128)(2,1)S(1)} %copy-done.3, ...), custom_call_target="tpu_custom_call" | custom-call | flops 805306368 | bytes 6291456 | tf_op jit(solution)/shard_map/pallas_call | solution.py:322
  66.4 4.6 %shard_map.94 = (bf16[256,1024]{1,0:T(8,128)(2,1)}, bf16[256,1024]{1,0:T(8,128)(2,1)}, f32[4,8,256]{2,1,0:T(8,128)S(1)}) custom-call(s32[3]{0:T(128)S(1)} %pad_add_fusion.info, s32[2,8]{1,0:T(2,128)S(1)} %copy-done.4, bf16[256,1024]{1,0:T(8,128)(2,1)S(1)} %copy-done, ...), custom_call_target="tpu_custom_call", output_to_operand_aliasing={{0}: (11, {}), {1}: (12, {})} | custom-call | flops 805306368 | bytes 6291456 | tf_op jit(solution)/shard_map/pallas_call | solution.py:322
  71.0 1.9 %collective-permute-start.17 = (f32[4,8,256]{2,1,0:T(8,128)S(1)}, f32[4,8,256]{2,1,0:T(8,128)S(1)}, u32[]{:S(2)}, u32[]{:S(2)}) collective-permute-start(f32[4,8,256]{2,1,0:T(8,128)S(1)} %get-tuple-element.45.refs_8_), channel_id=1, source_target_pairs={{8,0},{9,1},{10,2},{11,3},{12,4},{13,5},{14,6},{15,7},{0,8},{1,9},... | collective-permute-start | bytes 98312 | tf_op jit(solution)/shard_map/ppermute | solution.py:358
  72.8 1.3 %collective-permute-start.16 = (f32[4,8,256]{2,1,0:T(8,128)S(1)}, f32[4,8,256]{2,1,0:T(8,128)S(1)}, u32[]{:S(2)}, u32[]{:S(2)}) collective-permute-start(f32[4,8,256]{2,1,0:T(8,128)S(1)} %get-tuple-element.45.refs_8_), channel_id=1, source_target_pairs={{4,0},{5,1},{6,2},{7,3},{8,4},{9,5},{10,6},{11,7},{12,8},{13,9},{1... | collective-permute-start | bytes 98312 | tf_op jit(solution)/shard_map/ppermute | solution.py:358
  74.2 1.2 %collective-permute-start.15 = (f32[4,8,256]{2,1,0:T(8,128)S(1)}, f32[4,8,256]{2,1,0:T(8,128)S(1)}, u32[]{:S(2)}, u32[]{:S(2)}) collective-permute-start(f32[4,8,256]{2,1,0:T(8,128)S(1)} %get-tuple-element.45.refs_8_), channel_id=1, source_target_pairs={{2,0},{3,1},{4,2},{5,3},{6,4},{7,5},{8,6},{9,7},{10,8},{11,9},{12,... | collective-permute-start | bytes 98312 | tf_op jit(solution)/shard_map/ppermute | solution.py:358
  75.9 1.8 %shard_map.95 = (f32[8,256,768]{2,1,0:T(8,128)S(1)}, f32[8,256,768]{2,1,0:T(8,128)S(1)}) custom-call(bf16[256,1024]{1,0:T(8,128)(2,1)S(1)} %copy-done, bf16[256,1024]{1,0:T(8,128)(2,1)S(1)} %copy-done.2, bf16[256,1024]{1,0:T(8,128)(2,1)S(1)} %copy-done.3, bf16[256,1024]{1,0:T(8,128)(2,1)S(1)} %copy-done.1, ...), custom_call_target="tpu_custom_call" | custom-call | flops 1610612736 | bytes 6291456 | tf_op jit(solution)/shard_map/pallas_call | solution.py:435
  78.1 3.5 %shard_map.96 = (bf16[256,1024]{1,0:T(8,128)(2,1)}, bf16[256,1024]{1,0:T(8,128)(2,1)}) custom-call(s32[3]{0:T(128)S(1)} %pad_add_fusion.info, f32[8,256,768]{2,1,0:T(8,128)S(1)} %get-tuple-element.43.score_ref, f32[8,256,768]{2,1,0:T(8,128)S(1)} %get-tuple-element.44.grad_ref, bf16[256,1024]{1,0:T(8,128)(2,1)S(1)} %copy-done, ...), custom_call_target="tpu_custom_call" | custom-call | flops 1610612736 | bytes 6291456 | tf_op jit(solution)/shard_map/pallas_call | solution.py:322
  (53 shorter events, 2.6 us)
Async XLA Ops:
  0.6 1.4 %copy-start.1 = (bf16[256,1024]{1,0:T(8,128)(2,1)S(1)}, bf16[256,1024]{1,0:T(8,128)(2,1)}, u32[]{:S(2)}) copy-start(bf16[256,1024]{1,0:T(8,128)(2,1)} %g_ref.7) | copy-start | bytes 1572868
  0.6 1.5 %copy-start = (bf16[256,1024]{1,0:T(8,128)(2,1)S(1)}, bf16[256,1024]{1,0:T(8,128)(2,1)}, u32[]{:S(2)}) copy-start(bf16[256,1024]{1,0:T(8,128)(2,1)} %q_ref.7) | copy-start | bytes 1572868
  2.2 9.3 %copy-start.5 = (bf16[256,512]{1,0:T(8,128)(2,1)}, bf16[256,512]{1,0:T(8,128)(2,1)S(1)}, u32[]{:S(2)}) copy-start(bf16[256,512]{1,0:T(8,128)(2,1)S(1)} %get-tuple-element.74) | copy-start | bytes 786436
  2.2 9.5 %copy-start.7 = (bf16[256,512]{1,0:T(8,128)(2,1)}, bf16[256,512]{1,0:T(8,128)(2,1)S(1)}, u32[]{:S(2)}) copy-start(bf16[256,512]{1,0:T(8,128)(2,1)S(1)} %get-tuple-element.68) | copy-start | bytes 786436
  2.2 9.5 %copy-start.9 = (bf16[256,512]{1,0:T(8,128)(2,1)}, bf16[256,512]{1,0:T(8,128)(2,1)S(1)}, u32[]{:S(2)}) copy-start(bf16[256,512]{1,0:T(8,128)(2,1)S(1)} %get-tuple-element.76) | copy-start | bytes 786436
  2.3 9.5 %copy-start.13 = (bf16[256,512]{1,0:T(8,128)(2,1)}, bf16[256,512]{1,0:T(8,128)(2,1)S(1)}, u32[]{:S(2)}) copy-start(bf16[256,512]{1,0:T(8,128)(2,1)S(1)} %get-tuple-element.67) | copy-start | bytes 786436
  2.3 9.5 %copy-start.14 = (bf16[256,512]{1,0:T(8,128)(2,1)}, bf16[256,512]{1,0:T(8,128)(2,1)S(1)}, u32[]{:S(2)}) copy-start(bf16[256,512]{1,0:T(8,128)(2,1)S(1)} %get-tuple-element.77) | copy-start | bytes 786436
  2.9 15.7 %collective-permute-start.9 = (bf16[512,512]{1,0:T(8,128)(2,1)S(1)}, bf16[512,512]{1,0:T(8,128)(2,1)S(1)}, u32[]{:S(2)}, u32[]{:S(2)}) collective-permute-start(bf16[512,512]{1,0:T(8,128)(2,1)S(1)} %get-tuple-element.60), channel_id=1, source_target_pairs={{0,2},{1,3},{2,0},{3,1},{4,6},{5,7},{6,4},{7,5},{8,10},{9,11},{10,... | collective-permute-start | bytes 1572872 | tf_op jit(solution)/shard_map/ppermute | solution.py:355
  5.9 15.8 %collective-permute-start.7 = (bf16[512,512]{1,0:T(8,128)(2,1)S(1)}, bf16[512,512]{1,0:T(8,128)(2,1)}, u32[]{:S(2)}, u32[]{:S(2)}) collective-permute-start(bf16[512,512]{1,0:T(8,128)(2,1)S(1)} %get-tuple-element.61), channel_id=1, source_target_pairs={{0,4},{1,5},{2,6},{3,7},{4,8},{5,9},{6,10},{7,11},{8,12},{9,13},{1... | collective-permute-start | bytes 1572872 | tf_op jit(solution)/shard_map/ppermute | solution.py:349
  10.2 16.7 %collective-permute-start.8 = (bf16[512,512]{1,0:T(8,128)(2,1)S(1)}, bf16[512,512]{1,0:T(8,128)(2,1)S(1)}, u32[]{:S(2)}, u32[]{:S(2)}) collective-permute-start(bf16[512,512]{1,0:T(8,128)(2,1)S(1)} %get-tuple-element.62), channel_id=1, source_target_pairs={{4,0},{5,1},{6,2},{7,3},{8,4},{9,5},{10,6},{11,7},{12,8},{13,9},{1... | collective-permute-start | bytes 1572872 | tf_op jit(solution)/shard_map/ppermute | solution.py:352
  11.8 20.3 %collective-permute-start.2 = (bf16[512,512]{1,0:T(8,128)(2,1)S(1)}, bf16[512,512]{1,0:T(8,128)(2,1)}, u32[]{:S(2)}, u32[]{:S(2)}) collective-permute-start(bf16[512,512]{1,0:T(8,128)(2,1)S(1)} %get-tuple-element.71), channel_id=1, source_target_pairs={{0,2},{1,3},{2,0},{3,1},{4,6},{5,7},{6,4},{7,5},{8,10},{9,11},{10,... | collective-permute-start | bytes 1572872 | tf_op jit(solution)/shard_map/ppermute | solution.py:355
  12.3 21.1 %collective-permute-start = (bf16[512,512]{1,0:T(8,128)(2,1)S(1)}, bf16[512,512]{1,0:T(8,128)(2,1)}, u32[]{:S(2)}, u32[]{:S(2)}) collective-permute-start(bf16[512,512]{1,0:T(8,128)(2,1)S(1)} %get-tuple-element.72), channel_id=1, source_target_pairs={{0,4},{1,5},{2,6},{3,7},{4,8},{5,9},{6,10},{7,11},{8,12},{9,13},{1... | collective-permute-start | bytes 1572872 | tf_op jit(solution)/shard_map/ppermute | solution.py:349
  18.7 25.4 %copy-start.15 = (bf16[512,512]{1,0:T(8,128)(2,1)}, bf16[512,512]{1,0:T(8,128)(2,1)S(1)}, u32[]{:S(2)}) copy-start(bf16[512,512]{1,0:T(8,128)(2,1)S(1)} %collective-permute-done.9) | copy-start | bytes 1572868
  18.7 19.5 %collective-permute-start.1 = (bf16[512,512]{1,0:T(8,128)(2,1)S(1)}, bf16[512,512]{1,0:T(8,128)(2,1)S(1)}, u32[]{:S(2)}, u32[]{:S(2)}) collective-permute-start(bf16[512,512]{1,0:T(8,128)(2,1)S(1)} %get-tuple-element.73), channel_id=1, source_target_pairs={{4,0},{5,1},{6,2},{7,3},{8,4},{9,5},{10,6},{11,7},{12,8},{13,9},{1... | collective-permute-start | bytes 1572872 | tf_op jit(solution)/shard_map/ppermute | solution.py:352
  27.0 17.1 %collective-permute-start.10 = (bf16[512,512]{1,0:T(8,128)(2,1)S(1)}, bf16[512,512]{1,0:T(8,128)(2,1)S(1)}, u32[]{:S(2)}, u32[]{:S(2)}) collective-permute-start(bf16[512,512]{1,0:T(8,128)(2,1)S(1)} %broadcast_select_fusion.2), channel_id=1, source_target_pairs={{0,2},{1,3},{2,0},{3,1},{4,6},{5,7},{6,4},{7,5},{8,10},{9,11},{10,... | collective-permute-start | bytes 1572872 | tf_op jit(solution)/shard_map/ppermute | solution.py:355
  28.6 17.6 %collective-permute-start.11 = (bf16[512,512]{1,0:T(8,128)(2,1)}, bf16[512,512]{1,0:T(8,128)(2,1)}, u32[]{:S(2)}, u32[]{:S(2)}) collective-permute-start(bf16[512,512]{1,0:T(8,128)(2,1)} %collective-permute-done.7.refs_2_), channel_id=1, source_target_pairs={{0,4},{1,5},{2,6},{3,7},{4,8},{5,9},{6,10},{7,11},{8,12},{9,13},{1... | collective-permute-start | bytes 1572872 | tf_op jit(solution)/shard_map/ppermute | solution.py:349
  32.1 17.3 %collective-permute-start.12 = (bf16[512,512]{1,0:T(8,128)(2,1)S(1)}, bf16[512,512]{1,0:T(8,128)(2,1)S(1)}, u32[]{:S(2)}, u32[]{:S(2)}) collective-permute-start(bf16[512,512]{1,0:T(8,128)(2,1)S(1)} %collective-permute-done.8.refs_2_), channel_id=1, source_target_pairs={{4,0},{5,1},{6,2},{7,3},{8,4},{9,5},{10,6},{11,7},{12,8},{13,9},{1... | collective-permute-start | bytes 1572872 | tf_op jit(solution)/shard_map/ppermute | solution.py:352
  38.2 15.9 %collective-permute-start.4 = (bf16[512,512]{1,0:T(8,128)(2,1)}, bf16[512,512]{1,0:T(8,128)(2,1)}, u32[]{:S(2)}, u32[]{:S(2)}) collective-permute-start(bf16[512,512]{1,0:T(8,128)(2,1)} %collective-permute-done.refs_2_), channel_id=1, source_target_pairs={{0,4},{1,5},{2,6},{3,7},{4,8},{5,9},{6,10},{7,11},{8,12},{9,13},{1... | collective-permute-start | bytes 1572872 | tf_op jit(solution)/shard_map/ppermute | solution.py:349
  42.5 10.6 %collective-permute-start.3 = (bf16[512,512]{1,0:T(8,128)(2,1)}, bf16[512,512]{1,0:T(8,128)(2,1)}, u32[]{:S(2)}, u32[]{:S(2)}) collective-permute-start(bf16[512,512]{1,0:T(8,128)(2,1)} %broadcast_select_fusion.6), channel_id=1, source_target_pairs={{0,2},{1,3},{2,0},{3,1},{4,6},{5,7},{6,4},{7,5},{8,10},{9,11},{10,... | collective-permute-start | bytes 1572872 | tf_op jit(solution)/shard_map/ppermute | solution.py:355
  44.9 14.0 %collective-permute-start.5 = (bf16[512,512]{1,0:T(8,128)(2,1)S(1)}, bf16[512,512]{1,0:T(8,128)(2,1)S(1)}, u32[]{:S(2)}, u32[]{:S(2)}) collective-permute-start(bf16[512,512]{1,0:T(8,128)(2,1)S(1)} %collective-permute-done.1.refs_6_), channel_id=1, source_target_pairs={{4,0},{5,1},{6,2},{7,3},{8,4},{9,5},{10,6},{11,7},{12,8},{13,9},{1... | collective-permute-start | bytes 1572872 | tf_op jit(solution)/shard_map/ppermute | solution.py:352
  51.3 7.6 %copy-start.6 = (bf16[256,512]{1,0:T(8,128)(2,1)S(1)}, bf16[256,512]{1,0:T(8,128)(2,1)}, u32[]{:S(2)}) copy-start(bf16[256,512]{1,0:T(8,128)(2,1)} %copy-done.5) | copy-start | bytes 786436
  51.3 7.6 %copy-start.8 = (bf16[256,512]{1,0:T(8,128)(2,1)S(1)}, bf16[256,512]{1,0:T(8,128)(2,1)}, u32[]{:S(2)}) copy-start(bf16[256,512]{1,0:T(8,128)(2,1)} %copy-done.7) | copy-start | bytes 786436
  51.4 7.5 %copy-start.10 = (bf16[256,512]{1,0:T(8,128)(2,1)S(1)}, bf16[256,512]{1,0:T(8,128)(2,1)}, u32[]{:S(2)}) copy-start(bf16[256,512]{1,0:T(8,128)(2,1)} %copy-done.9) | copy-start | bytes 786436
  51.4 10.1 %collective-permute-start.13 = (bf16[1024,512]{1,0:T(8,128)(2,1)S(1)}, bf16[1024,512]{1,0:T(8,128)(2,1)S(1)}, u32[]{:S(2)}, u32[]{:S(2)}) collective-permute-start(bf16[1024,512]{1,0:T(8,128)(2,1)S(1)} %pad_maximum_fusion.1), channel_id=1, source_target_pairs={{0,1},{1,0},{2,3},{3,2},{4,5},{5,4},{6,7},{7,6},{8,9},{9,8},{10,11... | collective-permute-start | bytes 3145736 | tf_op jit(solution)/shard_map/ppermute | solution.py:355
  60.5 1.0 %copy-start.2 = (bf16[256,1024]{1,0:T(8,128)(2,1)S(1)}, bf16[256,1024]{1,0:T(8,128)(2,1)}, u32[]{:S(2)}) copy-start(bf16[256,1024]{1,0:T(8,128)(2,1)} %k_ref.5) | copy-start | bytes 1572868
  60.5 1.2 %copy-start.3 = (bf16[256,1024]{1,0:T(8,128)(2,1)S(1)}, bf16[256,1024]{1,0:T(8,128)(2,1)}, u32[]{:S(2)}) copy-start(bf16[256,1024]{1,0:T(8,128)(2,1)} %v_ref.5) | copy-start | bytes 1572868
  60.6 1.2 %copy-start.4 = (s32[2,8]{1,0:T(2,128)S(1)}, s32[2,8]{1,0:T(2,128)}, u32[]{:S(2)}) copy-start(s32[2,8]{1,0:T(2,128)} %kb.3) | copy-start | bytes 196
  60.6 5.7 %collective-permute-start.6 = (bf16[1024,512]{1,0:T(8,128)(2,1)S(1)}, bf16[1024,512]{1,0:T(8,128)(2,1)S(1)}, u32[]{:S(2)}, u32[]{:S(2)}) collective-permute-start(bf16[1024,512]{1,0:T(8,128)(2,1)S(1)} %pad_maximum_fusion), channel_id=1, source_target_pairs={{0,1},{1,0},{2,3},{3,2},{4,5},{5,4},{6,7},{7,6},{8,9},{9,8},{10,11... | collective-permute-start | bytes 3145736 | tf_op jit(solution)/shard_map/ppermute | solution.py:355
  71.0 6.7 %collective-permute-start.17 = (f32[4,8,256]{2,1,0:T(8,128)S(1)}, f32[4,8,256]{2,1,0:T(8,128)S(1)}, u32[]{:S(2)}, u32[]{:S(2)}) collective-permute-start(f32[4,8,256]{2,1,0:T(8,128)S(1)} %get-tuple-element.45.refs_8_), channel_id=1, source_target_pairs={{8,0},{9,1},{10,2},{11,3},{12,4},{13,5},{14,6},{15,7},{0,8},{1,9},... | collective-permute-start | bytes 98312 | tf_op jit(solution)/shard_map/ppermute | solution.py:358
  72.8 4.9 %collective-permute-start.16 = (f32[4,8,256]{2,1,0:T(8,128)S(1)}, f32[4,8,256]{2,1,0:T(8,128)S(1)}, u32[]{:S(2)}, u32[]{:S(2)}) collective-permute-start(f32[4,8,256]{2,1,0:T(8,128)S(1)} %get-tuple-element.45.refs_8_), channel_id=1, source_target_pairs={{4,0},{5,1},{6,2},{7,3},{8,4},{9,5},{10,6},{11,7},{12,8},{13,9},{1... | collective-permute-start | bytes 98312 | tf_op jit(solution)/shard_map/ppermute | solution.py:358
  74.2 3.9 %collective-permute-start.15 = (f32[4,8,256]{2,1,0:T(8,128)S(1)}, f32[4,8,256]{2,1,0:T(8,128)S(1)}, u32[]{:S(2)}, u32[]{:S(2)}) collective-permute-start(f32[4,8,256]{2,1,0:T(8,128)S(1)} %get-tuple-element.45.refs_8_), channel_id=1, source_target_pairs={{2,0},{3,1},{4,2},{5,3},{6,4},{7,5},{8,6},{9,7},{10,8},{11,9},{12,... | collective-permute-start | bytes 98312 | tf_op jit(solution)/shard_map/ppermute | solution.py:358
  75.4 2.7 %collective-permute-start.14 = (f32[4,8,256]{2,1,0:T(8,128)S(1)}, f32[4,8,256]{2,1,0:T(8,128)S(1)}, u32[]{:S(2)}, u32[]{:S(2)}) collective-permute-start(f32[4,8,256]{2,1,0:T(8,128)S(1)} %get-tuple-element.45.refs_8_), channel_id=1, source_target_pairs={{1,0},{2,1},{3,2},{4,3},{5,4},{6,5},{7,6},{8,7},{9,8},{10,9},{11,1... | collective-permute-start | bytes 98312 | tf_op jit(solution)/shard_map/ppermute | solution.py:358
  (3 other events, 2.3 us)

commit v5 on v4

--- a/solution.py
+++ b/solution.py
@@ -58,11 +58,12 @@
                 stage(units[turn - lag])
 
 
-def send_head(copies, head, first, pairs, sems):
+def send_head(copies, head, pairs, sems):
+    columns = pl.ds(head * HEAD_DIM, HEAD_DIM)
     for index, (source, target) in enumerate(pairs):
         copy = pltpu.make_async_copy(
-            source.at[:, pl.ds(head * HEAD_DIM, HEAD_DIM)],
-            target.at[:, pl.ds((first + head) * HEAD_DIM, HEAD_DIM)],
+            source.at[:, columns],
+            target.at[:, columns],
             sems.at[index, head],
         )
         copy.start()
@@ -71,7 +72,7 @@
 
 def query_kernel(hops, first, info, kb, q_ref, k_ref, v_ref, g_ref, *refs):
     behind = refs[: len(hops) + (first > 0)]
-    att_out, dq_out, stat_ref, att_ref, dq_ref, sems, bias_ref = refs[-7:]
+    att_ref, dq_ref, stat_ref, bias_ref = refs[-4:]
     heads = att_ref.shape[1] // HEAD_DIM
     base = first
     device, valid = info[0], info[1]
@@ -181,14 +182,8 @@
         ]
         query_grad = pair_product(score_grad, stack(unit, k_ref, 0))
         dq_ref[place(unit)] = (jnp.concatenate(query_grad, axis=1) * SCALE).astype(jnp.bfloat16)
-        if unit[1] == 1:
-            for head in (2 * unit[0], 2 * unit[0] + 1):
-                send_head(copies, head, first, ((att_ref, att_out), (dq_ref, dq_out)), sems)
-
-    copies = []
+
     staged(units, (products, soften, attend, finish), QUERY_LAG)
-    for copy in copies:
-        copy.wait()
 
 
 def key_stack(hops, chunks, heads, refs):
@@ -234,7 +229,8 @@
 def key_kernel(hops, chunks, info, score_ref, grad_ref, q_ref, g_ref, *refs):
     count = len(hops)
     stats = refs[chunks * count : (chunks + 1) * count + 1]
-    dk_out, dv_out, dk_ref, dv_ref, sems = refs[-5:]
+    fronts = refs[(chunks + 1) * count + 1 : (chunks + 1) * count + 1 + 2 * chunks]
+    att_out, dq_out, dk_out, dv_out, dk_ref, dv_ref, sems, front_sems = refs[-8:]
     heads = dk_ref.shape[1] // HEAD_DIM
     device, valid, devices = info[0], info[1], info[2]
     flags = [ref[3] for ref in stats]
@@ -302,38 +298,64 @@
         dv_ref[rows, columns] = jnp.where(key_ok, value_grad, 0.0).astype(jnp.bfloat16)
         if unit[1] == 1:
             for head in (2 * unit[0], 2 * unit[0] + 1):
-                send_head(copies, head, 0, ((dk_ref, dk_out), (dv_ref, dv_out)), sems)
+                send_head(copies, head, ((dk_ref, dk_out), (dv_ref, dv_out)), sems)
 
     copies = []
+    for chunk in range(chunks):
+        width = dk_ref.shape[1] // chunks
+        for index, target in enumerate((att_out, dq_out)):
+            copy = pltpu.make_async_copy(
+                fronts[2 * chunk + index],
+                target.at[:, pl.ds(chunk * width, width)],
+                front_sems.at[index, chunk],
+            )
+            copy.start()
+            copies.append(copy)
     staged(units, (soften, finish), KEY_LAG)
     for copy in copies:
         copy.wait()
 
 
-def call(kernel, heads, scalars, arrays, previous, out_shapes, scratch, flops):
-    width = heads * HEAD_DIM
-    in_specs = [pl.BlockSpec(memory_space=pltpu.SMEM) for _ in scalars]
-    in_specs += [pl.BlockSpec(memory_space=pltpu.VMEM) for _ in arrays]
-    in_specs += [pl.BlockSpec(memory_space=pl.ANY) for _ in previous]
-    before = len(scalars) + len(arrays)
-    out_specs = [pl.BlockSpec(memory_space=pl.ANY)] * 2
-    out_specs += [pl.BlockSpec(memory_space=pltpu.VMEM)] * (len(out_shapes) - 2)
-    rows = out_shapes[0].shape[0]
+def mix_kernel(first, info, q_ref, k_ref, v_ref, g_ref, one_ref, two_ref, out_ref, key_ref, query_ref):
+    device = info[0]
+    rows, width = q_ref.shape[0], one_ref.shape[1]
+    columns = slice(first * HEAD_DIM, first * HEAD_DIM + width)
+    side, core = (device >> 1) & 1, device & 1
+
+    @pl.when(side == 0)
+    def _():
+        key_ref[...] = two_ref[...]
+        query_ref[...] = one_ref[...]
+
+    @pl.when(side == 1)
+    def _():
+        key_ref[...] = one_ref[...]
+        query_ref[...] = two_ref[...]
+
+    @pl.when(core == 0)
+    def _():
+        out_ref[:rows] = k_ref[:, columns]
+        out_ref[rows : 2 * rows] = v_ref[:, columns]
+        out_ref[2 * rows :] = query_ref[...]
+
+    @pl.when(core == 1)
+    def _():
+        out_ref[: 2 * rows] = key_ref[...]
+        out_ref[2 * rows : 3 * rows] = q_ref[:, columns]
+        out_ref[3 * rows :] = g_ref[:, columns]
+
+
+def call(kernel, scalars, arrays, out_shapes, scratch=(), flops=0, to_hbm=False):
+    vmem = pl.BlockSpec(memory_space=pltpu.VMEM)
     return pl.pallas_call(
         kernel,
-        in_specs=in_specs,
-        out_specs=out_specs,
+        in_specs=[pl.BlockSpec(memory_space=pltpu.SMEM)] * len(scalars) + [vmem] * len(arrays),
+        out_specs=[pl.BlockSpec(memory_space=pl.ANY) if to_hbm else vmem] * len(out_shapes),
         out_shape=out_shapes,
-        scratch_shapes=[
-            pltpu.VMEM((rows, width), jnp.bfloat16),
-            pltpu.VMEM((rows, width), jnp.bfloat16),
-            pltpu.SemaphoreType.DMA((2, heads)),
-        ]
-        + scratch,
-        input_output_aliases={before + index: index for index in range(len(previous))},
+        scratch_shapes=list(scratch),
         cost_estimate=pl.CostEstimate(flops=flops, bytes_accessed=6 << 20, transcendentals=0),
         compiler_params=pltpu.CompilerParams(vmem_limit_bytes=16 << 20),
-    )(*scalars, *arrays, *previous)
+    )(*scalars, *arrays)
 
 
 def local(queries, keys, values, out_grad, key_blocks, path_length):
@@ -381,6 +403,8 @@
     full = jax.ShapeDtypeStruct((rows_dev, columns), jnp.bfloat16)
     stat_shape = jax.ShapeDtypeStruct((4, max(head_count, LEVELS), rows_dev), jnp.float32)
     pieces = 2 + len(hops)
+    part = jax.ShapeDtypeStruct((rows_dev, width), jnp.bfloat16)
+    raw_shape = jax.ShapeDtypeStruct((head_count, rows_dev, pieces * BLOCK), jnp.float32)
     flops = heads * 2 * pieces * 4 * 2 * BLOCK**3
 
     middle = []
@@ -399,18 +423,17 @@
     for chunk in range(CHUNKS):
         (key_pack, query_pack), (side_1, side_2, keys_by, queries_by) = packs[chunk], middle[chunk]
         side_2, keys_by[8], queries_by[8] = lax.optimization_barrier((side_2, keys_by[8], queries_by[8]))
-        keys_by[2] = jnp.where(side == 0, side_2, side_1)
-        queries_by[2] = jnp.where(side == 0, side_1, side_2)
-        neighbour = swap(
-            jnp.concatenate(
-                [
-                    jnp.where(core == 0, key_pack, keys_by[2]),
-                    jnp.where(core == 0, queries_by[2], query_pack),
-                ],
-                axis=0,
+        packed, keys_by[2], queries_by[2] = call(
+            functools.partial(mix_kernel, chunk * heads),
+            (info,),
+            own + (side_1, side_2),
+            (
+                jax.ShapeDtypeStruct((4 * rows_dev, width), jnp.bfloat16),
+                jax.ShapeDtypeStruct((2 * rows_dev, width), jnp.bfloat16),
+                jax.ShapeDtypeStruct((2 * rows_dev, width), jnp.bfloat16),
             ),
-            1,
-        )
+        )
+        neighbour = swap(packed, 1)
         moved.append(
             (
                 [neighbour] + [keys_by[hop] for hop in hops[1:]],
@@ -419,38 +442,33 @@
         )
         att, dq, stat = call(
             functools.partial(query_kernel, hops, chunk * heads),
-            heads,
             (info, key_blocks),
             own + tuple(moved[chunk][0]) + tuple(stats[-1:]),
-            front,
-            (full, full, stat_shape),
+            (part, part, stat_shape),
             [pltpu.VMEM((2, BLOCK, pieces * BLOCK), jnp.float32)],
             flops,
         )
-        front = (att, dq)
+        front += (att, dq)
         stats.append(stat)
-    stats = [stat] + [back_round(stat, hop) for hop in hops]
+    stats = (stat,) + tuple(back_round(stat, hop) for hop in hops)
     ahead = sum((tuple(pair[1]) for pair in moved), ())
-    raw_shape = jax.ShapeDtypeStruct((head_count, rows_dev, pieces * BLOCK), jnp.float32)
-    raw = pl.pallas_call(
-        functools.partial(product_kernel, hops, CHUNKS),
-        in_specs=[pl.BlockSpec(memory_space=pltpu.VMEM)] * (len(own) + len(ahead)),
-        out_specs=[pl.BlockSpec(memory_space=pltpu.VMEM)] * 2,
-        out_shape=(raw_shape, raw_shape),
-        cost_estimate=pl.CostEstimate(flops=2 * flops, bytes_accessed=6 << 20, transcendentals=0),
-        compiler_params=pltpu.CompilerParams(vmem_limit_bytes=16 << 20),
-    )(*own, *ahead)
-    back = call(
+    raw = call(
+        functools.partial(product_kernel, hops, CHUNKS), (), own + ahead, (raw_shape, raw_shape), (), 2 * flops
+    )
+    return call(
         functools.partial(key_kernel, hops, CHUNKS),
-        head_count,
         (info,),
-        tuple(raw) + (queries, out_grad) + ahead + tuple(stats),
-        (),
-        (full, full),
-        [],
+        tuple(raw) + (queries, out_grad) + ahead + stats + front,
+        (full,) * 4,
+        [
+            pltpu.VMEM((rows_dev, columns), jnp.bfloat16),
+            pltpu.VMEM((rows_dev, columns), jnp.bfloat16),
+            pltpu.SemaphoreType.DMA((2, head_count)),
+            pltpu.SemaphoreType.DMA((2, CHUNKS)),
+        ],
         2 * flops,
+        to_hbm=True,
     )
-    return (front[0], front[1], back[0], back[1])
 
 
 def solution(mesh):

time: 82.3 us -> 78.8 us (0.957)
  waiting for transfers between devices: 23.7 us -> 29.2 us
  other arithmetic: 5.08 us -> 0.72 us
  starting transfers between devices: 33.5 us -> 30.2 us
    select_n x2 -> x0, other arithmetic: 3.53 us -> none  [local(): jnp.where(core == 0, key_pack, keys_by[2])]
    ppermute x4, waiting for transfers between devices: 2.79 us -> 6.23 us  [up(): lax.ppermute(value, 'ctx', [(at, at + steps) for at in range(devices - st...]
    ppermute x6, waiting for transfers between devices: 2.55 us -> 4.65 us  [swap(): return lax.ppermute(value, 'ctx', [(at, at ^ bit) for at in range(devices)])]
    ppermute x6, starting transfers between devices: 6.84 us -> 4.89 us  [swap(): return lax.ppermute(value, 'ctx', [(at, at ^ bit) for at in range(devices)])]
    unnamed x34 -> x10, local copies, waits for them, and re-layouts: 1.63 us -> 0.03 us
    ppermute x4, starting transfers between devices: 16.6 us -> 15 us  [up(): lax.ppermute(value, 'ctx', [(at, at + steps) for at in range(devices - st...]
    slice x1, local copies, waits for them, and re-layouts: 0.07 us -> 1.26 us  [local(): queries[:, cut]]
    pallas_call x4 -> x6, Pallas kernels: 14.5 us -> 13.9 us  [call(): pl.pallas_call(kernel, in_specs=[pl.BlockSpec(memory_space=pltpu.SMEM)] *...]
  transfers between devices with their start and end apart: 18 -> 18, of which waited for: 9 -> 11; matrix products, arithmetic and copies ran while one was open for 6% -> 1% of each run, Pallas kernels for 8% -> 9%
where the time goes in v5:
time: 78.8 us; the launch traced here: 78.4 us
  starting transfers between devices  30.2 us (38%)
  waiting for transfers between devices  29.2 us (37%)
  Pallas kernels  13.9 us (18%)
  local copies, waits for them, and re-layouts  2.69 us (3%)
  between operations  1.71 us (2%)
    ppermute x4, waiting for transfers between devices, down(): lax.ppermute(value, 'ctx', [(at + steps, at) for at in range(devices - st...  17.5 us
    ppermute x4, starting transfers between devices, up(): lax.ppermute(value, 'ctx', [(at, at + steps) for at in range(devices - st...  15 us
    pallas_call x6, Pallas kernels, call(): pl.pallas_call(kernel, in_specs=[pl.BlockSpec(memory_space=pltpu.SMEM)] *...  13.9 us
    ppermute x4, waiting for transfers between devices, up(): lax.ppermute(value, 'ctx', [(at, at + steps) for at in range(devices - st...  6.23 us
    ppermute x4, starting transfers between devices, back_round(): lax.ppermute(value, 'ctx', [((at + steps) % devices, at) for at in range(...  5.16 us
    ppermute x4, starting transfers between devices, down(): lax.ppermute(value, 'ctx', [(at + steps, at) for at in range(devices - st...  5.15 us
    ppermute x6, starting transfers between devices, swap(): return lax.ppermute(value, 'ctx', [(at, at ^ bit) for at in range(devices)])  4.89 us
    ppermute x6, waiting for transfers between devices, swap(): return lax.ppermute(value, 'ctx', [(at, at ^ bit) for at in range(devices)])  4.65 us
  transfers between devices with their start and end apart: 18, of which 11 were waited for; matrix products, arithmetic and copies ran while one was open for 1% of the time, Pallas kernels for 9%

profile of v5, /device:TPU:0, one launch (start us, length us, event | category | flops | bytes accessed | tf_op | source)
XLA Modules:
  0.0 78.4 jit_solution(5536677171652347547)
XLA Ops:
  0.7 1.4 %fusion.2 = (bf16[256,512]{1,0:T(8,128)(2,1)S(1)}, bf16[256,512]{1,0:T(8,128)(2,1)S(1)}, bf16[256,512]{1,0:T(8,128)(2,1)S(1)}, bf16[256,512]{1,0:T(8,128)(2,1)S(1)}) fusion(bf16[256,1024]{1,0:T(8,128)(2,1)} %k_ref.9, bf16[256,1024]{1,0:T(8,128)(2,1)} %v_ref.9), kind=kLoop, calls=%fused_computation.11 | loop fusion | bytes 2097152 | tf_op jit(solution)/shard_map/slice | solution.py:389
  2.1 1.3 %fusion = (bf16[256,512]{1,0:T(8,128)(2,1)S(1)}, bf16[256,512]{1,0:T(8,128)(2,1)S(1)}, bf16[256,512]{1,0:T(8,128)(2,1)S(1)}, bf16[256,512]{1,0:T(8,128)(2,1)S(1)}) fusion(bf16[256,1024]{1,0:T(8,128)(2,1)} %q_ref.11, bf16[256,1024]{1,0:T(8,128)(2,1)} %g_ref.11), kind=kLoop, calls=%fused_computation.9 | loop fusion | bytes 2097152 | tf_op jit(solution)/shard_map/slice | solution.py:390
  3.6 3.0 %collective-permute-start.2 = (bf16[512,512]{1,0:T(8,128)(2,1)S(1)}, bf16[512,512]{1,0:T(8,128)(2,1)S(1)}, u32[]{:S(2)}, u32[]{:S(2)}) collective-permute-start(bf16[512,512]{1,0:T(8,128)(2,1)S(1)} %get-tuple-element.67), channel_id=1, source_target_pairs={{0,2},{1,3},{2,0},{3,1},{4,6},{5,7},{6,4},{7,5},{8,10},{9,11},{10,... | collective-permute-start | bytes 1572872 | tf_op jit(solution)/shard_map/ppermute | solution.py:377
  6.7 3.5 %collective-permute-start = (bf16[512,512]{1,0:T(8,128)(2,1)S(1)}, bf16[512,512]{1,0:T(8,128)(2,1)S(1)}, u32[]{:S(2)}, u32[]{:S(2)}) collective-permute-start(bf16[512,512]{1,0:T(8,128)(2,1)S(1)} %get-tuple-element.68), channel_id=1, source_target_pairs={{0,4},{1,5},{2,6},{3,7},{4,8},{5,9},{6,10},{7,11},{8,12},{9,13},{1... | collective-permute-start | bytes 1572872 | tf_op jit(solution)/shard_map/ppermute | solution.py:371
  10.2 1.3 %collective-permute-start.1 = (bf16[512,512]{1,0:T(8,128)(2,1)S(1)}, bf16[512,512]{1,0:T(8,128)(2,1)S(1)}, u32[]{:S(2)}, u32[]{:S(2)}) collective-permute-start(bf16[512,512]{1,0:T(8,128)(2,1)S(1)} %get-tuple-element.69), channel_id=1, source_target_pairs={{4,0},{5,1},{6,2},{7,3},{8,4},{9,5},{10,6},{11,7},{12,8},{13,9},{1... | collective-permute-start | bytes 1572872 | tf_op jit(solution)/shard_map/ppermute | solution.py:374
  11.7 0.6 collective-permute-start.9
  12.3 4.6 %collective-permute-start.7 = (bf16[512,512]{1,0:T(8,128)(2,1)S(1)}, bf16[512,512]{1,0:T(8,128)(2,1)S(1)}, u32[]{:S(2)}, u32[]{:S(2)}) collective-permute-start(bf16[512,512]{1,0:T(8,128)(2,1)S(1)} %get-tuple-element.57), channel_id=1, source_target_pairs={{0,4},{1,5},{2,6},{3,7},{4,8},{5,9},{6,10},{7,11},{8,12},{9,13},{1... | collective-permute-start | bytes 1572872 | tf_op jit(solution)/shard_map/ppermute | solution.py:371
  16.9 2.5 %collective-permute-done.2.one_ref = bf16[512,512]{1,0:T(8,128)(2,1)S(1)} collective-permute-done((bf16[512,512]{1,0:T(8,128)(2,1)S(1)}, bf16[512,512]{1,0:T(8,128)(2,1)S(1)}, u32[]{:S(2)}, u32[]{:S(2)}) %collective-permute-start.2) | collective-permute-done | bytes 524320 | tf_op jit(solution)/shard_map/ppermute | solution.py:377
  19.4 1.3 %collective-permute-start.8 = (bf16[512,512]{1,0:T(8,128)(2,1)S(1)}, bf16[512,512]{1,0:T(8,128)(2,1)S(1)}, u32[]{:S(2)}, u32[]{:S(2)}) collective-permute-start(bf16[512,512]{1,0:T(8,128)(2,1)S(1)} %get-tuple-element.58), channel_id=1, source_target_pairs={{4,0},{5,1},{6,2},{7,3},{8,4},{9,5},{10,6},{11,7},{12,8},{13,9},{1... | collective-permute-start | bytes 1572872 | tf_op jit(solution)/shard_map/ppermute | solution.py:374
  20.7 1.8 %collective-permute-done.refs_2_ = bf16[512,512]{1,0:T(8,128)(2,1)S(1)} collective-permute-done((bf16[512,512]{1,0:T(8,128)(2,1)S(1)}, bf16[512,512]{1,0:T(8,128)(2,1)S(1)}, u32[]{:S(2)}, u32[]{:S(2)}) %collective-permute-start) | collective-permute-done | bytes 524320 | tf_op jit(solution)/shard_map/ppermute | solution.py:371
  22.5 4.4 %collective-permute-done.1.refs_2_ = bf16[512,512]{1,0:T(8,128)(2,1)S(1)} collective-permute-done((bf16[512,512]{1,0:T(8,128)(2,1)S(1)}, bf16[512,512]{1,0:T(8,128)(2,1)S(1)}, u32[]{:S(2)}, u32[]{:S(2)}) %collective-permute-start.1) | collective-permute-done | bytes 524320 | tf_op jit(solution)/shard_map/ppermute | solution.py:374
  27.6 3.5 %collective-permute-start.4 = (bf16[512,512]{1,0:T(8,128)(2,1)S(1)}, bf16[512,512]{1,0:T(8,128)(2,1)S(1)}, u32[]{:S(2)}, u32[]{:S(2)}) collective-permute-start(bf16[512,512]{1,0:T(8,128)(2,1)S(1)} %collective-permute-done.refs_2_), channel_id=1, source_target_pairs={{0,4},{1,5},{2,6},{3,7},{4,8},{5,9},{6,10},{7,11},{8,12},{9,13},{1... | collective-permute-start | bytes 1572872 | tf_op jit(solution)/shard_map/ppermute | solution.py:371
  31.1 1.3 %collective-permute-start.5 = (bf16[512,512]{1,0:T(8,128)(2,1)S(1)}, bf16[512,512]{1,0:T(8,128)(2,1)S(1)}, u32[]{:S(2)}, u32[]{:S(2)}) collective-permute-start(bf16[512,512]{1,0:T(8,128)(2,1)S(1)} %collective-permute-done.1.refs_2_), channel_id=1, source_target_pairs={{4,0},{5,1},{6,2},{7,3},{8,4},{9,5},{10,6},{11,7},{12,8},{13,9},{1... | collective-permute-start | bytes 1572872 | tf_op jit(solution)/shard_map/ppermute | solution.py:374
  32.4 1.4 %collective-permute-done.7.refs_2_ = bf16[512,512]{1,0:T(8,128)(2,1)S(1)} collective-permute-done((bf16[512,512]{1,0:T(8,128)(2,1)S(1)}, bf16[512,512]{1,0:T(8,128)(2,1)S(1)}, u32[]{:S(2)}, u32[]{:S(2)}) %collective-permute-start.7) | collective-permute-done | bytes 524320 | tf_op jit(solution)/shard_map/ppermute | solution.py:371
  33.7 4.4 %collective-permute-done.8.refs_6_ = bf16[512,512]{1,0:T(8,128)(2,1)S(1)} collective-permute-done((bf16[512,512]{1,0:T(8,128)(2,1)S(1)}, bf16[512,512]{1,0:T(8,128)(2,1)S(1)}, u32[]{:S(2)}, u32[]{:S(2)}) %collective-permute-start.8) | collective-permute-done | bytes 524320 | tf_op jit(solution)/shard_map/ppermute | solution.py:374
  38.2 3.5 %collective-permute-start.11 = (bf16[512,512]{1,0:T(8,128)(2,1)S(1)}, bf16[512,512]{1,0:T(8,128)(2,1)S(1)}, u32[]{:S(2)}, u32[]{:S(2)}) collective-permute-start(bf16[512,512]{1,0:T(8,128)(2,1)S(1)} %collective-permute-done.7.refs_2_), channel_id=1, source_target_pairs={{0,4},{1,5},{2,6},{3,7},{4,8},{5,9},{6,10},{7,11},{8,12},{9,13},{1... | collective-permute-start | bytes 1572872 | tf_op jit(solution)/shard_map/ppermute | solution.py:371
  42.3 1.3 %collective-permute-start.12 = (bf16[512,512]{1,0:T(8,128)(2,1)S(1)}, bf16[512,512]{1,0:T(8,128)(2,1)S(1)}, u32[]{:S(2)}, u32[]{:S(2)}) collective-permute-start(bf16[512,512]{1,0:T(8,128)(2,1)S(1)} %collective-permute-done.8.refs_6_), channel_id=1, source_target_pairs={{4,0},{5,1},{6,2},{7,3},{8,4},{9,5},{10,6},{11,7},{12,8},{13,9},{1... | collective-permute-start | bytes 1572872 | tf_op jit(solution)/shard_map/ppermute | solution.py:374
  44.3 0.7 collective-permute-done.4.refs_3_
  45.0 4.4 %collective-permute-done.5.refs_3_ = bf16[512,512]{1,0:T(8,128)(2,1)S(1)} collective-permute-done((bf16[512,512]{1,0:T(8,128)(2,1)S(1)}, bf16[512,512]{1,0:T(8,128)(2,1)S(1)}, u32[]{:S(2)}, u32[]{:S(2)}) %collective-permute-start.5) | collective-permute-done | bytes 524320 | tf_op jit(solution)/shard_map/ppermute | solution.py:374
  49.4 0.7 shard_map.93
  50.2 2.1 %collective-permute-done.10.two_ref = bf16[512,512]{1,0:T(8,128)(2,1)S(1)} collective-permute-done((bf16[512,512]{1,0:T(8,128)(2,1)S(1)}, bf16[512,512]{1,0:T(8,128)(2,1)S(1)}, u32[]{:S(2)}, u32[]{:S(2)}) %collective-permute-start.10) | collective-permute-done | bytes 524320 | tf_op jit(solution)/shard_map/ppermute | solution.py:377
  52.3 2.4 %collective-permute-done.11.refs_3_ = bf16[512,512]{1,0:T(8,128)(2,1)S(1)} collective-permute-done((bf16[512,512]{1,0:T(8,128)(2,1)S(1)}, bf16[512,512]{1,0:T(8,128)(2,1)S(1)}, u32[]{:S(2)}, u32[]{:S(2)}) %collective-permute-start.11) | collective-permute-done | bytes 524320 | tf_op jit(solution)/shard_map/ppermute | solution.py:371
  54.7 4.1 %collective-permute-done.12.refs_7_ = bf16[512,512]{1,0:T(8,128)(2,1)S(1)} collective-permute-done((bf16[512,512]{1,0:T(8,128)(2,1)S(1)}, bf16[512,512]{1,0:T(8,128)(2,1)S(1)}, u32[]{:S(2)}, u32[]{:S(2)}) %collective-permute-start.12) | collective-permute-done | bytes 524320 | tf_op jit(solution)/shard_map/ppermute | solution.py:374
  58.9 0.7 shard_map.94
  59.7 3.5 %shard_map.96 = (bf16[256,512]{1,0:T(8,128)(2,1)S(1)}, bf16[256,512]{1,0:T(8,128)(2,1)S(1)}, f32[4,8,256]{2,1,0:T(8,128)S(1)}) custom-call(s32[3]{0:T(128)S(1)} %pad_add_fusion.info, s32[2,8]{1,0:T(2,128)S(1)} %copy-done.4, bf16[256,1024]{1,0:T(8,128)(2,1)S(1)} %copy-done, bf16[256,1024]{1,0:T(8,128)(2,1)S(1)} %copy-done.2, bf16[256,1024]{1,0:T(8,128)(2,1)S(1)} %copy-done.3, ...), custom_call_target="tpu_custom_call" | custom-call | flops 805306368 | bytes 6291456 | tf_op jit(solution)/shard_map/pallas_call | solution.py:350
  63.2 3.4 %shard_map.97 = (bf16[256,512]{1,0:T(8,128)(2,1)S(1)}, bf16[256,512]{1,0:T(8,128)(2,1)S(1)}, f32[4,8,256]{2,1,0:T(8,128)S(1)}) custom-call(s32[3]{0:T(128)S(1)} %pad_add_fusion.info, s32[2,8]{1,0:T(2,128)S(1)} %copy-done.4, bf16[256,1024]{1,0:T(8,128)(2,1)S(1)} %copy-done, bf16[256,1024]{1,0:T(8,128)(2,1)S(1)} %copy-done.2, bf16[256,1024]{1,0:T(8,128)(2,1)S(1)} %copy-done.3, ...), custom_call_target="tpu_custom_call" | custom-call | flops 805306368 | bytes 6291456 | tf_op jit(solution)/shard_map/pallas_call | solution.py:350
  66.6 2.6 %collective-permute-start.17 = (f32[4,8,256]{2,1,0:T(8,128)S(1)}, f32[4,8,256]{2,1,0:T(8,128)S(1)}, u32[]{:S(2)}, u32[]{:S(2)}) collective-permute-start(f32[4,8,256]{2,1,0:T(8,128)S(1)} %get-tuple-element.51.refs_8_), channel_id=1, source_target_pairs={{8,0},{9,1},{10,2},{11,3},{12,4},{13,5},{14,6},{15,7},{0,8},{1,9},... | collective-permute-start | bytes 98312 | tf_op jit(solution)/shard_map/ppermute | solution.py:380
  69.2 1.3 %collective-permute-start.16 = (f32[4,8,256]{2,1,0:T(8,128)S(1)}, f32[4,8,256]{2,1,0:T(8,128)S(1)}, u32[]{:S(2)}, u32[]{:S(2)}) collective-permute-start(f32[4,8,256]{2,1,0:T(8,128)S(1)} %get-tuple-element.51.refs_8_), channel_id=1, source_target_pairs={{4,0},{5,1},{6,2},{7,3},{8,4},{9,5},{10,6},{11,7},{12,8},{13,9},{1... | collective-permute-start | bytes 98312 | tf_op jit(solution)/shard_map/ppermute | solution.py:380
  71.0 0.8 collective-permute-start.14
  71.8 1.8 %shard_map.95 = (f32[8,256,768]{2,1,0:T(8,128)S(1)}, f32[8,256,768]{2,1,0:T(8,128)S(1)}) custom-call(bf16[256,1024]{1,0:T(8,128)(2,1)S(1)} %copy-done, bf16[256,1024]{1,0:T(8,128)(2,1)S(1)} %copy-done.2, bf16[256,1024]{1,0:T(8,128)(2,1)S(1)} %copy-done.3, bf16[256,1024]{1,0:T(8,128)(2,1)S(1)} %copy-done.1, ...), custom_call_target="tpu_custom_call" | custom-call | flops 1610612736 | bytes 6291456 | tf_op jit(solution)/shard_map/pallas_call | solution.py:350
  73.6 0.9 %collective-permute-done.15.refs_10_ = f32[4,8,256]{2,1,0:T(8,128)S(1)} collective-permute-done((f32[4,8,256]{2,1,0:T(8,128)S(1)}, f32[4,8,256]{2,1,0:T(8,128)S(1)}, u32[]{:S(2)}, u32[]{:S(2)}) %collective-permute-start.15) | collective-permute-done | bytes 32800 | tf_op jit(solution)/shard_map/ppermute | solution.py:380
  74.5 3.8 %shard_map.98 = (bf16[256,1024]{1,0:T(8,128)(2,1)}, bf16[256,1024]{1,0:T(8,128)(2,1)}, bf16[256,1024]{1,0:T(8,128)(2,1)}, bf16[256,1024]{1,0:T(8,128)(2,1)}) custom-call(s32[3]{0:T(128)S(1)} %pad_add_fusion.info, f32[8,256,768]{2,1,0:T(8,128)S(1)} %get-tuple-element.44.score_ref, f32[8,256,768]{2,1,0:T(8,128)S(1)} %get-tuple-element.45.grad_ref, ...), custom_call_target="tpu_custom_call" | custom-call | flops 1610612736 | bytes 6291456 | tf_op jit(solution)/shard_map/pallas_call | solution.py:350
  (27 shorter events, 2.5 us)
Async XLA Ops:
  0.7 48.8 %copy-start = (bf16[256,1024]{1,0:T(8,128)(2,1)S(1)}, bf16[256,1024]{1,0:T(8,128)(2,1)}, u32[]{:S(2)}) copy-start(bf16[256,1024]{1,0:T(8,128)(2,1)} %q_ref.11) | copy-start | bytes 1572868
  0.7 48.8 %copy-start.1 = (bf16[256,1024]{1,0:T(8,128)(2,1)S(1)}, bf16[256,1024]{1,0:T(8,128)(2,1)}, u32[]{:S(2)}) copy-start(bf16[256,1024]{1,0:T(8,128)(2,1)} %g_ref.11) | copy-start | bytes 1572868
  0.7 48.7 %copy-start.2 = (bf16[256,1024]{1,0:T(8,128)(2,1)S(1)}, bf16[256,1024]{1,0:T(8,128)(2,1)}, u32[]{:S(2)}) copy-start(bf16[256,1024]{1,0:T(8,128)(2,1)} %k_ref.9) | copy-start | bytes 1572868
  0.7 48.7 %copy-start.3 = (bf16[256,1024]{1,0:T(8,128)(2,1)S(1)}, bf16[256,1024]{1,0:T(8,128)(2,1)}, u32[]{:S(2)}) copy-start(bf16[256,1024]{1,0:T(8,128)(2,1)} %v_ref.9) | copy-start | bytes 1572868
  3.6 56.0 %copy-start.4 = (s32[2,8]{1,0:T(2,128)S(1)}, s32[2,8]{1,0:T(2,128)}, u32[]{:S(2)}) copy-start(s32[2,8]{1,0:T(2,128)} %kb.3) | copy-start | bytes 196
  3.6 15.8 %collective-permute-start.2 = (bf16[512,512]{1,0:T(8,128)(2,1)S(1)}, bf16[512,512]{1,0:T(8,128)(2,1)S(1)}, u32[]{:S(2)}, u32[]{:S(2)}) collective-permute-start(bf16[512,512]{1,0:T(8,128)(2,1)S(1)} %get-tuple-element.67), channel_id=1, source_target_pairs={{0,2},{1,3},{2,0},{3,1},{4,6},{5,7},{6,4},{7,5},{8,10},{9,11},{10,... | collective-permute-start | bytes 1572872 | tf_op jit(solution)/shard_map/ppermute | solution.py:377
  6.7 15.8 %collective-permute-start = (bf16[512,512]{1,0:T(8,128)(2,1)S(1)}, bf16[512,512]{1,0:T(8,128)(2,1)S(1)}, u32[]{:S(2)}, u32[]{:S(2)}) collective-permute-start(bf16[512,512]{1,0:T(8,128)(2,1)S(1)} %get-tuple-element.68), channel_id=1, source_target_pairs={{0,4},{1,5},{2,6},{3,7},{4,8},{5,9},{6,10},{7,11},{8,12},{9,13},{1... | collective-permute-start | bytes 1572872 | tf_op jit(solution)/shard_map/ppermute | solution.py:371
  10.2 16.8 %collective-permute-start.1 = (bf16[512,512]{1,0:T(8,128)(2,1)S(1)}, bf16[512,512]{1,0:T(8,128)(2,1)S(1)}, u32[]{:S(2)}, u32[]{:S(2)}) collective-permute-start(bf16[512,512]{1,0:T(8,128)(2,1)S(1)} %get-tuple-element.69), channel_id=1, source_target_pairs={{4,0},{5,1},{6,2},{7,3},{8,4},{9,5},{10,6},{11,7},{12,8},{13,9},{1... | collective-permute-start | bytes 1572872 | tf_op jit(solution)/shard_map/ppermute | solution.py:374
  11.7 19.3 %collective-permute-start.9 = (bf16[512,512]{1,0:T(8,128)(2,1)S(1)}, bf16[512,512]{1,0:T(8,128)(2,1)S(1)}, u32[]{:S(2)}, u32[]{:S(2)}) collective-permute-start(bf16[512,512]{1,0:T(8,128)(2,1)S(1)} %get-tuple-element.56), channel_id=1, source_target_pairs={{0,2},{1,3},{2,0},{3,1},{4,6},{5,7},{6,4},{7,5},{8,10},{9,11},{10,... | collective-permute-start | bytes 1572872 | tf_op jit(solution)/shard_map/ppermute | solution.py:377
  12.3 21.4 %collective-permute-start.7 = (bf16[512,512]{1,0:T(8,128)(2,1)S(1)}, bf16[512,512]{1,0:T(8,128)(2,1)S(1)}, u32[]{:S(2)}, u32[]{:S(2)}) collective-permute-start(bf16[512,512]{1,0:T(8,128)(2,1)S(1)} %get-tuple-element.57), channel_id=1, source_target_pairs={{0,4},{1,5},{2,6},{3,7},{4,8},{5,9},{6,10},{7,11},{8,12},{9,13},{1... | collective-permute-start | bytes 1572872 | tf_op jit(solution)/shard_map/ppermute | solution.py:371
  19.4 18.8 %collective-permute-start.8 = (bf16[512,512]{1,0:T(8,128)(2,1)S(1)}, bf16[512,512]{1,0:T(8,128)(2,1)S(1)}, u32[]{:S(2)}, u32[]{:S(2)}) collective-permute-start(bf16[512,512]{1,0:T(8,128)(2,1)S(1)} %get-tuple-element.58), channel_id=1, source_target_pairs={{4,0},{5,1},{6,2},{7,3},{8,4},{9,5},{10,6},{11,7},{12,8},{13,9},{1... | collective-permute-start | bytes 1572872 | tf_op jit(solution)/shard_map/ppermute | solution.py:374
  27.0 15.3 %collective-permute-start.3 = (bf16[512,512]{1,0:T(8,128)(2,1)S(1)}, bf16[512,512]{1,0:T(8,128)(2,1)S(1)}, u32[]{:S(2)}, u32[]{:S(2)}) collective-permute-start(bf16[512,512]{1,0:T(8,128)(2,1)S(1)} %broadcast_select_fusion.2), channel_id=1, source_target_pairs={{0,2},{1,3},{2,0},{3,1},{4,6},{5,7},{6,4},{7,5},{8,10},{9,11},{10,... | collective-permute-start | bytes 1572872 | tf_op jit(solution)/shard_map/ppermute | solution.py:377
  27.6 17.4 %collective-permute-start.4 = (bf16[512,512]{1,0:T(8,128)(2,1)S(1)}, bf16[512,512]{1,0:T(8,128)(2,1)S(1)}, u32[]{:S(2)}, u32[]{:S(2)}) collective-permute-start(bf16[512,512]{1,0:T(8,128)(2,1)S(1)} %collective-permute-done.refs_2_), channel_id=1, source_target_pairs={{0,4},{1,5},{2,6},{3,7},{4,8},{5,9},{6,10},{7,11},{8,12},{9,13},{1... | collective-permute-start | bytes 1572872 | tf_op jit(solution)/shard_map/ppermute | solution.py:371
  31.1 18.3 %collective-permute-start.5 = (bf16[512,512]{1,0:T(8,128)(2,1)S(1)}, bf16[512,512]{1,0:T(8,128)(2,1)S(1)}, u32[]{:S(2)}, u32[]{:S(2)}) collective-permute-start(bf16[512,512]{1,0:T(8,128)(2,1)S(1)} %collective-permute-done.1.refs_2_), channel_id=1, source_target_pairs={{4,0},{5,1},{6,2},{7,3},{8,4},{9,5},{10,6},{11,7},{12,8},{13,9},{1... | collective-permute-start | bytes 1572872 | tf_op jit(solution)/shard_map/ppermute | solution.py:374
  38.2 16.6 %collective-permute-start.11 = (bf16[512,512]{1,0:T(8,128)(2,1)S(1)}, bf16[512,512]{1,0:T(8,128)(2,1)S(1)}, u32[]{:S(2)}, u32[]{:S(2)}) collective-permute-start(bf16[512,512]{1,0:T(8,128)(2,1)S(1)} %collective-permute-done.7.refs_2_), channel_id=1, source_target_pairs={{0,4},{1,5},{2,6},{3,7},{4,8},{5,9},{6,10},{7,11},{8,12},{9,13},{1... | collective-permute-start | bytes 1572872 | tf_op jit(solution)/shard_map/ppermute | solution.py:371
  41.7 10.6 %collective-permute-start.10 = (bf16[512,512]{1,0:T(8,128)(2,1)S(1)}, bf16[512,512]{1,0:T(8,128)(2,1)S(1)}, u32[]{:S(2)}, u32[]{:S(2)}) collective-permute-start(bf16[512,512]{1,0:T(8,128)(2,1)S(1)} %broadcast_select_fusion), channel_id=1, source_target_pairs={{0,2},{1,3},{2,0},{3,1},{4,6},{5,7},{6,4},{7,5},{8,10},{9,11},{10,... | collective-permute-start | bytes 1572872 | tf_op jit(solution)/shard_map/ppermute | solution.py:377
  42.3 16.6 %collective-permute-start.12 = (bf16[512,512]{1,0:T(8,128)(2,1)S(1)}, bf16[512,512]{1,0:T(8,128)(2,1)S(1)}, u32[]{:S(2)}, u32[]{:S(2)}) collective-permute-start(bf16[512,512]{1,0:T(8,128)(2,1)S(1)} %collective-permute-done.8.refs_6_), channel_id=1, source_target_pairs={{4,0},{5,1},{6,2},{7,3},{8,4},{9,5},{10,6},{11,7},{12,8},{13,9},{1... | collective-permute-start | bytes 1572872 | tf_op jit(solution)/shard_map/ppermute | solution.py:374
  50.1 9.5 %collective-permute-start.6 = (bf16[1024,512]{1,0:T(8,128)(2,1)S(1)}, bf16[1024,512]{1,0:T(8,128)(2,1)S(1)}, u32[]{:S(2)}, u32[]{:S(2)}) collective-permute-start(bf16[1024,512]{1,0:T(8,128)(2,1)S(1)} %get-tuple-element.34), channel_id=1, source_target_pairs={{0,1},{1,0},{2,3},{3,2},{4,5},{5,4},{6,7},{7,6},{8,9},{9,8},{10,11... | collective-permute-start | bytes 3145736 | tf_op jit(solution)/shard_map/ppermute | solution.py:377
  59.6 3.6 %collective-permute-start.13 = (bf16[1024,512]{1,0:T(8,128)(2,1)S(1)}, bf16[1024,512]{1,0:T(8,128)(2,1)S(1)}, u32[]{:S(2)}, u32[]{:S(2)}) collective-permute-start(bf16[1024,512]{1,0:T(8,128)(2,1)S(1)} %get-tuple-element.41), channel_id=1, source_target_pairs={{0,1},{1,0},{2,3},{3,2},{4,5},{5,4},{6,7},{7,6},{8,9},{9,8},{10,11... | collective-permute-start | bytes 3145736 | tf_op jit(solution)/shard_map/ppermute | solution.py:377
  66.6 7.0 %collective-permute-start.17 = (f32[4,8,256]{2,1,0:T(8,128)S(1)}, f32[4,8,256]{2,1,0:T(8,128)S(1)}, u32[]{:S(2)}, u32[]{:S(2)}) collective-permute-start(f32[4,8,256]{2,1,0:T(8,128)S(1)} %get-tuple-element.51.refs_8_), channel_id=1, source_target_pairs={{8,0},{9,1},{10,2},{11,3},{12,4},{13,5},{14,6},{15,7},{0,8},{1,9},... | collective-permute-start | bytes 98312 | tf_op jit(solution)/shard_map/ppermute | solution.py:380
  69.2 4.4 %collective-permute-start.16 = (f32[4,8,256]{2,1,0:T(8,128)S(1)}, f32[4,8,256]{2,1,0:T(8,128)S(1)}, u32[]{:S(2)}, u32[]{:S(2)}) collective-permute-start(f32[4,8,256]{2,1,0:T(8,128)S(1)} %get-tuple-element.51.refs_8_), channel_id=1, source_target_pairs={{4,0},{5,1},{6,2},{7,3},{8,4},{9,5},{10,6},{11,7},{12,8},{13,9},{1... | collective-permute-start | bytes 98312 | tf_op jit(solution)/shard_map/ppermute | solution.py:380
  70.6 3.9 %collective-permute-start.15 = (f32[4,8,256]{2,1,0:T(8,128)S(1)}, f32[4,8,256]{2,1,0:T(8,128)S(1)}, u32[]{:S(2)}, u32[]{:S(2)}) collective-permute-start(f32[4,8,256]{2,1,0:T(8,128)S(1)} %get-tuple-element.51.refs_8_), channel_id=1, source_target_pairs={{2,0},{3,1},{4,2},{5,3},{6,4},{7,5},{8,6},{9,7},{10,8},{11,9},{12,... | collective-permute-start | bytes 98312 | tf_op jit(solution)/shard_map/ppermute | solution.py:380
  71.0 3.5 %collective-permute-start.14 = (f32[4,8,256]{2,1,0:T(8,128)S(1)}, f32[4,8,256]{2,1,0:T(8,128)S(1)}, u32[]{:S(2)}, u32[]{:S(2)}) collective-permute-start(f32[4,8,256]{2,1,0:T(8,128)S(1)} %get-tuple-element.51.refs_8_), channel_id=1, source_target_pairs={{1,0},{2,1},{3,2},{4,3},{5,4},{6,5},{7,6},{8,7},{9,8},{10,9},{11,1... | collective-permute-start | bytes 98312 | tf_op jit(solution)/shard_map/ppermute | solution.py:380

commit v6 on v5

--- a/solution.py
+++ b/solution.py
@@ -12,6 +12,7 @@
 BLOCK = 128
 LEVELS = 8
 CHUNKS = 2
+MARK = 8 * 10**9
 QUERY_LAG = (0, 1, 2, 3)
 KEY_LAG = (0, 1)
 FAR = 1e30
@@ -316,7 +317,11 @@
         copy.wait()
 
 
-def mix_kernel(first, info, q_ref, k_ref, v_ref, g_ref, one_ref, two_ref, out_ref, key_ref, query_ref):
+def mark_kernel(in_ref, out_ref):
+    out_ref[...] = in_ref[...]
+
+
+def mix_kernel(first, info, kb, q_ref, k_ref, v_ref, g_ref, one_ref, two_ref, out_ref, key_ref, query_ref):
     device = info[0]
     rows, width = q_ref.shape[0], one_ref.shape[1]
     columns = slice(first * HEAD_DIM, first * HEAD_DIM + width)
@@ -353,7 +358,7 @@
         out_specs=[pl.BlockSpec(memory_space=pl.ANY) if to_hbm else vmem] * len(out_shapes),
         out_shape=out_shapes,
         scratch_shapes=list(scratch),
-        cost_estimate=pl.CostEstimate(flops=flops, bytes_accessed=6 << 20, transcendentals=0),
+        cost_estimate=pl.CostEstimate(flops=flops, bytes_accessed=0, transcendentals=0),
         compiler_params=pltpu.CompilerParams(vmem_limit_bytes=16 << 20),
     )(*scalars, *arrays)
 
@@ -422,10 +427,13 @@
     front, stats, moved = (), [], []
     for chunk in range(CHUNKS):
         (key_pack, query_pack), (side_1, side_2, keys_by, queries_by) = packs[chunk], middle[chunk]
-        side_2, keys_by[8], queries_by[8] = lax.optimization_barrier((side_2, keys_by[8], queries_by[8]))
+        if chunk < CHUNKS - 1:
+            side_2, keys_by[8], queries_by[8] = lax.optimization_barrier(
+                (side_2, keys_by[8], queries_by[8])
+            )
         packed, keys_by[2], queries_by[2] = call(
             functools.partial(mix_kernel, chunk * heads),
-            (info,),
+            (info, key_blocks),
             own + (side_1, side_2),
             (
                 jax.ShapeDtypeStruct((4 * rows_dev, width), jnp.bfloat16),
@@ -440,10 +448,17 @@
                 [neighbour] + [queries_by[hop] for hop in hops[1:]],
             )
         )
+    mark = jnp.zeros((8, 128), jnp.float32)
+    at = hops.index(8)
+    moved[-1][0][at], moved[-1][1][at], mark = lax.optimization_barrier(
+        (moved[-1][0][at], moved[-1][1][at], mark)
+    )
+    mark = call(mark_kernel, (), (mark,), [jax.ShapeDtypeStruct(mark.shape, mark.dtype)], (), MARK)[0]
+    for chunk in range(CHUNKS):
         att, dq, stat = call(
             functools.partial(query_kernel, hops, chunk * heads),
             (info, key_blocks),
-            own + tuple(moved[chunk][0]) + tuple(stats[-1:]),
+            own + tuple(moved[chunk][0]) + (tuple(stats[-1:]) or (mark,)),
             (part, part, stat_shape),
             [pltpu.VMEM((2, BLOCK, pieces * BLOCK), jnp.float32)],
             flops,

time: 78.8 us -> 77.8 us (0.987)
    ppermute x4, waiting for transfers between devices: 6.23 us -> 5.44 us  [up(): lax.ppermute(value, 'ctx', [(at, at + steps) for at in range(devices - st...]
    pallas_call x6 -> x7, Pallas kernels: 13.9 us -> 13.7 us  [call(): pl.pallas_call(kernel, in_specs=[pl.BlockSpec(memory_space=pltpu.SMEM)] *...]
  transfers between devices with their start and end apart: 18 -> 18, of which waited for: 11 -> 12; matrix products, arithmetic and copies ran while one was open for 1% -> 1% of each run, Pallas kernels for 9% -> 9%
where the time goes in v6:
time: 77.8 us; the launch traced here: 77.4 us
  starting transfers between devices  29.5 us (38%)
  waiting for transfers between devices  29.2 us (38%)
  Pallas kernels  13.7 us (18%)
  local copies, waits for them, and re-layouts  2.68 us (3%)
  between operations  1.72 us (2%)
    ppermute x4, waiting for transfers between devices, down(): lax.ppermute(value, 'ctx', [(at + steps, at) for at in range(devices - st...  17.5 us
    ppermute x4, starting transfers between devices, up(): lax.ppermute(value, 'ctx', [(at, at + steps) for at in range(devices - st...  15 us
    pallas_call x7, Pallas kernels, call(): pl.pallas_call(kernel, in_specs=[pl.BlockSpec(memory_space=pltpu.SMEM)] *...  13.7 us
    ppermute x4, waiting for transfers between devices, up(): lax.ppermute(value, 'ctx', [(at, at + steps) for at in range(devices - st...  5.44 us
    ppermute x4, starting transfers between devices, down(): lax.ppermute(value, 'ctx', [(at + steps, at) for at in range(devices - st...  5.16 us
    ppermute x6, starting transfers between devices, swap(): return lax.ppermute(value, 'ctx', [(at, at ^ bit) for at in range(devices)])  4.89 us
    ppermute x6, waiting for transfers between devices, swap(): return lax.ppermute(value, 'ctx', [(at, at ^ bit) for at in range(devices)])  4.65 us
    ppermute x4, starting transfers between devices, back_round(): lax.ppermute(value, 'ctx', [((at + steps) % devices, at) for at in range(...  4.41 us
  transfers between devices with their start and end apart: 18, of which 12 were waited for; matrix products, arithmetic and copies ran while one was open for 1% of the time, Pallas kernels for 9%

profile of v6, /device:TPU:0, one launch (start us, length us, event | category | flops | bytes accessed | tf_op | source)
XLA Modules:
  0.0 77.4 jit_solution(13606411334241959507)
XLA Ops:
  0.7 1.4 %fusion.2 = (bf16[256,512]{1,0:T(8,128)(2,1)S(1)}, bf16[256,512]{1,0:T(8,128)(2,1)S(1)}, bf16[256,512]{1,0:T(8,128)(2,1)S(1)}, bf16[256,512]{1,0:T(8,128)(2,1)S(1)}) fusion(bf16[256,1024]{1,0:T(8,128)(2,1)} %k_ref.9, bf16[256,1024]{1,0:T(8,128)(2,1)} %v_ref.9), kind=kLoop, calls=%fused_computation.11 | loop fusion | bytes 2097152 | tf_op jit(solution)/shard_map/slice | solution.py:394
  2.1 1.3 %fusion = (bf16[256,512]{1,0:T(8,128)(2,1)S(1)}, bf16[256,512]{1,0:T(8,128)(2,1)S(1)}, bf16[256,512]{1,0:T(8,128)(2,1)S(1)}, bf16[256,512]{1,0:T(8,128)(2,1)S(1)}) fusion(bf16[256,1024]{1,0:T(8,128)(2,1)} %q_ref.11, bf16[256,1024]{1,0:T(8,128)(2,1)} %g_ref.11), kind=kLoop, calls=%fused_computation.9 | loop fusion | bytes 2097152 | tf_op jit(solution)/shard_map/slice | solution.py:395
  3.6 3.0 %collective-permute-start.2 = (bf16[512,512]{1,0:T(8,128)(2,1)S(1)}, bf16[512,512]{1,0:T(8,128)(2,1)S(1)}, u32[]{:S(2)}, u32[]{:S(2)}) collective-permute-start(bf16[512,512]{1,0:T(8,128)(2,1)S(1)} %get-tuple-element.67), channel_id=1, source_target_pairs={{0,2},{1,3},{2,0},{3,1},{4,6},{5,7},{6,4},{7,5},{8,10},{9,11},{10,... | collective-permute-start | bytes 1572872 | tf_op jit(solution)/shard_map/ppermute | solution.py:382
  6.6 3.5 %collective-permute-start = (bf16[512,512]{1,0:T(8,128)(2,1)S(1)}, bf16[512,512]{1,0:T(8,128)(2,1)S(1)}, u32[]{:S(2)}, u32[]{:S(2)}) collective-permute-start(bf16[512,512]{1,0:T(8,128)(2,1)S(1)} %get-tuple-element.68), channel_id=1, source_target_pairs={{0,4},{1,5},{2,6},{3,7},{4,8},{5,9},{6,10},{7,11},{8,12},{9,13},{1... | collective-permute-start | bytes 1572872 | tf_op jit(solution)/shard_map/ppermute | solution.py:376
  10.1 1.3 %collective-permute-start.1 = (bf16[512,512]{1,0:T(8,128)(2,1)S(1)}, bf16[512,512]{1,0:T(8,128)(2,1)S(1)}, u32[]{:S(2)}, u32[]{:S(2)}) collective-permute-start(bf16[512,512]{1,0:T(8,128)(2,1)S(1)} %get-tuple-element.69), channel_id=1, source_target_pairs={{4,0},{5,1},{6,2},{7,3},{8,4},{9,5},{10,6},{11,7},{12,8},{13,9},{1... | collective-permute-start | bytes 1572872 | tf_op jit(solution)/shard_map/ppermute | solution.py:379
  11.7 0.6 collective-permute-start.9
  12.2 4.6 %collective-permute-start.7 = (bf16[512,512]{1,0:T(8,128)(2,1)S(1)}, bf16[512,512]{1,0:T(8,128)(2,1)S(1)}, u32[]{:S(2)}, u32[]{:S(2)}) collective-permute-start(bf16[512,512]{1,0:T(8,128)(2,1)S(1)} %get-tuple-element.57), channel_id=1, source_target_pairs={{0,4},{1,5},{2,6},{3,7},{4,8},{5,9},{6,10},{7,11},{8,12},{9,13},{1... | collective-permute-start | bytes 1572872 | tf_op jit(solution)/shard_map/ppermute | solution.py:376
  16.8 2.6 %collective-permute-done.2.one_ref = bf16[512,512]{1,0:T(8,128)(2,1)S(1)} collective-permute-done((bf16[512,512]{1,0:T(8,128)(2,1)S(1)}, bf16[512,512]{1,0:T(8,128)(2,1)S(1)}, u32[]{:S(2)}, u32[]{:S(2)}) %collective-permute-start.2) | collective-permute-done | bytes 524320 | tf_op jit(solution)/shard_map/ppermute | solution.py:382
  19.4 1.3 %collective-permute-start.8 = (bf16[512,512]{1,0:T(8,128)(2,1)S(1)}, bf16[512,512]{1,0:T(8,128)(2,1)S(1)}, u32[]{:S(2)}, u32[]{:S(2)}) collective-permute-start(bf16[512,512]{1,0:T(8,128)(2,1)S(1)} %get-tuple-element.58), channel_id=1, source_target_pairs={{4,0},{5,1},{6,2},{7,3},{8,4},{9,5},{10,6},{11,7},{12,8},{13,9},{1... | collective-permute-start | bytes 1572872 | tf_op jit(solution)/shard_map/ppermute | solution.py:379
  20.7 1.8 %collective-permute-done.refs_2_ = bf16[512,512]{1,0:T(8,128)(2,1)S(1)} collective-permute-done((bf16[512,512]{1,0:T(8,128)(2,1)S(1)}, bf16[512,512]{1,0:T(8,128)(2,1)S(1)}, u32[]{:S(2)}, u32[]{:S(2)}) %collective-permute-start) | collective-permute-done | bytes 524320 | tf_op jit(solution)/shard_map/ppermute | solution.py:376
  22.5 4.4 %collective-permute-done.1.refs_2_ = bf16[512,512]{1,0:T(8,128)(2,1)S(1)} collective-permute-done((bf16[512,512]{1,0:T(8,128)(2,1)S(1)}, bf16[512,512]{1,0:T(8,128)(2,1)S(1)}, u32[]{:S(2)}, u32[]{:S(2)}) %collective-permute-start.1) | collective-permute-done | bytes 524320 | tf_op jit(solution)/shard_map/ppermute | solution.py:379
  27.0 0.6 collective-permute-start.3
  27.5 3.5 %collective-permute-start.4 = (bf16[512,512]{1,0:T(8,128)(2,1)S(1)}, bf16[512,512]{1,0:T(8,128)(2,1)S(1)}, u32[]{:S(2)}, u32[]{:S(2)}) collective-permute-start(bf16[512,512]{1,0:T(8,128)(2,1)S(1)} %collective-permute-done.refs_2_), channel_id=1, source_target_pairs={{0,4},{1,5},{2,6},{3,7},{4,8},{5,9},{6,10},{7,11},{8,12},{9,13},{1... | collective-permute-start | bytes 1572872 | tf_op jit(solution)/shard_map/ppermute | solution.py:376
  31.0 1.3 %collective-permute-start.5 = (bf16[512,512]{1,0:T(8,128)(2,1)S(1)}, bf16[512,512]{1,0:T(8,128)(2,1)S(1)}, u32[]{:S(2)}, u32[]{:S(2)}) collective-permute-start(bf16[512,512]{1,0:T(8,128)(2,1)S(1)} %collective-permute-done.1.refs_2_), channel_id=1, source_target_pairs={{4,0},{5,1},{6,2},{7,3},{8,4},{9,5},{10,6},{11,7},{12,8},{13,9},{1... | collective-permute-start | bytes 1572872 | tf_op jit(solution)/shard_map/ppermute | solution.py:379
  32.3 1.4 %collective-permute-done.7.refs_2_ = bf16[512,512]{1,0:T(8,128)(2,1)S(1)} collective-permute-done((bf16[512,512]{1,0:T(8,128)(2,1)S(1)}, bf16[512,512]{1,0:T(8,128)(2,1)S(1)}, u32[]{:S(2)}, u32[]{:S(2)}) %collective-permute-start.7) | collective-permute-done | bytes 524320 | tf_op jit(solution)/shard_map/ppermute | solution.py:376
  33.7 4.4 %collective-permute-done.8.refs_6_ = bf16[512,512]{1,0:T(8,128)(2,1)S(1)} collective-permute-done((bf16[512,512]{1,0:T(8,128)(2,1)S(1)}, bf16[512,512]{1,0:T(8,128)(2,1)S(1)}, u32[]{:S(2)}, u32[]{:S(2)}) %collective-permute-start.8) | collective-permute-done | bytes 524320 | tf_op jit(solution)/shard_map/ppermute | solution.py:379
  38.8 3.5 %collective-permute-start.12 = (bf16[512,512]{1,0:T(8,128)(2,1)S(1)}, bf16[512,512]{1,0:T(8,128)(2,1)S(1)}, u32[]{:S(2)}, u32[]{:S(2)}) collective-permute-start(bf16[512,512]{1,0:T(8,128)(2,1)S(1)} %collective-permute-done.7.refs_2_), channel_id=1, source_target_pairs={{0,4},{1,5},{2,6},{3,7},{4,8},{5,9},{6,10},{7,11},{8,12},{9,13},{1... | collective-permute-start | bytes 1572872 | tf_op jit(solution)/shard_map/ppermute | solution.py:376
  42.3 1.3 %collective-permute-start.13 = (bf16[512,512]{1,0:T(8,128)(2,1)S(1)}, bf16[512,512]{1,0:T(8,128)(2,1)S(1)}, u32[]{:S(2)}, u32[]{:S(2)}) collective-permute-start(bf16[512,512]{1,0:T(8,128)(2,1)S(1)} %collective-permute-done.8.refs_6_), channel_id=1, source_target_pairs={{4,0},{5,1},{6,2},{7,3},{8,4},{9,5},{10,6},{11,7},{12,8},{13,9},{1... | collective-permute-start | bytes 1572872 | tf_op jit(solution)/shard_map/ppermute | solution.py:379
  44.3 0.6 collective-permute-done.4.refs_3_
  44.9 4.4 %collective-permute-done.5.refs_3_ = bf16[512,512]{1,0:T(8,128)(2,1)S(1)} collective-permute-done((bf16[512,512]{1,0:T(8,128)(2,1)S(1)}, bf16[512,512]{1,0:T(8,128)(2,1)S(1)}, u32[]{:S(2)}, u32[]{:S(2)}) %collective-permute-start.5) | collective-permute-done | bytes 524320 | tf_op jit(solution)/shard_map/ppermute | solution.py:379
  49.4 0.7 shard_map.93
  50.2 2.1 %collective-permute-done.10.two_ref = bf16[512,512]{1,0:T(8,128)(2,1)S(1)} collective-permute-done((bf16[512,512]{1,0:T(8,128)(2,1)S(1)}, bf16[512,512]{1,0:T(8,128)(2,1)S(1)}, u32[]{:S(2)}, u32[]{:S(2)}) %collective-permute-start.10) | collective-permute-done | bytes 524320 | tf_op jit(solution)/shard_map/ppermute | solution.py:382
  52.3 0.7 shard_map.94
  53.1 1.6 %collective-permute-done.12.refs_3_ = bf16[512,512]{1,0:T(8,128)(2,1)S(1)} collective-permute-done((bf16[512,512]{1,0:T(8,128)(2,1)S(1)}, bf16[512,512]{1,0:T(8,128)(2,1)S(1)}, u32[]{:S(2)}, u32[]{:S(2)}) %collective-permute-start.12) | collective-permute-done | bytes 524320 | tf_op jit(solution)/shard_map/ppermute | solution.py:376
  54.7 4.1 %collective-permute-done.13.refs_7_ = bf16[512,512]{1,0:T(8,128)(2,1)S(1)} collective-permute-done((bf16[512,512]{1,0:T(8,128)(2,1)S(1)}, bf16[512,512]{1,0:T(8,128)(2,1)S(1)}, u32[]{:S(2)}, u32[]{:S(2)}) %collective-permute-start.13) | collective-permute-done | bytes 524320 | tf_op jit(solution)/shard_map/ppermute | solution.py:379
  58.9 3.3 %shard_map.97 = (bf16[256,512]{1,0:T(8,128)(2,1)S(1)}, bf16[256,512]{1,0:T(8,128)(2,1)S(1)}, f32[4,8,256]{2,1,0:T(8,128)S(1)}) custom-call(s32[3]{0:T(128)S(1)} %pad_add_fusion.info, s32[2,8]{1,0:T(2,128)S(1)} %copy-done.4, bf16[256,1024]{1,0:T(8,128)(2,1)S(1)} %copy-done, bf16[256,1024]{1,0:T(8,128)(2,1)S(1)} %copy-done.2, bf16[256,1024]{1,0:T(8,128)(2,1)S(1)} %copy-done.3, ...), custom_call_target="tpu_custom_call" | custom-call | flops 805306368 | tf_op jit(solution)/shard_map/pallas_call | solution.py:355
  62.2 3.3 %shard_map.98 = (bf16[256,512]{1,0:T(8,128)(2,1)S(1)}, bf16[256,512]{1,0:T(8,128)(2,1)S(1)}, f32[4,8,256]{2,1,0:T(8,128)S(1)}) custom-call(s32[3]{0:T(128)S(1)} %pad_add_fusion.info, s32[2,8]{1,0:T(2,128)S(1)} %copy-done.4, bf16[256,1024]{1,0:T(8,128)(2,1)S(1)} %copy-done, bf16[256,1024]{1,0:T(8,128)(2,1)S(1)} %copy-done.2, bf16[256,1024]{1,0:T(8,128)(2,1)S(1)} %copy-done.3, ...), custom_call_target="tpu_custom_call" | custom-call | flops 805306368 | tf_op jit(solution)/shard_map/pallas_call | solution.py:355
  65.6 2.6 %collective-permute-start.17 = (f32[4,8,256]{2,1,0:T(8,128)S(1)}, f32[4,8,256]{2,1,0:T(8,128)S(1)}, u32[]{:S(2)}, u32[]{:S(2)}) collective-permute-start(f32[4,8,256]{2,1,0:T(8,128)S(1)} %get-tuple-element.51.refs_8_), channel_id=1, source_target_pairs={{8,0},{9,1},{10,2},{11,3},{12,4},{13,5},{14,6},{15,7},{0,8},{1,9},... | collective-permute-start | bytes 98312 | tf_op jit(solution)/shard_map/ppermute | solution.py:385
  68.2 1.4 %collective-permute-start.16 = (f32[4,8,256]{2,1,0:T(8,128)S(1)}, f32[4,8,256]{2,1,0:T(8,128)S(1)}, u32[]{:S(2)}, u32[]{:S(2)}) collective-permute-start(f32[4,8,256]{2,1,0:T(8,128)S(1)} %get-tuple-element.51.refs_8_), channel_id=1, source_target_pairs={{4,0},{5,1},{6,2},{7,3},{8,4},{9,5},{10,6},{11,7},{12,8},{13,9},{1... | collective-permute-start | bytes 98312 | tf_op jit(solution)/shard_map/ppermute | solution.py:385
  70.0 1.8 %shard_map.95 = (f32[8,256,768]{2,1,0:T(8,128)S(1)}, f32[8,256,768]{2,1,0:T(8,128)S(1)}) custom-call(bf16[256,1024]{1,0:T(8,128)(2,1)S(1)} %copy-done, bf16[256,1024]{1,0:T(8,128)(2,1)S(1)} %copy-done.2, bf16[256,1024]{1,0:T(8,128)(2,1)S(1)} %copy-done.3, bf16[256,1024]{1,0:T(8,128)(2,1)S(1)} %copy-done.1, ...), custom_call_target="tpu_custom_call" | custom-call | flops 1610612736 | tf_op jit(solution)/shard_map/pallas_call | solution.py:355
  72.1 1.4 %collective-permute-done.15.refs_10_ = f32[4,8,256]{2,1,0:T(8,128)S(1)} collective-permute-done((f32[4,8,256]{2,1,0:T(8,128)S(1)}, f32[4,8,256]{2,1,0:T(8,128)S(1)}, u32[]{:S(2)}, u32[]{:S(2)}) %collective-permute-start.15) | collective-permute-done | bytes 32800 | tf_op jit(solution)/shard_map/ppermute | solution.py:385
  73.5 3.8 %shard_map.99 = (bf16[256,1024]{1,0:T(8,128)(2,1)}, bf16[256,1024]{1,0:T(8,128)(2,1)}, bf16[256,1024]{1,0:T(8,128)(2,1)}, bf16[256,1024]{1,0:T(8,128)(2,1)}) custom-call(s32[3]{0:T(128)S(1)} %pad_add_fusion.info, f32[8,256,768]{2,1,0:T(8,128)S(1)} %get-tuple-element.43.score_ref, f32[8,256,768]{2,1,0:T(8,128)S(1)} %get-tuple-element.44.grad_ref, ...), custom_call_target="tpu_custom_call" | custom-call | flops 1610612736 | tf_op jit(solution)/shard_map/pallas_call | solution.py:355
  (29 shorter events, 2.1 us)
Async XLA Ops:
  0.7 48.7 %copy-start = (bf16[256,1024]{1,0:T(8,128)(2,1)S(1)}, bf16[256,1024]{1,0:T(8,128)(2,1)}, u32[]{:S(2)}) copy-start(bf16[256,1024]{1,0:T(8,128)(2,1)} %q_ref.11) | copy-start | bytes 1572868
  0.7 48.7 %copy-start.1 = (bf16[256,1024]{1,0:T(8,128)(2,1)S(1)}, bf16[256,1024]{1,0:T(8,128)(2,1)}, u32[]{:S(2)}) copy-start(bf16[256,1024]{1,0:T(8,128)(2,1)} %g_ref.11) | copy-start | bytes 1572868
  0.7 48.7 %copy-start.2 = (bf16[256,1024]{1,0:T(8,128)(2,1)S(1)}, bf16[256,1024]{1,0:T(8,128)(2,1)}, u32[]{:S(2)}) copy-start(bf16[256,1024]{1,0:T(8,128)(2,1)} %k_ref.9) | copy-start | bytes 1572868
  0.7 48.7 %copy-start.3 = (bf16[256,1024]{1,0:T(8,128)(2,1)S(1)}, bf16[256,1024]{1,0:T(8,128)(2,1)}, u32[]{:S(2)}) copy-start(bf16[256,1024]{1,0:T(8,128)(2,1)} %v_ref.9) | copy-start | bytes 1572868
  0.7 48.7 %copy-start.4 = (s32[2,8]{1,0:T(2,128)S(1)}, s32[2,8]{1,0:T(2,128)}, u32[]{:S(2)}) copy-start(s32[2,8]{1,0:T(2,128)} %kb.7) | copy-start | bytes 196
  3.6 15.8 %collective-permute-start.2 = (bf16[512,512]{1,0:T(8,128)(2,1)S(1)}, bf16[512,512]{1,0:T(8,128)(2,1)S(1)}, u32[]{:S(2)}, u32[]{:S(2)}) collective-permute-start(bf16[512,512]{1,0:T(8,128)(2,1)S(1)} %get-tuple-element.67), channel_id=1, source_target_pairs={{0,2},{1,3},{2,0},{3,1},{4,6},{5,7},{6,4},{7,5},{8,10},{9,11},{10,... | collective-permute-start | bytes 1572872 | tf_op jit(solution)/shard_map/ppermute | solution.py:382
  6.6 15.8 %collective-permute-start = (bf16[512,512]{1,0:T(8,128)(2,1)S(1)}, bf16[512,512]{1,0:T(8,128)(2,1)S(1)}, u32[]{:S(2)}, u32[]{:S(2)}) collective-permute-start(bf16[512,512]{1,0:T(8,128)(2,1)S(1)} %get-tuple-element.68), channel_id=1, source_target_pairs={{0,4},{1,5},{2,6},{3,7},{4,8},{5,9},{6,10},{7,11},{8,12},{9,13},{1... | collective-permute-start | bytes 1572872 | tf_op jit(solution)/shard_map/ppermute | solution.py:376
  10.1 16.8 %collective-permute-start.1 = (bf16[512,512]{1,0:T(8,128)(2,1)S(1)}, bf16[512,512]{1,0:T(8,128)(2,1)S(1)}, u32[]{:S(2)}, u32[]{:S(2)}) collective-permute-start(bf16[512,512]{1,0:T(8,128)(2,1)S(1)} %get-tuple-element.69), channel_id=1, source_target_pairs={{4,0},{5,1},{6,2},{7,3},{8,4},{9,5},{10,6},{11,7},{12,8},{13,9},{1... | collective-permute-start | bytes 1572872 | tf_op jit(solution)/shard_map/ppermute | solution.py:379
  11.7 19.4 %collective-permute-start.9 = (bf16[512,512]{1,0:T(8,128)(2,1)S(1)}, bf16[512,512]{1,0:T(8,128)(2,1)S(1)}, u32[]{:S(2)}, u32[]{:S(2)}) collective-permute-start(bf16[512,512]{1,0:T(8,128)(2,1)S(1)} %get-tuple-element.56), channel_id=1, source_target_pairs={{0,2},{1,3},{2,0},{3,1},{4,6},{5,7},{6,4},{7,5},{8,10},{9,11},{10,... | collective-permute-start | bytes 1572872 | tf_op jit(solution)/shard_map/ppermute | solution.py:382
  12.2 21.5 %collective-permute-start.7 = (bf16[512,512]{1,0:T(8,128)(2,1)S(1)}, bf16[512,512]{1,0:T(8,128)(2,1)S(1)}, u32[]{:S(2)}, u32[]{:S(2)}) collective-permute-start(bf16[512,512]{1,0:T(8,128)(2,1)S(1)} %get-tuple-element.57), channel_id=1, source_target_pairs={{0,4},{1,5},{2,6},{3,7},{4,8},{5,9},{6,10},{7,11},{8,12},{9,13},{1... | collective-permute-start | bytes 1572872 | tf_op jit(solution)/shard_map/ppermute | solution.py:376
  19.4 18.8 %collective-permute-start.8 = (bf16[512,512]{1,0:T(8,128)(2,1)S(1)}, bf16[512,512]{1,0:T(8,128)(2,1)S(1)}, u32[]{:S(2)}, u32[]{:S(2)}) collective-permute-start(bf16[512,512]{1,0:T(8,128)(2,1)S(1)} %get-tuple-element.58), channel_id=1, source_target_pairs={{4,0},{5,1},{6,2},{7,3},{8,4},{9,5},{10,6},{11,7},{12,8},{13,9},{1... | collective-permute-start | bytes 1572872 | tf_op jit(solution)/shard_map/ppermute | solution.py:379
  27.0 15.3 %collective-permute-start.3 = (bf16[512,512]{1,0:T(8,128)(2,1)S(1)}, bf16[512,512]{1,0:T(8,128)(2,1)S(1)}, u32[]{:S(2)}, u32[]{:S(2)}) collective-permute-start(bf16[512,512]{1,0:T(8,128)(2,1)S(1)} %broadcast_select_fusion.2), channel_id=1, source_target_pairs={{0,2},{1,3},{2,0},{3,1},{4,6},{5,7},{6,4},{7,5},{8,10},{9,11},{10,... | collective-permute-start | bytes 1572872 | tf_op jit(solution)/shard_map/ppermute | solution.py:382
  27.5 17.4 %collective-permute-start.4 = (bf16[512,512]{1,0:T(8,128)(2,1)S(1)}, bf16[512,512]{1,0:T(8,128)(2,1)S(1)}, u32[]{:S(2)}, u32[]{:S(2)}) collective-permute-start(bf16[512,512]{1,0:T(8,128)(2,1)S(1)} %collective-permute-done.refs_2_), channel_id=1, source_target_pairs={{0,4},{1,5},{2,6},{3,7},{4,8},{5,9},{6,10},{7,11},{8,12},{9,13},{1... | collective-permute-start | bytes 1572872 | tf_op jit(solution)/shard_map/ppermute | solution.py:376
  31.0 18.3 %collective-permute-start.5 = (bf16[512,512]{1,0:T(8,128)(2,1)S(1)}, bf16[512,512]{1,0:T(8,128)(2,1)S(1)}, u32[]{:S(2)}, u32[]{:S(2)}) collective-permute-start(bf16[512,512]{1,0:T(8,128)(2,1)S(1)} %collective-permute-done.1.refs_2_), channel_id=1, source_target_pairs={{4,0},{5,1},{6,2},{7,3},{8,4},{9,5},{10,6},{11,7},{12,8},{13,9},{1... | collective-permute-start | bytes 1572872 | tf_op jit(solution)/shard_map/ppermute | solution.py:379
  38.2 14.1 %collective-permute-start.10 = (bf16[512,512]{1,0:T(8,128)(2,1)S(1)}, bf16[512,512]{1,0:T(8,128)(2,1)S(1)}, u32[]{:S(2)}, u32[]{:S(2)}) collective-permute-start(bf16[512,512]{1,0:T(8,128)(2,1)S(1)} %broadcast_select_fusion), channel_id=1, source_target_pairs={{0,2},{1,3},{2,0},{3,1},{4,6},{5,7},{6,4},{7,5},{8,10},{9,11},{10,... | collective-permute-start | bytes 1572872 | tf_op jit(solution)/shard_map/ppermute | solution.py:382
  38.8 15.9 %collective-permute-start.12 = (bf16[512,512]{1,0:T(8,128)(2,1)S(1)}, bf16[512,512]{1,0:T(8,128)(2,1)S(1)}, u32[]{:S(2)}, u32[]{:S(2)}) collective-permute-start(bf16[512,512]{1,0:T(8,128)(2,1)S(1)} %collective-permute-done.7.refs_2_), channel_id=1, source_target_pairs={{0,4},{1,5},{2,6},{3,7},{4,8},{5,9},{6,10},{7,11},{8,12},{9,13},{1... | collective-permute-start | bytes 1572872 | tf_op jit(solution)/shard_map/ppermute | solution.py:376
  42.3 16.6 %collective-permute-start.13 = (bf16[512,512]{1,0:T(8,128)(2,1)S(1)}, bf16[512,512]{1,0:T(8,128)(2,1)S(1)}, u32[]{:S(2)}, u32[]{:S(2)}) collective-permute-start(bf16[512,512]{1,0:T(8,128)(2,1)S(1)} %collective-permute-done.8.refs_6_), channel_id=1, source_target_pairs={{4,0},{5,1},{6,2},{7,3},{8,4},{9,5},{10,6},{11,7},{12,8},{13,9},{1... | collective-permute-start | bytes 1572872 | tf_op jit(solution)/shard_map/ppermute | solution.py:379
  50.1 8.7 %collective-permute-start.6 = (bf16[1024,512]{1,0:T(8,128)(2,1)S(1)}, bf16[1024,512]{1,0:T(8,128)(2,1)S(1)}, u32[]{:S(2)}, u32[]{:S(2)}) collective-permute-start(bf16[1024,512]{1,0:T(8,128)(2,1)S(1)} %get-tuple-element.34), channel_id=1, source_target_pairs={{0,1},{1,0},{2,3},{3,2},{4,5},{5,4},{6,7},{7,6},{8,9},{9,8},{10,11... | collective-permute-start | bytes 3145736 | tf_op jit(solution)/shard_map/ppermute | solution.py:382
  53.0 9.2 %collective-permute-start.11 = (bf16[1024,512]{1,0:T(8,128)(2,1)S(1)}, bf16[1024,512]{1,0:T(8,128)(2,1)S(1)}, u32[]{:S(2)}, u32[]{:S(2)}) collective-permute-start(bf16[1024,512]{1,0:T(8,128)(2,1)S(1)} %get-tuple-element.40), channel_id=1, source_target_pairs={{0,1},{1,0},{2,3},{3,2},{4,5},{5,4},{6,7},{7,6},{8,9},{9,8},{10,11... | collective-permute-start | bytes 3145736 | tf_op jit(solution)/shard_map/ppermute | solution.py:382
  65.6 6.3 %collective-permute-start.17 = (f32[4,8,256]{2,1,0:T(8,128)S(1)}, f32[4,8,256]{2,1,0:T(8,128)S(1)}, u32[]{:S(2)}, u32[]{:S(2)}) collective-permute-start(f32[4,8,256]{2,1,0:T(8,128)S(1)} %get-tuple-element.51.refs_8_), channel_id=1, source_target_pairs={{8,0},{9,1},{10,2},{11,3},{12,4},{13,5},{14,6},{15,7},{0,8},{1,9},... | collective-permute-start | bytes 98312 | tf_op jit(solution)/shard_map/ppermute | solution.py:385
  68.2 3.9 %collective-permute-start.16 = (f32[4,8,256]{2,1,0:T(8,128)S(1)}, f32[4,8,256]{2,1,0:T(8,128)S(1)}, u32[]{:S(2)}, u32[]{:S(2)}) collective-permute-start(f32[4,8,256]{2,1,0:T(8,128)S(1)} %get-tuple-element.51.refs_8_), channel_id=1, source_target_pairs={{4,0},{5,1},{6,2},{7,3},{8,4},{9,5},{10,6},{11,7},{12,8},{13,9},{1... | collective-permute-start | bytes 98312 | tf_op jit(solution)/shard_map/ppermute | solution.py:385
  69.6 3.9 %collective-permute-start.15 = (f32[4,8,256]{2,1,0:T(8,128)S(1)}, f32[4,8,256]{2,1,0:T(8,128)S(1)}, u32[]{:S(2)}, u32[]{:S(2)}) collective-permute-start(f32[4,8,256]{2,1,0:T(8,128)S(1)} %get-tuple-element.51.refs_8_), channel_id=1, source_target_pairs={{2,0},{3,1},{4,2},{5,3},{6,4},{7,5},{8,6},{9,7},{10,8},{11,9},{12,... | collective-permute-start | bytes 98312 | tf_op jit(solution)/shard_map/ppermute | solution.py:385
  70.0 3.5 %collective-permute-start.14 = (f32[4,8,256]{2,1,0:T(8,128)S(1)}, f32[4,8,256]{2,1,0:T(8,128)S(1)}, u32[]{:S(2)}, u32[]{:S(2)}) collective-permute-start(f32[4,8,256]{2,1,0:T(8,128)S(1)} %get-tuple-element.51.refs_8_), channel_id=1, source_target_pairs={{1,0},{2,1},{3,2},{4,3},{5,4},{6,5},{7,6},{8,7},{9,8},{10,9},{11,1... | collective-permute-start | bytes 98312 | tf_op jit(solution)/shard_map/ppermute | solution.py:385
